TPU v7x, 32 devices: a whole 2x2x4 slice. The times are simulated.
32 devices in a mesh: seq: 4 (over y, x), clip: 8 (over z, core).
Axes of the slice: x: 2, y: 2, z: 4, core: 2. Of those that a mesh axis runs over, the one named last changes fastest.
Arguments:
- frames_in: bfloat16 [8, 2048, 1024], P('clip', 'seq'), may hold values from -6 to 6
- text_states: bfloat16 [8, 256, 1024], P('clip'), may hold values from -6 to 6
- clip_lengths: int32 [8, 4], P('clip'), may hold values from 0 to 2048, as said below
- self_gain: float32 [1024], replicated, may hold values from 0.5 to 1.5
- self_bias: float32 [1024], replicated, may hold values from -1.5 to 1.5
- query_weight: bfloat16 [1024, 1024], replicated, may hold values from -0.1875 to 0.1875
- key_weight: bfloat16 [1024, 1024], replicated, may hold values from -0.1875 to 0.1875
- value_weight: bfloat16 [1024, 1024], replicated, may hold values from -0.1875 to 0.1875
- output_weight: bfloat16 [1024, 1024], replicated, may hold values from -0.75 to 0.75
- cross_gain: float32 [1024], replicated, may hold values from 0.5 to 1.5
- cross_bias: float32 [1024], replicated, may hold values from -1.5 to 1.5
- cross_query: bfloat16 [1024, 1024], replicated, may hold values from -0.1875 to 0.1875
- cross_key: bfloat16 [1024, 1024], replicated, may hold values from -0.1875 to 0.1875
- cross_value: bfloat16 [1024, 1024], replicated, may hold values from -0.1875 to 0.1875
- cross_output: bfloat16 [1024, 1024], replicated, may hold values from -0.75 to 0.75
- feed_gain: float32 [1024], replicated, may hold values from 0.5 to 1.5
- feed_bias: float32 [1024], replicated, may hold values from -1.5 to 1.5
- feed_upward: bfloat16 [1024, 4096], replicated, may hold values from -0.1875 to 0.1875
- feed_downward: bfloat16 [4096, 1024], replicated, may hold values from -0.09375 to 0.09375
- grad_out: bfloat16 [8, 2048, 1024], P('clip', 'seq'), may hold values from -6 to 6
Outputs:
- frames_out: bfloat16 [8, 2048, 1024], P('clip', 'seq')
- frames_grad: float32 [8, 2048, 1024], P('clip', 'seq')
- text_grad: float32 [8, 256, 1024], P('clip')
- self_gain_grad: float32 [1024], P('clip')
- self_bias_grad: float32 [1024], P('clip')
- query_grad: float32 [1024, 1024], P('clip')
- key_grad: float32 [1024, 1024], P('clip')
- value_grad: float32 [1024, 1024], P('clip')
- output_grad: float32 [1024, 1024], P('clip')
- cross_gain_grad: float32 [1024], P('clip')
- cross_bias_grad: float32 [1024], P('clip')
- cross_query_grad: float32 [1024, 1024], P('clip')
- cross_key_grad: float32 [1024, 1024], P('clip')
- cross_value_grad: float32 [1024, 1024], P('clip')
- cross_output_grad: float32 [1024, 1024], P('clip')
- feed_gain_grad: float32 [1024], P('clip')
- feed_bias_grad: float32 [1024], P('clip')
- upward_grad: float32 [1024, 4096], P('clip')
- downward_grad: float32 [4096, 1024], P('clip')
Inputs may be any that keep to these rules, and one draw needn't show every extreme that they name: `clip_lengths`: in each group the lengths sum to 2048 and the first is more than 1536; where the first is 2048 the others are 0, else each of the others is 1 or more.
All inputs are finite; a program needn't handle non-finite values.
Results may differ from a plain program's by a relative error of at most 0.02.
Values may be sent and summed in bfloat16 or wider, within the bound.
A program may use at most 256 MiB of HBM per device.

v0:
```python
import jax
import jax.numpy as jnp
from jax import lax
from jax.sharding import PartitionSpec as P

D = 1024
HEADS = 16
HD = 64
TEXT = 64
CLIPS = 4


EPS = 1e-05
NEG = -1e30
SQRT_HALF = 0.7071067811865476
INV_ROOT_TWO_PI = 0.3989422804014327


def matmul(left, right):
    return jnp.dot(left, right, preferred_element_type=jnp.float32)


def left_times(left, right):
    return lax.dot_general(
        left, right, (((0,), (0,)), ((), ())), preferred_element_type=jnp.float32
    )


def right_times(left, right):
    return lax.dot_general(
        left, right, (((1,), (1,)), ((), ())), preferred_element_type=jnp.float32
    )


def norm_forward(values, gain, bias):
    center = values - jnp.mean(values, axis=-1, keepdims=True)
    scaled = lax.rsqrt(jnp.mean(center * center, axis=-1, keepdims=True) + EPS)
    unit = center * scaled
    return (unit * gain + bias, unit, scaled)


def norm_backward(upstream, unit, scaled, gain):
    along = upstream * gain
    inner = (
        along
        - jnp.mean(along, axis=-1, keepdims=True)
        - unit * jnp.mean(along * unit, axis=-1, keepdims=True)
    )
    return (inner * scaled, jnp.sum(upstream * unit, axis=0), jnp.sum(upstream, axis=0))


def gelu_slope(values):
    return (
        0.5 * (1.0 + lax.erf(values * SQRT_HALF))
        + values * jnp.exp(-0.5 * values * values) * INV_ROOT_TWO_PI
    )


def softmax_rows(scores):
    top = jnp.max(scores, axis=-1, keepdims=True)
    expo = jnp.exp(scores - top)
    total = jnp.sum(expo, axis=-1, keepdims=True)
    return (expo / total, top[..., 0] + jnp.log(total[..., 0]))


def shards(
    frames_in,
    text_states,
    clip_lengths,
    self_gain,
    self_bias,
    query_weight,
    key_weight,
    value_weight,
    output_weight,
    cross_gain,
    cross_bias,
    cross_query,
    cross_key,
    cross_value,
    cross_output,
    feed_gain,
    feed_bias,
    feed_upward,
    feed_downward,
    grad_out,
):
    count = lax.axis_size("seq")
    place = lax.axis_index("seq")
    local = frames_in.shape[1]
    total_frames = local * count
    block = min(512, total_frames)
    blocks = total_frames // block
    scale = HD ** (-0.5)
    lengths = clip_lengths[0]
    ends = jnp.cumsum(lengths)
    begins = ends - lengths
    slots = jnp.arange(CLIPS, dtype=jnp.int32)
    positions = jnp.arange(total_frames, dtype=jnp.int32)
    owner_all = jnp.sum((ends[None, :] <= positions[:, None]).astype(jnp.int32), axis=1)
    first_all = jnp.sum(jnp.where(owner_all[:, None] == slots[None, :], begins[None, :], 0), axis=1)
    owner_mine = lax.dynamic_slice_in_dim(owner_all, place * local, local, 0)
    frames = frames_in[0].astype(jnp.float32)
    text = text_states[0]
    text_rows = text.shape[0]
    normed, unit_one, scale_one = norm_forward(frames, self_gain, self_bias)
    normed_low = normed.astype(jnp.bfloat16)
    query = matmul(normed_low, query_weight).astype(jnp.bfloat16)
    keys = matmul(normed_low, key_weight).astype(jnp.bfloat16)
    values = matmul(normed_low, value_weight).astype(jnp.bfloat16)
    query_heads, key_heads, value_heads = (
        lax.all_to_all(query, "seq", split_axis=1, concat_axis=0, tiled=True),
        lax.all_to_all(keys, "seq", split_axis=1, concat_axis=0, tiled=True),
        lax.all_to_all(values, "seq", split_axis=1, concat_axis=0, tiled=True),
    )
    width = query_heads.shape[1]
    heads_local = width // HD
    keys_split = key_heads.reshape(total_frames, heads_local, HD)
    values_split = value_heads.reshape(total_frames, heads_local, HD)

    def scores_of(index):
        start = index * block
        rows_q = lax.dynamic_slice_in_dim(query_heads, start, block, 0).reshape(
            block, heads_local, HD
        )
        scores = (
            jnp.einsum("qhe,khe->hqk", rows_q, keys_split, preferred_element_type=jnp.float32)
            * scale
        )
        rows = start + jnp.arange(block, dtype=jnp.int32)
        lower = lax.dynamic_slice_in_dim(first_all, start, block, 0)
        allowed = (positions[None, :] <= rows[:, None]) & (positions[None, :] >= lower[:, None])
        return (rows_q, scores, allowed)

    def attend(index):
        rows_q, scores, allowed = scores_of(index)
        probs, log_total = softmax_rows(jnp.where(allowed[None], scores, NEG))
        mixed = jnp.einsum(
            "hqk,khe->qhe",
            probs.astype(jnp.bfloat16),
            values_split,
            preferred_element_type=jnp.float32,
        )
        return (mixed.reshape(block, width).astype(jnp.bfloat16), log_total)

    mixed_blocks, log_totals = lax.map(attend, jnp.arange(blocks, dtype=jnp.int32))
    attended = mixed_blocks.reshape(total_frames, width)
    attended_frames = lax.all_to_all(attended, "seq", split_axis=0, concat_axis=1, tiled=True)
    after_self = frames + matmul(attended_frames, output_weight)
    normed_two, unit_two, scale_two = norm_forward(after_self, cross_gain, cross_bias)
    normed_two_low = normed_two.astype(jnp.bfloat16)
    cross_q = matmul(normed_two_low, cross_query).astype(jnp.bfloat16)
    cross_k = matmul(text, cross_key).astype(jnp.bfloat16)
    cross_v = matmul(text, cross_value).astype(jnp.bfloat16)
    cq_split = cross_q.reshape(local, HEADS, HD)
    ck_split = cross_k.reshape(text_rows, HEADS, HD)
    cv_split = cross_v.reshape(text_rows, HEADS, HD)
    key_clip = jnp.arange(text_rows, dtype=jnp.int32) // TEXT
    cross_allowed = owner_mine[:, None] == key_clip[None, :]
    cross_scores = (
        jnp.einsum("qhe,khe->hqk", cq_split, ck_split, preferred_element_type=jnp.float32) * scale
    )
    cross_probs, cross_log = softmax_rows(jnp.where(cross_allowed[None], cross_scores, NEG))
    cross_mixed = (
        jnp.einsum(
            "hqk,khe->qhe",
            cross_probs.astype(jnp.bfloat16),
            cv_split,
            preferred_element_type=jnp.float32,
        )
        .reshape(local, D)
        .astype(jnp.bfloat16)
    )
    after_cross = after_self + matmul(cross_mixed, cross_output)
    normed_three, unit_three, scale_three = norm_forward(after_cross, feed_gain, feed_bias)
    normed_three_low = normed_three.astype(jnp.bfloat16)
    hidden = matmul(normed_three_low, feed_upward)
    active = jax.nn.gelu(hidden, approximate=False).astype(jnp.bfloat16)
    output = after_cross + matmul(active, feed_downward)
    upstream = grad_out[0].astype(jnp.float32)
    upstream_low = upstream.astype(jnp.bfloat16)
    grad_down = left_times(active, upstream_low)
    grad_active = right_times(upstream_low, feed_downward)
    grad_hidden = (grad_active * gelu_slope(hidden)).astype(jnp.bfloat16)
    grad_up = left_times(normed_three_low, grad_hidden)
    grad_normed_three = right_times(grad_hidden, feed_upward)
    back_three, grad_feed_gain, grad_feed_bias = norm_backward(
        grad_normed_three, unit_three, scale_three, feed_gain
    )
    grad_cross = upstream + back_three
    grad_cross_low = grad_cross.astype(jnp.bfloat16)
    grad_cross_out = left_times(cross_mixed, grad_cross_low)
    grad_mixed = (
        right_times(grad_cross_low, cross_output).astype(jnp.bfloat16).reshape(local, HEADS, HD)
    )
    grad_cross_probs = jnp.einsum(
        "qhe,khe->hqk", grad_mixed, cv_split, preferred_element_type=jnp.float32
    )
    value_part = jnp.einsum(
        "hqk,qhe->khe",
        cross_probs.astype(jnp.bfloat16),
        grad_mixed,
        preferred_element_type=jnp.float32,
    ).reshape(text_rows, D)
    inner_cross = jnp.sum(cross_probs * grad_cross_probs, axis=-1, keepdims=True)
    grad_cross_scores = (cross_probs * (grad_cross_probs - inner_cross)).astype(jnp.bfloat16)
    grad_query_cross = (
        (
            jnp.einsum(
                "hqk,khe->qhe", grad_cross_scores, ck_split, preferred_element_type=jnp.float32
            )
            * scale
        )
        .reshape(local, D)
        .astype(jnp.bfloat16)
    )
    key_part = (
        jnp.einsum("hqk,qhe->khe", grad_cross_scores, cq_split, preferred_element_type=jnp.float32)
        * scale
    ).reshape(text_rows, D)
    key_total, value_total = (
        lax.psum(key_part.astype(jnp.bfloat16), "seq").astype(jnp.float32),
        lax.psum(value_part.astype(jnp.bfloat16), "seq").astype(jnp.float32),
    )
    key_low = key_total.astype(jnp.bfloat16)
    value_low = value_total.astype(jnp.bfloat16)
    text_grad = right_times(key_low, cross_key) + right_times(value_low, cross_value)
    share = text_rows // count
    text_share = lax.dynamic_slice_in_dim(text, place * share, share, 0)
    grad_cross_key = left_times(
        text_share, lax.dynamic_slice_in_dim(key_low, place * share, share, 0)
    )
    grad_cross_value = left_times(
        text_share, lax.dynamic_slice_in_dim(value_low, place * share, share, 0)
    )
    grad_cross_query = left_times(normed_two_low, grad_query_cross)
    grad_normed_two = right_times(grad_query_cross, cross_query)
    back_two, grad_cross_gain, grad_cross_bias = norm_backward(
        grad_normed_two, unit_two, scale_two, cross_gain
    )
    grad_self = grad_cross + back_two
    grad_self_low = grad_self.astype(jnp.bfloat16)
    grad_output_w = left_times(attended_frames, grad_self_low)
    grad_attended = right_times(grad_self_low, output_weight).astype(jnp.bfloat16)
    grad_heads = lax.all_to_all(grad_attended, "seq", split_axis=1, concat_axis=0, tiled=True)

    def backward_block(carry, index):
        key_sum, value_sum = carry
        rows_q, scores, allowed = scores_of(index)
        rows_grad = lax.dynamic_slice_in_dim(grad_heads, index * block, block, 0).reshape(
            block, heads_local, HD
        )
        probs = jnp.where(allowed[None], jnp.exp(scores - log_totals[index][..., None]), 0.0)
        grad_probs = jnp.einsum(
            "qhe,khe->hqk", rows_grad, values_split, preferred_element_type=jnp.float32
        )
        value_sum = value_sum + jnp.einsum(
            "hqk,qhe->khe",
            probs.astype(jnp.bfloat16),
            rows_grad,
            preferred_element_type=jnp.float32,
        )
        inner = jnp.sum(probs * grad_probs, axis=-1, keepdims=True)
        grad_scores = (probs * (grad_probs - inner)).astype(jnp.bfloat16)
        rows_dq = (
            jnp.einsum("hqk,khe->qhe", grad_scores, keys_split, preferred_element_type=jnp.float32)
            * scale
        )
        key_sum = (
            key_sum
            + jnp.einsum("hqk,qhe->khe", grad_scores, rows_q, preferred_element_type=jnp.float32)
            * scale
        )
        return ((key_sum, value_sum), rows_dq.reshape(block, width).astype(jnp.bfloat16))

    empty = jnp.zeros((total_frames, heads_local, HD), jnp.float32)
    (key_sum, value_sum), query_blocks = lax.scan(
        backward_block, (empty, empty), jnp.arange(blocks, dtype=jnp.int32)
    )
    grad_query_heads = query_blocks.reshape(total_frames, width)
    grad_key_heads = key_sum.reshape(total_frames, width).astype(jnp.bfloat16)
    grad_value_heads = value_sum.reshape(total_frames, width).astype(jnp.bfloat16)
    grad_query, grad_key, grad_value = (
        lax.all_to_all(grad_query_heads, "seq", split_axis=0, concat_axis=1, tiled=True),
        lax.all_to_all(grad_key_heads, "seq", split_axis=0, concat_axis=1, tiled=True),
        lax.all_to_all(grad_value_heads, "seq", split_axis=0, concat_axis=1, tiled=True),
    )
    grad_query_w = left_times(normed_low, grad_query)
    grad_key_w = left_times(normed_low, grad_key)
    grad_value_w = left_times(normed_low, grad_value)
    grad_normed = (
        right_times(grad_query, query_weight)
        + right_times(grad_key, key_weight)
        + right_times(grad_value, value_weight)
    )
    back_one, grad_self_gain, grad_self_bias = norm_backward(
        grad_normed, unit_one, scale_one, self_gain
    )
    frames_grad = grad_self + back_one
    partial_sums = (
        lax.psum_scatter(grad_self_gain, "clip", scatter_dimension=0, tiled=True),
        lax.psum_scatter(grad_self_bias, "clip", scatter_dimension=0, tiled=True),
        lax.psum_scatter(grad_query_w, "clip", scatter_dimension=0, tiled=True),
        lax.psum_scatter(grad_key_w, "clip", scatter_dimension=0, tiled=True),
        lax.psum_scatter(grad_value_w, "clip", scatter_dimension=0, tiled=True),
        lax.psum_scatter(grad_output_w, "clip", scatter_dimension=0, tiled=True),
        lax.psum_scatter(grad_cross_gain, "clip", scatter_dimension=0, tiled=True),
        lax.psum_scatter(grad_cross_bias, "clip", scatter_dimension=0, tiled=True),
        lax.psum_scatter(grad_cross_query, "clip", scatter_dimension=0, tiled=True),
        lax.psum_scatter(grad_cross_key, "clip", scatter_dimension=0, tiled=True),
        lax.psum_scatter(grad_cross_value, "clip", scatter_dimension=0, tiled=True),
        lax.psum_scatter(grad_cross_out, "clip", scatter_dimension=0, tiled=True),
        lax.psum_scatter(grad_feed_gain, "clip", scatter_dimension=0, tiled=True),
        lax.psum_scatter(grad_feed_bias, "clip", scatter_dimension=0, tiled=True),
        lax.psum_scatter(grad_up, "clip", scatter_dimension=0, tiled=True),
        lax.psum_scatter(grad_down, "clip", scatter_dimension=0, tiled=True),
    )
    summed = (
        lax.psum(partial_sums[0].astype(jnp.bfloat16), "seq").astype(jnp.float32),
        lax.psum(partial_sums[1].astype(jnp.bfloat16), "seq").astype(jnp.float32),
        lax.psum(partial_sums[2].astype(jnp.bfloat16), "seq").astype(jnp.float32),
        lax.psum(partial_sums[3].astype(jnp.bfloat16), "seq").astype(jnp.float32),
        lax.psum(partial_sums[4].astype(jnp.bfloat16), "seq").astype(jnp.float32),
        lax.psum(partial_sums[5].astype(jnp.bfloat16), "seq").astype(jnp.float32),
        lax.psum(partial_sums[6].astype(jnp.bfloat16), "seq").astype(jnp.float32),
        lax.psum(partial_sums[7].astype(jnp.bfloat16), "seq").astype(jnp.float32),
        lax.psum(partial_sums[8].astype(jnp.bfloat16), "seq").astype(jnp.float32),
        lax.psum(partial_sums[9].astype(jnp.bfloat16), "seq").astype(jnp.float32),
        lax.psum(partial_sums[10].astype(jnp.bfloat16), "seq").astype(jnp.float32),
        lax.psum(partial_sums[11].astype(jnp.bfloat16), "seq").astype(jnp.float32),
        lax.psum(partial_sums[12].astype(jnp.bfloat16), "seq").astype(jnp.float32),
        lax.psum(partial_sums[13].astype(jnp.bfloat16), "seq").astype(jnp.float32),
        lax.psum(partial_sums[14].astype(jnp.bfloat16), "seq").astype(jnp.float32),
        lax.psum(partial_sums[15].astype(jnp.bfloat16), "seq").astype(jnp.float32),
    )
    return (
        output.astype(jnp.bfloat16)[None],
        frames_grad[None],
        text_grad[None],
        summed[0],
        summed[1],
        summed[2],
        summed[3],
        summed[4],
        summed[5],
        summed[6],
        summed[7],
        summed[8],
        summed[9],
        summed[10],
        summed[11],
        summed[12],
        summed[13],
        summed[14],
        summed[15],
    )


def solution(mesh):
    return jax.shard_map(
        shards,
        mesh=mesh,
        in_specs=(
            P("clip", "seq", None),
            P("clip", None, None),
            P("clip", None),
            P(),
            P(),
            P(),
            P(),
            P(),
            P(),
            P(),
            P(),
            P(),
            P(),
            P(),
            P(),
            P(),
            P(),
            P(),
            P(),
            P("clip", "seq", None),
        ),
        out_specs=(
            P("clip", "seq", None),
            P("clip", "seq", None),
            P("clip", None, None),
            P("clip"),
            P("clip"),
            P("clip", None),
            P("clip", None),
            P("clip", None),
            P("clip", None),
            P("clip"),
            P("clip"),
            P("clip", None),
            P("clip", None),
            P("clip", None),
            P("clip", None),
            P("clip"),
            P("clip"),
            P("clip", None),
            P("clip", None),
        ),
        check_vma=False,
    )
```

profile of v0, /device:TPU:0, one launch (start us, length us, event | category | flops | bytes accessed | tf_op | source)
XLA Modules:
  0.0 1239.2 jit_solution(8055833950676872411)
XLA Ops:
  15.3 5.2 all-to-all-start.1
  24.4 10.3 all-to-all-done.1
  43.0 9.4 all-to-all-done.2
  73.3 68.9 %while.30 = (s32[]{:T(128)}, bf16[4,512,256]{1,2,0:T(8,128)(2,1)}, f32[4,4,512]{2,1,0:T(4,128)}, s32[4]{0:T(128)S(1)}, s32[2048]{0:T(1024)S(1)}, /*index=5*/bf16...) while((s32[]{:T(128)}, bf16[4,512,256]{1,2,0:T(8,128)(2,1)}, ...), condition=%wide.region_8.9_spmd.clone.clone, body=%wide.region_5.8_spmd.clone.clone.sunk | while | flops 1127348736 | bytes 62467288 | solution.py:146
  168.0 7.4 fusion.122
  182.5 27.0 %fusion.30 = (bf16[512,4096]{1,0:T(8,128)(2,1)}, f32[512,4096]{1,0:T(8,128)}) fusion(bf16[1024,4096]{1,0:T(8,128)(2,1)} %param.41, f32[512,1024]{1,0:T(8,128)S(1)} %get-tuple-element.388, f32[1024]{0:T(1024)S(1)} %copy-done.74, f32[1024]{0:T(1024)S(1)} %copy-done.59, f32[512]{0:T(512)S(1)} %add_rsqrt_fusion, f32[512]{0:T(512)S(1)} %broadcast_multiply_fusion.6), kind=kOutput, calls=%fused_computation.46 | convolution fusion | flops 4433903616 | bytes 23080960 | tf_op jit(solution)/shard_map/dot_general | solution.py:20
  209.5 11.7 fusion.36
  221.3 7.6 multiply_reduce_fusion.2
  235.6 5.3 multiply_reduce_fusion.1
  240.9 5.6 fusion.78
  265.7 5.3 fusion.90
  272.2 4.9 fusion.93
  277.2 29.6 %all-reduce.15.cloned.1.call-done = (bf16[256,1024]{0,1:T(8,128)(2,1)}, bf16[256,1024]{0,1:T(8,128)(2,1)}) async-done(((bf16[256,1024]{0,1:T(8,128)(2,1)}, bf16[256,1024]{0,1:T(8,128)(2,1)}), (bf16[256,1024]{0,1:T(8,128)(2,1)}, bf16[256,1024]{0,1:T(8,128)(2,1)})) %all-reduce.15.cloned.1.call-update) | async-done | bytes 1048592 | tf_op jit(solution)/shard_map/psum | solution.py:222
  321.7 11.0 all-to-all-done.4
  333.8 267.2 %while.31 = (s32[]{:T(128)}, f32[2048,4,64]{0,2,1:T(8,128)}, f32[2048,4,64]{0,2,1:T(8,128)}, bf16[4,512,256]{1,2,0:T(8,128)(2,1)}, s32[4]{0:T(128)S(1)}, /*index...) while((s32[]{:T(128)}, f32[2048,4,64]{0,2,1:T(8,128)}, ...), condition=%wide.region_22.23_spmd.clone.clone, body=%wide.region_20.22_spmd.clone.clone.sunk | while | flops 2753296896 | bytes 179637072 | solution.py:277
  338.5 8.1 fusion.229
  352.7 12.6 %multiply_reduce_fusion.12 = (f32[4,512]{1,0:T(4,128)S(1)}, f32[4,512,2048]{2,1,0:T(8,128)}) fusion(f32[4,512,2048]{2,1,0:T(8,128)} %fusion.229, f32[4,512]{1,0:T(4,128)S(1)} %dynamic-slice_bitcast_fusion.2, pred[512,2048]{1,0:T(8,128)(4,1)S(1)} %fusion.230, bf16[512,4,64]{0,2,1:T(8,128)(2,1)} %bitcast.273, ...), kind=kOutput, calls=%fused_computation.19.clone.1 | convolution fusion | flops 557840384 | bytes 35930112 | tf_op jit(solution)/shard_map/while/body/eval_jaxpr/qhe,khe->hqk/dot_general | solution.py:254
  365.4 15.6 %multiply_convert_fusion.4 = bf16[4,512,2048]{2,1,0:T(8,128)(2,1)} fusion(f32[4,512,2048]{2,1,0:T(8,128)} %get-tuple-element.520, f32[4,512,2048]{2,1,0:T(8,128)} %fusion.229, f32[4,512]{1,0:T(4,128)S(1)} %get-tuple-element.521, f32[4,512]{1,0:T(4,128)S(1)} %dynamic-slice_bitcast_fusion.2, pred[512,2048]{1,0:T(8,128)(4,1)S(1)} %fusion.230), kind=kLoop, calls=%fused_computation.18.clone.1 | loop fusion | flops 25165824 | bytes 43008000 | tf_op jit(solution)/shard_map/while/body/eval_jaxpr/convert_element_type | solution.py:264
  381.0 6.5 fusion.231
  390.9 9.5 fusion.232
  404.7 8.1 fusion.229
  418.9 12.6 %multiply_reduce_fusion.12 = (f32[4,512]{1,0:T(4,128)S(1)}, f32[4,512,2048]{2,1,0:T(8,128)}) fusion(f32[4,512,2048]{2,1,0:T(8,128)} %fusion.229, f32[4,512]{1,0:T(4,128)S(1)} %dynamic-slice_bitcast_fusion.2, pred[512,2048]{1,0:T(8,128)(4,1)S(1)} %fusion.230, bf16[512,4,64]{0,2,1:T(8,128)(2,1)} %bitcast.273, ...), kind=kOutput, calls=%fused_computation.19.clone.1 | convolution fusion | flops 557840384 | bytes 35930112 | tf_op jit(solution)/shard_map/while/body/eval_jaxpr/qhe,khe->hqk/dot_general | solution.py:254
  431.5 15.5 %multiply_convert_fusion.4 = bf16[4,512,2048]{2,1,0:T(8,128)(2,1)} fusion(f32[4,512,2048]{2,1,0:T(8,128)} %get-tuple-element.520, f32[4,512,2048]{2,1,0:T(8,128)} %fusion.229, f32[4,512]{1,0:T(4,128)S(1)} %get-tuple-element.521, f32[4,512]{1,0:T(4,128)S(1)} %dynamic-slice_bitcast_fusion.2, pred[512,2048]{1,0:T(8,128)(4,1)S(1)} %fusion.230), kind=kLoop, calls=%fused_computation.18.clone.1 | loop fusion | flops 25165824 | bytes 43008000 | tf_op jit(solution)/shard_map/while/body/eval_jaxpr/convert_element_type | solution.py:264
  447.0 7.1 fusion.231
  457.5 10.0 fusion.232
  471.9 8.1 fusion.229
  486.1 12.7 %multiply_reduce_fusion.12 = (f32[4,512]{1,0:T(4,128)S(1)}, f32[4,512,2048]{2,1,0:T(8,128)}) fusion(f32[4,512,2048]{2,1,0:T(8,128)} %fusion.229, f32[4,512]{1,0:T(4,128)S(1)} %dynamic-slice_bitcast_fusion.2, pred[512,2048]{1,0:T(8,128)(4,1)S(1)} %fusion.230, bf16[512,4,64]{0,2,1:T(8,128)(2,1)} %bitcast.273, ...), kind=kOutput, calls=%fused_computation.19.clone.1 | convolution fusion | flops 557840384 | bytes 35930112 | tf_op jit(solution)/shard_map/while/body/eval_jaxpr/qhe,khe->hqk/dot_general | solution.py:254
  498.8 15.5 %multiply_convert_fusion.4 = bf16[4,512,2048]{2,1,0:T(8,128)(2,1)} fusion(f32[4,512,2048]{2,1,0:T(8,128)} %get-tuple-element.520, f32[4,512,2048]{2,1,0:T(8,128)} %fusion.229, f32[4,512]{1,0:T(4,128)S(1)} %get-tuple-element.521, f32[4,512]{1,0:T(4,128)S(1)} %dynamic-slice_bitcast_fusion.2, pred[512,2048]{1,0:T(8,128)(4,1)S(1)} %fusion.230), kind=kLoop, calls=%fused_computation.18.clone.1 | loop fusion | flops 25165824 | bytes 43008000 | tf_op jit(solution)/shard_map/while/body/eval_jaxpr/convert_element_type | solution.py:264
  514.3 7.0 fusion.231
  524.7 9.9 fusion.232
  538.9 8.1 fusion.229
  553.1 12.6 %multiply_reduce_fusion.12 = (f32[4,512]{1,0:T(4,128)S(1)}, f32[4,512,2048]{2,1,0:T(8,128)}) fusion(f32[4,512,2048]{2,1,0:T(8,128)} %fusion.229, f32[4,512]{1,0:T(4,128)S(1)} %dynamic-slice_bitcast_fusion.2, pred[512,2048]{1,0:T(8,128)(4,1)S(1)} %fusion.230, bf16[512,4,64]{0,2,1:T(8,128)(2,1)} %bitcast.273, ...), kind=kOutput, calls=%fused_computation.19.clone.1 | convolution fusion | flops 557840384 | bytes 35930112 | tf_op jit(solution)/shard_map/while/body/eval_jaxpr/qhe,khe->hqk/dot_general | solution.py:254
  565.7 14.8 %multiply_convert_fusion.4 = bf16[4,512,2048]{2,1,0:T(8,128)(2,1)} fusion(f32[4,512,2048]{2,1,0:T(8,128)} %get-tuple-element.520, f32[4,512,2048]{2,1,0:T(8,128)} %fusion.229, f32[4,512]{1,0:T(4,128)S(1)} %get-tuple-element.521, f32[4,512]{1,0:T(4,128)S(1)} %dynamic-slice_bitcast_fusion.2, pred[512,2048]{1,0:T(8,128)(4,1)S(1)} %fusion.230), kind=kLoop, calls=%fused_computation.18.clone.1 | loop fusion | flops 25165824 | bytes 43008000 | tf_op jit(solution)/shard_map/while/body/eval_jaxpr/convert_element_type | solution.py:264
  580.5 7.0 fusion.231
  590.9 9.9 fusion.232
  603.8 16.7 %all_to_all.134 = bf16[4,512,256]{1,2,0:T(8,128)(2,1)S(1)} all-to-all(bf16[4,512,256]{1,2,0:T(8,128)(2,1)S(1)} %copy.136), channel_id=1, replica_groups=mesh['seq'=4,'clip'=8] {'seq'}, dimensions={0} | all-to-all | bytes 2097152 | tf_op jit(solution)/shard_map/all_to_all | solution.py:285
  626.9 14.6 %all_to_all.135 = bf16[4,512,256]{1,2,0:T(8,128)(2,1)S(1)} all-to-all(bf16[4,512,256]{1,2,0:T(8,128)(2,1)S(1)} %copy.137), channel_id=1, replica_groups=mesh['seq'=4,'clip'=8] {'seq'}, dimensions={0} | all-to-all | bytes 2097152 | tf_op jit(solution)/shard_map/all_to_all | solution.py:286
  646.3 13.4 %all_to_all.136 = bf16[4,512,256]{1,2,0:T(8,128)(2,1)S(1)} all-to-all(bf16[4,512,256]{1,2,0:T(8,128)(2,1)S(1)} %copy-done.22), channel_id=1, replica_groups=mesh['seq'=4,'clip'=8] {'seq'}, dimensions={0} | all-to-all | bytes 2097152 | tf_op jit(solution)/shard_map/all_to_all | solution.py:284
  664.9 10.5 fusion.110
  675.5 12.8 %fusion.83 = f32[4096,1024]{1,0:T(8,128)} fusion(bf16[512,4096]{1,0:T(8,128)(2,1)} %get-tuple-element.389, bf16[1,512,1024]{2,1,0:T(8,128)(2,1)} %param.43), kind=kOutput, calls=%fused_computation.144 | convolution fusion | flops 4294967296 | bytes 22020096 | tf_op jit(solution)/shard_map/dot_general | solution.py:24
  701.0 22.8 %reduce-scatter.15.cloned.1.call-done = f32[128,1024]{1,0:T(8,128)} async-done(((f32[1024,1024]{1,0:T(8,128)}), f32[128,1024]{1,0:T(8,128)}) %reduce-scatter.15.cloned.1.call-update) | async-done | bytes 524304 | tf_op jit(solution)/shard_map/reduce_scatter | solution.py:305
  725.6 48.4 %reduce-scatter.11.cloned.1.call-done = f32[128,1024]{1,0:T(8,128)} async-done(((f32[1024,1024]{1,0:T(8,128)}), f32[128,1024]{1,0:T(8,128)}) %reduce-scatter.11.cloned.1.call-update) | async-done | bytes 524304 | tf_op jit(solution)/shard_map/reduce_scatter | solution.py:303
  775.8 166.7 %reduce-scatter.27.cloned.1.call-done = f32[128,4096]{1,0:T(8,128)} async-done(((f32[1024,4096]{1,0:T(8,128)}), f32[128,4096]{1,0:T(8,128)}) %reduce-scatter.27.cloned.1.call-update) | async-done | bytes 2097168 | tf_op jit(solution)/shard_map/reduce_scatter | solution.py:315
  945.2 166.2 %reduce-scatter.29.cloned.1.call-done = f32[512,1024]{1,0:T(8,128)} async-done(((f32[4096,1024]{1,0:T(8,128)}), f32[512,1024]{1,0:T(8,128)}) %reduce-scatter.29.cloned.1.call-update) | async-done | bytes 2097168 | tf_op jit(solution)/shard_map/reduce_scatter | solution.py:316
  1114.1 10.8 fusion.76
  1136.2 26.0 %all-reduce.6 = (bf16[1024]{0:T(1024)(128)(2,1)S(1)}, bf16[1024]{0:T(1024)(128)(2,1)S(1)}, bf16[1024]{0:T(1024)(128)(2,1)S(1)}, bf16[1024]{0:T(1024)(128)(2,1)S(...) all-reduce(f32[1024]{0:T(1024)S(1)} %get-tuple-element.309, ...), channel_id=2, replica_groups=mesh['seq'=4,'clip'=8] {'clip'}, use_global_device_ids=true, to_apply=%region_28.29.clone | all-reduce | flops 6144 | bytes 36864
  1162.7 9.8 all-reduce.7
  1179.2 41.1 %all-reduce.13.cloned.1.call-done = (bf16[128,1024]{1,0:T(8,128)(2,1)}, bf16[128,1024]{1,0:T(8,128)(2,1)}, bf16[128,1024]{1,0:T(8,128)(2,1)}, bf16[128,1024]{1,0...) async-done(((bf16[128,1024]{1,0:T(8,128)(2,1)}, ...) | async-done | bytes 4194320 | tf_op jit(solution)/shard_map/psum | solution.py:321
  (405 shorter events, 296.4 us)
Async XLA Ops:
  8.0 156.2 %copy-start = (bf16[1024,1024]{1,0:T(8,128)(2,1)S(1)}, bf16[1024,1024]{1,0:T(8,128)(2,1)}, u32[]{:S(2)}) copy-start(bf16[1024,1024]{1,0:T(8,128)(2,1)} %param.35) | copy-start | bytes 6291460
  9.7 29.3 %copy-start.50 = (f32[512]{0:T(512)}, f32[512]{0:T(512)S(1)}, u32[]{:S(2)}) copy-start(f32[512]{0:T(512)S(1)} %broadcast_multiply_fusion.8) | copy-start | bytes 6148
  11.4 27.7 %copy-start.54 = (f32[512]{0:T(512)}, f32[512]{0:T(512)S(1)}, u32[]{:S(2)}) copy-start(f32[512]{0:T(512)S(1)} %add_rsqrt_fusion.2) | copy-start | bytes 6148
  15.3 19.4 %all-to-all-start.1 = ((bf16[512,4,256]{2,0,1:T(8,128)(2,1)}), bf16[512,4,256]{2,0,1:T(8,128)(2,1)}, u32[]{:S(2)}, u32[]{:S(2)}) async-start(bf16[512,4,256]{2,0,1:T(8,128)(2,1)} %bitcast.278), calls=%async_computation.1 | async-start | bytes 2097152 | tf_op jit(solution)/shard_map/all_to_all | solution.py:113
  34.8 17.7 %all-to-all-start.2 = ((bf16[512,4,256]{2,0,1:T(8,128)(2,1)}), bf16[512,4,256]{2,0,1:T(8,128)(2,1)}, u32[]{:S(2)}, u32[]{:S(2)}) async-start(bf16[512,4,256]{2,0,1:T(8,128)(2,1)} %bitcast.277), calls=%async_computation.2 | async-start | bytes 2097152 | tf_op jit(solution)/shard_map/all_to_all | solution.py:114
  41.9 15.0 %copy-start.76 = (s32[1,4]{1,0:T(1,128)S(1)}, s32[1,4]{1,0:T(1,128)}, u32[]{:S(2)}) copy-start(s32[1,4]{1,0:T(1,128)} %param.26) | copy-start | bytes 52
  52.4 17.6 %all-to-all-start = ((bf16[512,4,256]{2,0,1:T(8,128)(2,1)}), bf16[512,4,256]{2,0,1:T(8,128)(2,1)}, u32[]{:S(2)}, u32[]{:S(2)}) async-start(bf16[512,4,256]{2,0,1:T(8,128)(2,1)} %bitcast.223), calls=%async_computation | async-start | bytes 2097152 | tf_op jit(solution)/shard_map/all_to_all | solution.py:112
  142.2 8.0 copy-start.3
  142.2 8.0 copy-start.48
  142.2 17.4 %all-to-all-start.3 = ((bf16[4,512,256]{1,2,0:T(8,128)(2,1)}), bf16[4,512,256]{1,2,0:T(8,128)(2,1)}, u32[]{:S(2)}, u32[]{:S(2)}) async-start(bf16[4,512,256]{1,2,0:T(8,128)(2,1)} %get-tuple-element.137), calls=%async_computation.3 | async-start | bytes 2097152 | tf_op jit(solution)/shard_map/all_to_all | solution.py:148
  146.4 160.4 %all-reduce.15.cloned.1.call-start = ((), (), s32[]{:S(2)}) async-start(), calls=%async_computation.29 | async-start | bytes 2097152 | tf_op jit(solution)/shard_map/psum | solution.py:222
  153.0 6.7 copy-start.18
  180.2 41.1 %slice-start = ((s8[8388608]{0:T(1024)(128)(4,1)}), s8[4194304]{0:T(1024)(128)(4,1)S(1)}, s32[]{:S(2)}) async-start(s8[8388608]{0:T(1024)(128)(4,1)} %bitcast.304), calls=%async_computation.30 | async-start | bytes 8388608
  181.5 47.3 %copy-start.20 = (f32[512,1024]{1,0:T(8,128)}, f32[512,1024]{1,0:T(8,128)S(1)}, u32[]{:S(2)}) copy-start(f32[512,1024]{1,0:T(8,128)S(1)} %get-tuple-element.388) | copy-start | bytes 6291460
  181.6 47.3 %copy-start.52 = (f32[512]{0:T(512)}, f32[512]{0:T(512)S(1)}, u32[]{:S(2)}) copy-start(f32[512]{0:T(512)S(1)} %broadcast_multiply_fusion.6) | copy-start | bytes 6148
  182.5 46.4 %copy-start.56 = (f32[512]{0:T(512)}, f32[512]{0:T(512)S(1)}, u32[]{:S(2)}) copy-start(f32[512]{0:T(512)S(1)} %add_rsqrt_fusion) | copy-start | bytes 6148
  182.5 27.0 %copy-start.38 = (bf16[1,512,1024]{2,1,0:T(8,128)(2,1)S(1)}, bf16[1,512,1024]{2,1,0:T(8,128)(2,1)}, u32[]{:S(2)}) copy-start(bf16[1,512,1024]{2,1,0:T(8,128)(2,1)} %param.43) | copy-start | bytes 3145732
  182.5 38.8 %slice-start.1 = ((s8[8388608]{0:T(1024)(128)(4,1)}), s8[4194304]{0:T(1024)(128)(4,1)S(1)}, s32[]{:S(2)}) async-start(s8[8388608]{0:T(1024)(128)(4,1)} %bitcast.304), calls=%async_computation.31 | async-start | bytes 8388608
  235.6 5.3 copy-start.37
  253.4 436.9 %reduce-scatter.19.cloned.1.call-start = ((), (), s32[]{:S(2)}) async-start(), calls=%async_computation.22 | async-start | bytes 4718592 | tf_op jit(solution)/shard_map/reduce_scatter | solution.py:309
  260.6 431.5 %reduce-scatter.17.cloned.1.call-start = ((), (), s32[]{:S(2)}) async-start(), calls=%async_computation.21 | async-start | bytes 4718592 | tf_op jit(solution)/shard_map/reduce_scatter | solution.py:306
  265.7 44.9 %copy-start.9 = (f32[512,1024]{1,0:T(8,128)}, f32[512,1024]{1,0:T(8,128)S(1)}, u32[]{:S(2)}) copy-start(f32[512,1024]{1,0:T(8,128)S(1)} %multiply_add_fusion) | copy-start | bytes 6291460
  271.0 422.8 %reduce-scatter.25.cloned.1.call-start = ((), (), s32[]{:S(2)}) async-start(), calls=%async_computation.25 | async-start | bytes 4718592 | tf_op jit(solution)/shard_map/reduce_scatter | solution.py:312
  277.1 29.7 %copy-start.47 = (bf16[1,256,1024]{2,1,0:T(8,128)(2,1)S(1)}, bf16[1,256,1024]{2,1,0:T(8,128)(2,1)}, u32[]{:S(2)}) copy-start(bf16[1,256,1024]{2,1,0:T(8,128)(2,1)} %param.25) | copy-start | bytes 1572868
  277.1 418.5 %reduce-scatter.21.cloned.1.call-start = ((), (), s32[]{:S(2)}) async-start(), calls=%async_computation.23 | async-start | bytes 4718592 | tf_op jit(solution)/shard_map/reduce_scatter | solution.py:310
  313.4 5.4 copy-start.27
  314.5 18.2 %all-to-all-start.4 = ((bf16[512,4,256]{2,0,1:T(8,128)(2,1)}), bf16[512,4,256]{2,0,1:T(8,128)(2,1)}, u32[]{:S(2)}, u32[]{:S(2)}) async-start(bf16[512,4,256]{2,0,1:T(8,128)(2,1)} %bitcast.220), calls=%async_computation.4 | async-start | bytes 2097152 | tf_op jit(solution)/shard_map/all_to_all | solution.py:245
  318.8 378.6 %reduce-scatter.23.cloned.1.call-start = ((), (), s32[]{:S(2)}) async-start(), calls=%async_computation.24 | async-start | bytes 4718592 | tf_op jit(solution)/shard_map/reduce_scatter | solution.py:311
  321.6 12.1 copy-start.4
  321.6 12.1 copy-start.6
  321.7 377.5 %reduce-scatter.13.cloned.1.call-start = ((), (), s32[]{:S(2)}) async-start(), calls=%async_computation.19 | async-start | bytes 4718592 | tf_op jit(solution)/shard_map/reduce_scatter | solution.py:304
  381.0 6.5 copy-start.2
  447.0 7.1 copy-start.2
  514.3 7.0 copy-start.2
  580.5 7.0 copy-start.2
  603.5 17.0 %copy-start.19 = (bf16[1,512,1024]{2,1,0:T(8,128)(2,1)S(1)}, bf16[1,512,1024]{2,1,0:T(8,128)(2,1)}, u32[]{:S(2)}) copy-start(bf16[1,512,1024]{2,1,0:T(8,128)(2,1)} %param.24) | copy-start | bytes 3145732
  603.5 17.0 %copy-start.51 = (f32[512]{0:T(512)S(1)}, f32[512]{0:T(512)}, u32[]{:S(2)}) copy-start(f32[512]{0:T(512)} %copy-done.50) | copy-start | bytes 6148
  603.5 16.9 %copy-start.55 = (f32[512]{0:T(512)S(1)}, f32[512]{0:T(512)}, u32[]{:S(2)}) copy-start(f32[512]{0:T(512)} %copy-done.54) | copy-start | bytes 6148
  603.6 16.9 %copy-start.62 = (f32[1024]{0:T(1024)S(1)}, f32[1024]{0:T(1024)}, u32[]{:S(2)}) copy-start(f32[1024]{0:T(1024)} %param.27) | copy-start | bytes 12292
  603.6 16.9 %copy-start.73 = (f32[1024]{0:T(1024)S(1)}, f32[1024]{0:T(1024)}, u32[]{:S(2)}) copy-start(f32[1024]{0:T(1024)} %param.28) | copy-start | bytes 12292
  624.1 99.7 %reduce-scatter.15.cloned.1.call-start = ((), (), s32[]{:S(2)}) async-start(), calls=%async_computation.20 | async-start | bytes 4718592 | tf_op jit(solution)/shard_map/reduce_scatter | solution.py:305
  645.1 128.9 %reduce-scatter.11.cloned.1.call-start = ((), (), s32[]{:S(2)}) async-start(), calls=%async_computation.18 | async-start | bytes 4718592 | tf_op jit(solution)/shard_map/reduce_scatter | solution.py:303
  663.3 279.1 %reduce-scatter.27.cloned.1.call-start = ((), (), s32[]{:S(2)}) async-start(), calls=%async_computation.26 | async-start | bytes 18874368 | tf_op jit(solution)/shard_map/reduce_scatter | solution.py:315
  675.5 435.9 %reduce-scatter.29.cloned.1.call-start = ((), (), s32[]{:S(2)}) async-start(), calls=%async_computation.27 | async-start | bytes 18874368 | tf_op jit(solution)/shard_map/reduce_scatter | solution.py:316
  688.4 531.9 %all-reduce.13.cloned.1.call-start = ((), (), s32[]{:S(2)}) async-start(), calls=%async_computation.28 | async-start | bytes 8388608 | tf_op jit(solution)/shard_map/psum | solution.py:321
  1114.1 10.8 copy-start.25
  1114.1 10.8 copy-start.29
  1133.0 42.6 %copy-start.10 = (f32[512,1024]{1,0:T(8,128)S(1)}, f32[512,1024]{1,0:T(8,128)}, u32[]{:S(2)}) copy-start(f32[512,1024]{1,0:T(8,128)} %copy-done.9) | copy-start | bytes 6291460
  (58 other events, 160.4 us)
Sparse Core Ops, SparseCore 0:
  253.5 53.2 all-reduce.14
  1114.2 105.9 all-reduce.12
Sparse Core Ops, SparseCore 1:
  260.7 50.3 reduce-scatter.18
  313.2 47.9 reduce-scatter.16
  363.4 48.0 reduce-scatter.24
  413.7 48.0 reduce-scatter.20
  464.1 47.9 reduce-scatter.22
  624.2 49.3 reduce-scatter.12
  675.8 48.0 reduce-scatter.14
  726.0 48.0 reduce-scatter.10
  776.2 166.2 reduce-scatter.26
  944.8 166.5 reduce-scatter.28
where the time goes:
time: 1250 us; the launch traced here: 1240 us
  waiting for transfers between devices  509 us (41%)
  matrix products  372 us (30%)
  other arithmetic  143 us (11%)
  blocking collectives  80.5 us (6%)
  local copies, waits for them, and re-layouts  79.1 us (6%)
  starting transfers between devices  23.7 us (2%)
  between operations  17.3 us (1%)
  loops' own time  13.8 us (1%)
    reduce_scatter x1, waiting for transfers between devices, shards(): lax.psum_scatter(grad_up, 'clip', scatter_dimension=0, tiled=True)  167 us
    reduce_scatter x1, waiting for transfers between devices, shards(): lax.psum_scatter(grad_down, 'clip', scatter_dimension=0, tiled=True)  166 us
    convert_element_type x4, other arithmetic, backward_block(): grad_scores = (probs * (grad_probs - inner)).astype(jnp.bfloat16)  61.5 us
    dot_general x10, matrix products, matmul(): return jnp.dot(left, right, preferred_element_type=jnp.float32)  60.1 us
    dot_general x10, matrix products, left_times(): lax.dot_general(left, right, (((0,), (0,)), ((), ())), preferred_element_...  54.2 us
    dot_general x4, matrix products, backward_block(): jnp.einsum('qhe,khe->hqk', rows_grad, values_split, preferred_element_typ...  50.5 us
    reduce_scatter x1, waiting for transfers between devices, shards(): lax.psum_scatter(grad_query_w, 'clip', scatter_dimension=0, tiled=True)  48.4 us
    dot_general x8, matrix products, scores_of(): jnp.einsum('qhe,khe->hqk', rows_q, keys_split, preferred_element_type=jnp...  45.3 us
  transfers between devices with their start and end apart: 17, of which 11 were waited for; matrix products, arithmetic and copies ran while one was open for 32% of the time, Pallas kernels for 0%

commit v1 on v0

--- a/solution.py
+++ b/solution.py
@@ -1,6 +1,10 @@
+import math
+
 import jax
 import jax.numpy as jnp
 from jax import lax
+from jax.experimental import pallas as pl
+from jax.experimental.pallas import tpu as pltpu
 from jax.sharding import PartitionSpec as P
 
 D = 1024
@@ -14,6 +18,125 @@
 NEG = -1e30
 SQRT_HALF = 0.7071067811865476
 INV_ROOT_TWO_PI = 0.3989422804014327
+
+bf = jnp.bfloat16
+f32 = jnp.float32
+T, W, H, B = 2048, 256, 4, 256
+C2 = math.log2(math.e) / 8.0
+NT = (((1,), (1,)), ((), ()))
+NN = (((1,), (0,)), ((), ()))
+TN = (((0,), (0,)), ((), ()))
+
+
+def dg(a, b, d):
+    return lax.dot_general(a, b, d, preferred_element_type=f32)
+
+
+def lanemask(rows,h):
+    l=lax.broadcasted_iota(jnp.int32,(rows,W),1)
+    return (l//HD)==h
+def fwd_kernel(q_ref,k_ref,v_ref,first_ref,o_ref,lse_ref,s_ref):
+    nb=T//B
+    def qblock(i,masked):
+        r0=pl.multiple_of(i*B,B)
+        q=q_ref[pl.ds(r0,B),:]
+        row=lax.broadcasted_iota(jnp.int32,(B,B),0); col=lax.broadcasted_iota(jnp.int32,(B,B),1)
+        qm=[jnp.where(lanemask(B,h),q,jnp.zeros_like(q)) for h in range(H)]
+        fst=first_ref[pl.ds(r0,B),:]
+        def scores(j,carry,diag):
+            c0=pl.multiple_of(j*B,B)
+            k=k_ref[pl.ds(c0,B),:]
+            out=[]
+            for h in range(H):
+                s=dg(qm[h],k,NT)
+                if diag: s=jnp.where(col<=row,s,NEG)
+                if masked: s=jnp.where(col+c0>=fst,s,NEG)
+                s_ref[h,:,pl.ds(c0,B)]=s
+                m=jnp.maximum(s[:,:128],s[:,128:])
+                out.append(jnp.maximum(carry[h],m))
+            return tuple(out)
+        m=tuple(jnp.full((B,128),NEG,f32) for _ in range(H))
+        m=lax.fori_loop(0,i,lambda j,c:scores(j,c,False),m)
+        m=scores(i,m,True)
+        m=[jnp.max(x,axis=1,keepdims=True) for x in m]
+        def mix(j,carry):
+            acc,ls=carry
+            c0=pl.multiple_of(j*B,B)
+            v=v_ref[pl.ds(c0,B),:]
+            acc=list(acc); ls=list(ls)
+            for h in range(H):
+                p=jnp.exp2((s_ref[h,:,pl.ds(c0,B)]-m[h])*C2)
+                ls[h]=ls[h]+p[:,:128]+p[:,128:]
+                acc[h]=acc[h]+dg(p.astype(bf),v,NN)
+            return tuple(acc),tuple(ls)
+        acc,ls=lax.fori_loop(0,i+1,mix,(tuple(jnp.zeros((B,W),f32) for _ in range(H)),tuple(jnp.zeros((B,128),f32) for _ in range(H))))
+        o=jnp.zeros((B,W),f32)
+        lane=lax.broadcasted_iota(jnp.int32,(B,128),1)
+        lse=jnp.zeros((B,128),f32)
+        for h in range(H):
+            l=jnp.sum(ls[h],axis=1,keepdims=True)
+            o=jnp.where(lanemask(B,h),acc[h]/l,o)
+            lse=jnp.where(lane==h,m[h]*C2+jnp.log2(l),lse)
+        o_ref[pl.ds(r0,B),:]=o.astype(bf)
+        lse_ref[:,pl.ds(r0,B)]=lse.T[:8]
+    def body(i,c): qblock(i,False); return c
+    lax.fori_loop(0,6,body,0)
+    def body2(i,c): qblock(i,True); return c
+    lax.fori_loop(6,8,body2,0)
+def fwd(q,k,v,first):
+    return pl.pallas_call(fwd_kernel,out_shape=(jax.ShapeDtypeStruct((T,W),bf),jax.ShapeDtypeStruct((8,T),f32)),
+      in_specs=[pl.BlockSpec(memory_space=pltpu.VMEM)]*4,out_specs=(pl.BlockSpec(memory_space=pltpu.VMEM),)*2,
+      scratch_shapes=[pltpu.VMEM((H,B,T),f32)],
+      compiler_params=pltpu.CompilerParams(vmem_limit_bytes=48<<20))(q,k,v,first)
+
+def bwd_kernel(q_ref,k_ref,v_ref,o_ref,g_ref,lse_ref,first_ref,dq_ref,dk_ref,dv_ref,dka,dva):
+    nb=T//B
+    dka[...]=jnp.zeros_like(dka); dva[...]=jnp.zeros_like(dva)
+    def qblock(i,masked):
+        r0=pl.multiple_of(i*B,B)
+        q=q_ref[pl.ds(r0,B),:]; g=g_ref[pl.ds(r0,B),:]
+        go=g.astype(f32)*o_ref[pl.ds(r0,B),:].astype(f32)
+        hm=(lax.broadcasted_iota(jnp.int32,(8,W),1)//HD==lax.broadcasted_iota(jnp.int32,(8,W),0)).astype(f32)
+        delta=lax.dot_general(hm,go,NT,precision=lax.Precision.HIGHEST,preferred_element_type=f32)
+        lse=lse_ref[:,pl.ds(r0,B)]
+        fst=first_ref[:,pl.ds(r0,B)]
+        zero=jnp.zeros_like(q)
+        qm=[jnp.where(lanemask(B,h),q,zero) for h in range(H)]
+        gm=[jnp.where(lanemask(B,h),g,zero) for h in range(H)]
+        kvi=lax.broadcasted_iota(jnp.int32,(B,B),0); qi=lax.broadcasted_iota(jnp.int32,(B,B),1)
+        def tile(j,dq,diag):
+            c0=pl.multiple_of(j*B,B)
+            k=k_ref[pl.ds(c0,B),:]; v=v_ref[pl.ds(c0,B),:]
+            dv=jnp.zeros((B,W),f32); dk=jnp.zeros((B,W),f32)
+            for h in range(H):
+                st=dg(k,qm[h],NT)
+                p=jnp.exp2(st*C2-lse[h:h+1])
+                if diag: p=jnp.where(kvi<=qi,p,0.0)
+                if masked: p=jnp.where(kvi+c0>=fst,p,0.0)
+                dp=dg(v,gm[h],NT)
+                ds=(p*(dp-delta[h:h+1])).astype(bf)
+                dv=dv+dg(p.astype(bf),gm[h],NN)
+                dk=dk+dg(ds,qm[h],NN)
+                km=jnp.where(lanemask(B,h),k,zero)
+                dq=dq+dg(ds,km,TN)
+            dva[pl.ds(c0,B),:]+=dv
+            dka[pl.ds(c0,B),:]+=dk
+            return dq
+        dq=jnp.zeros((B,W),f32)
+        dq=lax.fori_loop(0,i,lambda j,c:tile(j,c,False),dq)
+        dq=tile(i,dq,True)
+        dq_ref[pl.ds(r0,B),:]=(dq*0.125).astype(bf)
+    def body(i,c): qblock(i,False); return c
+    lax.fori_loop(0,6,body,0)
+    def body2(i,c): qblock(i,True); return c
+    lax.fori_loop(6,8,body2,0)
+    dk_ref[...]=(dka[...]*0.125).astype(bf); dv_ref[...]=dva[...].astype(bf)
+def bwd(q,k,v,o,g,lse,first):
+    o1=jax.ShapeDtypeStruct((T,W),bf)
+    return pl.pallas_call(bwd_kernel,out_shape=(o1,o1,o1),
+      in_specs=[pl.BlockSpec(memory_space=pltpu.VMEM)]*7,out_specs=(pl.BlockSpec(memory_space=pltpu.VMEM),)*3,
+      scratch_shapes=[pltpu.VMEM((T,W),f32)]*2,
+      compiler_params=pltpu.CompilerParams(vmem_limit_bytes=48<<20))(q,k,v,o,g,lse,first)
 
 
 def matmul(left, right):
@@ -93,7 +216,8 @@
     blocks = total_frames // block
     scale = HD ** (-0.5)
     lengths = clip_lengths[0]
-    ends = jnp.cumsum(lengths)
+    slot = jnp.arange(CLIPS, dtype=jnp.int32)
+    ends = jnp.sum(jnp.where(slot[None, :] <= slot[:, None], lengths[None, :], 0), axis=1)
     begins = ends - lengths
     slots = jnp.arange(CLIPS, dtype=jnp.int32)
     positions = jnp.arange(total_frames, dtype=jnp.int32)
@@ -118,33 +242,7 @@
     keys_split = key_heads.reshape(total_frames, heads_local, HD)
     values_split = value_heads.reshape(total_frames, heads_local, HD)
 
-    def scores_of(index):
-        start = index * block
-        rows_q = lax.dynamic_slice_in_dim(query_heads, start, block, 0).reshape(
-            block, heads_local, HD
-        )
-        scores = (
-            jnp.einsum("qhe,khe->hqk", rows_q, keys_split, preferred_element_type=jnp.float32)
-            * scale
-        )
-        rows = start + jnp.arange(block, dtype=jnp.int32)
-        lower = lax.dynamic_slice_in_dim(first_all, start, block, 0)
-        allowed = (positions[None, :] <= rows[:, None]) & (positions[None, :] >= lower[:, None])
-        return (rows_q, scores, allowed)
-
-    def attend(index):
-        rows_q, scores, allowed = scores_of(index)
-        probs, log_total = softmax_rows(jnp.where(allowed[None], scores, NEG))
-        mixed = jnp.einsum(
-            "hqk,khe->qhe",
-            probs.astype(jnp.bfloat16),
-            values_split,
-            preferred_element_type=jnp.float32,
-        )
-        return (mixed.reshape(block, width).astype(jnp.bfloat16), log_total)
-
-    mixed_blocks, log_totals = lax.map(attend, jnp.arange(blocks, dtype=jnp.int32))
-    attended = mixed_blocks.reshape(total_frames, width)
+    attended, log_totals = fwd(query_heads, key_heads, value_heads, first_all[:, None])
     attended_frames = lax.all_to_all(attended, "seq", split_axis=0, concat_axis=1, tiled=True)
     after_self = frames + matmul(attended_frames, output_weight)
     normed_two, unit_two, scale_two = norm_forward(after_self, cross_gain, cross_bias)
@@ -244,42 +342,9 @@
     grad_attended = right_times(grad_self_low, output_weight).astype(jnp.bfloat16)
     grad_heads = lax.all_to_all(grad_attended, "seq", split_axis=1, concat_axis=0, tiled=True)
 
-    def backward_block(carry, index):
-        key_sum, value_sum = carry
-        rows_q, scores, allowed = scores_of(index)
-        rows_grad = lax.dynamic_slice_in_dim(grad_heads, index * block, block, 0).reshape(
-            block, heads_local, HD
-        )
-        probs = jnp.where(allowed[None], jnp.exp(scores - log_totals[index][..., None]), 0.0)
-        grad_probs = jnp.einsum(
-            "qhe,khe->hqk", rows_grad, values_split, preferred_element_type=jnp.float32
-        )
-        value_sum = value_sum + jnp.einsum(
-            "hqk,qhe->khe",
-            probs.astype(jnp.bfloat16),
-            rows_grad,
-            preferred_element_type=jnp.float32,
-        )
-        inner = jnp.sum(probs * grad_probs, axis=-1, keepdims=True)
-        grad_scores = (probs * (grad_probs - inner)).astype(jnp.bfloat16)
-        rows_dq = (
-            jnp.einsum("hqk,khe->qhe", grad_scores, keys_split, preferred_element_type=jnp.float32)
-            * scale
-        )
-        key_sum = (
-            key_sum
-            + jnp.einsum("hqk,qhe->khe", grad_scores, rows_q, preferred_element_type=jnp.float32)
-            * scale
-        )
-        return ((key_sum, value_sum), rows_dq.reshape(block, width).astype(jnp.bfloat16))
-
-    empty = jnp.zeros((total_frames, heads_local, HD), jnp.float32)
-    (key_sum, value_sum), query_blocks = lax.scan(
-        backward_block, (empty, empty), jnp.arange(blocks, dtype=jnp.int32)
-    )
-    grad_query_heads = query_blocks.reshape(total_frames, width)
-    grad_key_heads = key_sum.reshape(total_frames, width).astype(jnp.bfloat16)
-    grad_value_heads = value_sum.reshape(total_frames, width).astype(jnp.bfloat16)
+    grad_query_heads, grad_key_heads, grad_value_heads = bwd(
+        query_heads, key_heads, value_heads, attended, grad_heads, log_totals, first_all[None]
+    )
     grad_query, grad_key, grad_value = (
         lax.all_to_all(grad_query_heads, "seq", split_axis=0, concat_axis=1, tiled=True),
         lax.all_to_all(grad_key_heads, "seq", split_axis=0, concat_axis=1, tiled=True),
@@ -297,41 +362,30 @@
         grad_normed, unit_one, scale_one, self_gain
     )
     frames_grad = grad_self + back_one
-    partial_sums = (
-        lax.psum_scatter(grad_self_gain, "clip", scatter_dimension=0, tiled=True),
-        lax.psum_scatter(grad_self_bias, "clip", scatter_dimension=0, tiled=True),
-        lax.psum_scatter(grad_query_w, "clip", scatter_dimension=0, tiled=True),
-        lax.psum_scatter(grad_key_w, "clip", scatter_dimension=0, tiled=True),
-        lax.psum_scatter(grad_value_w, "clip", scatter_dimension=0, tiled=True),
-        lax.psum_scatter(grad_output_w, "clip", scatter_dimension=0, tiled=True),
-        lax.psum_scatter(grad_cross_gain, "clip", scatter_dimension=0, tiled=True),
-        lax.psum_scatter(grad_cross_bias, "clip", scatter_dimension=0, tiled=True),
-        lax.psum_scatter(grad_cross_query, "clip", scatter_dimension=0, tiled=True),
-        lax.psum_scatter(grad_cross_key, "clip", scatter_dimension=0, tiled=True),
-        lax.psum_scatter(grad_cross_value, "clip", scatter_dimension=0, tiled=True),
-        lax.psum_scatter(grad_cross_out, "clip", scatter_dimension=0, tiled=True),
-        lax.psum_scatter(grad_feed_gain, "clip", scatter_dimension=0, tiled=True),
-        lax.psum_scatter(grad_feed_bias, "clip", scatter_dimension=0, tiled=True),
-        lax.psum_scatter(grad_up, "clip", scatter_dimension=0, tiled=True),
-        lax.psum_scatter(grad_down, "clip", scatter_dimension=0, tiled=True),
-    )
+    def reduce_matrix(part):
+        part = lax.psum_scatter(part.astype(bf), "clip", scatter_dimension=0, tiled=True)
+        return lax.psum(part, "seq").astype(f32)
+
+    vectors = lax.psum(jnp.stack([grad_self_gain, grad_self_bias, grad_cross_gain, grad_cross_bias, grad_feed_gain, grad_feed_bias]), ("clip", "seq"))
+    width_out = vectors.shape[1] // lax.axis_size("clip")
+    vectors = lax.dynamic_slice_in_dim(vectors, lax.axis_index("clip") * width_out, width_out, 1)
     summed = (
-        lax.psum(partial_sums[0].astype(jnp.bfloat16), "seq").astype(jnp.float32),
-        lax.psum(partial_sums[1].astype(jnp.bfloat16), "seq").astype(jnp.float32),
-        lax.psum(partial_sums[2].astype(jnp.bfloat16), "seq").astype(jnp.float32),
-        lax.psum(partial_sums[3].astype(jnp.bfloat16), "seq").astype(jnp.float32),
-        lax.psum(partial_sums[4].astype(jnp.bfloat16), "seq").astype(jnp.float32),
-        lax.psum(partial_sums[5].astype(jnp.bfloat16), "seq").astype(jnp.float32),
-        lax.psum(partial_sums[6].astype(jnp.bfloat16), "seq").astype(jnp.float32),
-        lax.psum(partial_sums[7].astype(jnp.bfloat16), "seq").astype(jnp.float32),
-        lax.psum(partial_sums[8].astype(jnp.bfloat16), "seq").astype(jnp.float32),
-        lax.psum(partial_sums[9].astype(jnp.bfloat16), "seq").astype(jnp.float32),
-        lax.psum(partial_sums[10].astype(jnp.bfloat16), "seq").astype(jnp.float32),
-        lax.psum(partial_sums[11].astype(jnp.bfloat16), "seq").astype(jnp.float32),
-        lax.psum(partial_sums[12].astype(jnp.bfloat16), "seq").astype(jnp.float32),
-        lax.psum(partial_sums[13].astype(jnp.bfloat16), "seq").astype(jnp.float32),
-        lax.psum(partial_sums[14].astype(jnp.bfloat16), "seq").astype(jnp.float32),
-        lax.psum(partial_sums[15].astype(jnp.bfloat16), "seq").astype(jnp.float32),
+        vectors[0],
+        vectors[1],
+        reduce_matrix(grad_query_w),
+        reduce_matrix(grad_key_w),
+        reduce_matrix(grad_value_w),
+        reduce_matrix(grad_output_w),
+        vectors[2],
+        vectors[3],
+        reduce_matrix(grad_cross_query),
+        reduce_matrix(grad_cross_key),
+        reduce_matrix(grad_cross_value),
+        reduce_matrix(grad_cross_out),
+        vectors[4],
+        vectors[5],
+        reduce_matrix(grad_up),
+        reduce_matrix(grad_down),
     )
     return (
         output.astype(jnp.bfloat16)[None],

time: 1250 us -> 837 us (0.67)
  matrix products: 372 us -> 174 us
  waiting for transfers between devices: 509 us -> 360 us
  other arithmetic: 143 us -> 25.6 us
  Pallas kernels: 0 us -> 92.1 us
  local copies, waits for them, and re-layouts: 79.1 us -> 40.1 us
  blocking collectives: 80.5 us -> 101 us
  loops' own time: 13.8 us -> 0 us
    dot_general x28 -> x0, matrix products: 192 us -> none  [the longest x4 50.5 us: backward_block(): jnp.einsum('qhe,khe->hqk', rows_grad, values_split, preferred_element_typ...]
    reduce_scatter x10, waiting for transfers between devices: 404 us -> 256 us  [reduce_matrix(): lax.psum_scatter(part.astype(bf), 'clip', scatter_dimension=0, tiled=True)]
    pallas_call x0 -> x2, Pallas kernels: none -> 92.1 us  [the longest x1 53.5 us: bwd(): pl.pallas_call(bwd_kernel, out_shape=(o1, o1, o1), in_specs=[pl.BlockSpec...]
    convert_element_type x32 -> x10, other arithmetic: 98.9 us -> 11.1 us  [reduce_matrix(): return lax.psum(part, 'seq').astype(f32)]
    dynamic_slice x32 -> x1, local copies, waits for them, and re-layouts: 29.7 us -> 0.01 us  [shards(): lax.dynamic_slice_in_dim(vectors, lax.axis_index('clip') * width_out, wid...]
    psum x1, blocking collectives: 9.77 us -> 37.9 us  [shards(): lax.psum(jnp.stack([grad_self_gain, grad_self_bias, grad_cross_gain, grad...]
    unnamed x1 -> x0, blocking collectives: 26 us -> none
    all_to_all x0 -> x1, blocking collectives: none -> 17.7 us  [shards(): lax.all_to_all(grad_attended, 'seq', split_axis=1, concat_axis=0, tiled=T...]
  transfers between devices with their start and end apart: 17 -> 16, of which waited for: 11 -> 11; matrix products, arithmetic and copies ran while one was open for 32% -> 13% of each run, Pallas kernels for 0% -> 6%
where the time goes in v1:
time: 837 us; the launch traced here: 829 us
  waiting for transfers between devices  360 us (43%)
  matrix products  174 us (21%)
  blocking collectives  101 us (12%)
  Pallas kernels  92.1 us (11%)
  local copies, waits for them, and re-layouts  40.1 us (5%)
  other arithmetic  25.6 us (3%)
  starting transfers between devices  19.5 us (2%)
  between operations  16.8 us (2%)
    reduce_scatter x10, waiting for transfers between devices, reduce_matrix(): lax.psum_scatter(part.astype(bf), 'clip', scatter_dimension=0, tiled=True)  256 us
    dot_general x10, matrix products, matmul(): return jnp.dot(left, right, preferred_element_type=jnp.float32)  61.5 us
    pallas_call x1, Pallas kernels, bwd(): pl.pallas_call(bwd_kernel, out_shape=(o1, o1, o1), in_specs=[pl.BlockSpec...  53.5 us
    dot_general x10, matrix products, left_times(): lax.dot_general(left, right, (((0,), (0,)), ((), ())), preferred_element_...  47.4 us
    psum x1, waiting for transfers between devices, reduce_matrix(): return lax.psum(part, 'seq').astype(f32)  40.8 us
    pallas_call x1, Pallas kernels, fwd(): pl.pallas_call(fwd_kernel, out_shape=(jax.ShapeDtypeStruct((T, W), bf), j...  38.5 us
    psum x1, blocking collectives, shards(): lax.psum(jnp.stack([grad_self_gain, grad_self_bias, grad_cross_gain, grad...  37.9 us
    dot_general x10, matrix products, right_times(): lax.dot_general(left, right, (((1,), (1,)), ((), ())), preferred_element_...  37 us
  transfers between devices with their start and end apart: 16, of which 11 were waited for; matrix products, arithmetic and copies ran while one was open for 13% of the time, Pallas kernels for 6%

profile of v1, /device:TPU:0, one launch (start us, length us, event | category | flops | bytes accessed | tf_op | source)
XLA Modules:
  0.0 829.4 jit_solution(14606023458721001648)
XLA Ops:
  11.4 2.9 convolution_convert_fusion.14
  15.3 5.2 all-to-all-start.1
  20.5 3.2 convolution_convert_fusion.13
  24.7 9.4 %all-to-all-done.1 = bf16[512,4,256]{2,0,1:T(8,128)(2,1)S(1)} async-done(((bf16[512,4,256]{2,0,1:T(8,128)(2,1)}), bf16[512,4,256]{2,0,1:T(8,128)(2,1)S(1)}, u32[]{:S(2)}, u32[]{:S(2)}) %all-to-all-start.1) | async-done | bytes 1048608 | tf_op jit(solution)/shard_map/all_to_all | solution.py:237
  34.1 4.2 all-to-all-start.2
  38.4 3.2 convolution_convert_fusion.15
  42.7 8.9 %all-to-all-done.2 = bf16[512,4,256]{2,0,1:T(8,128)(2,1)} async-done(((bf16[512,4,256]{2,0,1:T(8,128)(2,1)}), bf16[512,4,256]{2,0,1:T(8,128)(2,1)}, u32[]{:S(2)}, u32[]{:S(2)}) %all-to-all-start.2) | async-done | bytes 1048608 | tf_op jit(solution)/shard_map/all_to_all | solution.py:238
  51.5 4.3 all-to-all-start
  57.5 11.5 %all-to-all-done = bf16[512,4,256]{2,0,1:T(8,128)(2,1)} async-done(((bf16[512,4,256]{2,0,1:T(8,128)(2,1)}), bf16[512,4,256]{2,0,1:T(8,128)(2,1)}, u32[]{:S(2)}, u32[]{:S(2)}) %all-to-all-start) | async-done | bytes 1048608 | tf_op jit(solution)/shard_map/all_to_all | solution.py:236
  70.2 38.5 %shard_map.339 = (bf16[2048,256]{1,0:T(8,128)(2,1)S(1)}, f32[8,2048]{1,0:T(8,128)S(1)}) custom-call(bf16[2048,256]{1,0:T(8,128)(2,1)} %bitcast.2.q_ref, bf16[2048,256]{1,0:T(8,128)(2,1)S(1)} %bitcast.203, bf16[2048,256]{1,0:T(8,128)(2,1)} %bitcast.6.v_ref, s32[2048,1]{1,0:T(8,128)S(1)} %copy-done.2), custom_call_target="tpu_custom_call" | custom-call | tf_op jit(solution)/shard_map/pallas_call | solution.py:87
  111.9 4.3 all-to-all-start.3
  116.4 3.3 convolution_convert_fusion.16
  121.8 3.3 convolution_convert_fusion.17
  129.3 3.5 fusion.84
  138.8 7.6 fusion.85
  146.4 4.5 fusion.46
  153.5 26.9 %fusion.3 = (bf16[512,4096]{1,0:T(8,128)(2,1)}, f32[512,4096]{1,0:T(8,128)}) fusion(bf16[1024,4096]{1,0:T(8,128)(2,1)} %param.37, f32[512,1024]{1,0:T(8,128)S(1)} %get-tuple-element.64, f32[1024]{0:T(1024)S(1)} %copy-done.59, f32[1024]{0:T(1024)S(1)} %copy-done.49, f32[512]{0:T(512)S(1)} %add_rsqrt_fusion, f32[512]{0:T(512)S(1)} %broadcast_multiply_fusion.6), kind=kOutput, calls=%fused_computation.5 | convolution fusion | flops 4433903616 | bytes 23080960 | tf_op jit(solution)/shard_map/dot_general | solution.py:143
  180.4 11.7 %fusion.9 = bf16[512,4096]{1,0:T(8,128)(2,1)} fusion(f32[512,4096]{1,0:T(8,128)} %get-tuple-element.66, bf16[4096,1024]{1,0:T(8,128)(2,1)} %param.38, bf16[1,512,1024]{2,1,0:T(8,128)(2,1)S(1)} %copy-done.34), kind=kOutput, calls=%fused_computation.11 | convolution fusion | flops 4315938816 | bytes 22020096 | tf_op jit(solution)/shard_map/dot_general | solution.py:153
  192.1 7.0 multiply_reduce_fusion.1
  205.7 5.3 multiply_reduce_fusion
  211.0 5.6 fusion.51
  216.6 4.3 multiply_convert_fusion
  223.6 3.3 multiply_convert_fusion.1
  227.9 2.9 convolution_convert_fusion.3
  230.9 4.1 multiply_reduce_fusion.2
  237.1 3.8 convolution_convert_fusion.4
  241.0 4.5 convolution_convert_fusion.2
  245.6 30.7 %all-reduce.7.cloned.1.call-done = (bf16[256,1024]{0,1:T(8,128)(2,1)}, bf16[256,1024]{0,1:T(8,128)(2,1)}) async-done(((bf16[256,1024]{0,1:T(8,128)(2,1)}, bf16[256,1024]{0,1:T(8,128)(2,1)}), (bf16[256,1024]{0,1:T(8,128)(2,1)}, bf16[256,1024]{0,1:T(8,128)(2,1)})) %all-reduce.7.cloned.1.call-update) | async-done | bytes 1048592 | tf_op jit(solution)/shard_map/psum | solution.py:320
  276.3 3.1 convolution_convert_fusion.9
  279.5 3.1 convolution_convert_fusion.8
  282.7 3.5 convolution_convert_fusion.10
  286.4 17.7 %all_to_all.152 = bf16[512,4,256]{2,0,1:T(8,128)(2,1)} all-to-all(bf16[512,4,256]{2,0,1:T(8,128)(2,1)S(1)} %bitcast.214), channel_id=1, replica_groups=mesh['seq'=4,'clip'=8] {'seq'}, dimensions={1} | all-to-all | bytes 2097152 | tf_op jit(solution)/shard_map/all_to_all | solution.py:343
  304.1 53.5 %shard_map.340 = (bf16[2048,256]{1,0:T(8,128)(2,1)S(1)}, bf16[2048,256]{1,0:T(8,128)(2,1)S(1)}, bf16[2048,256]{1,0:T(8,128)(2,1)S(1)}) custom-call(bf16[2048,256]{1,0:T(8,128)(2,1)} %bitcast.2.q_ref, bf16[2048,256]{1,0:T(8,128)(2,1)S(1)} %bitcast.204, bf16[2048,256]{1,0:T(8,128)(2,1)} %bitcast.6.v_ref, bf16[2048,256]{1,0:T(8,128)(2,1)} %copy-done.1, ...), custom_call_target="tpu_custom_call" | custom-call | tf_op jit(solution)/shard_map/pallas_call | solution.py:136
  363.0 16.5 %all_to_all.153 = bf16[4,512,256]{1,2,0:T(8,128)(2,1)S(1)} all-to-all(bf16[4,512,256]{1,2,0:T(8,128)(2,1)} %copy.84), channel_id=1, replica_groups=mesh['seq'=4,'clip'=8] {'seq'}, dimensions={0} | all-to-all | bytes 2097152 | tf_op jit(solution)/shard_map/all_to_all | solution.py:349
  385.9 15.2 %all_to_all.154 = bf16[4,512,256]{1,2,0:T(8,128)(2,1)S(1)} all-to-all(bf16[4,512,256]{1,2,0:T(8,128)(2,1)} %copy.85), channel_id=1, replica_groups=mesh['seq'=4,'clip'=8] {'seq'}, dimensions={0} | all-to-all | bytes 2097152 | tf_op jit(solution)/shard_map/all_to_all | solution.py:350
  402.1 2.9 convolution_convert_fusion.6
  407.5 14.0 %all_to_all.155 = bf16[4,512,256]{1,2,0:T(8,128)(2,1)S(1)} all-to-all(bf16[4,512,256]{1,2,0:T(8,128)(2,1)} %copy.86), channel_id=1, replica_groups=mesh['seq'=4,'clip'=8] {'seq'}, dimensions={0} | all-to-all | bytes 2097152 | tf_op jit(solution)/shard_map/all_to_all | solution.py:351
  425.6 10.8 %convolution_convert_fusion.1 = bf16[1024,4096]{1,0:T(8,128)(2,1)} fusion(bf16[512,4096]{1,0:T(8,128)(2,1)} %fusion.9, f32[512,1024]{1,0:T(8,128)} %copy-done.20, f32[1024]{0:T(1024)S(1)} %copy-done.59, f32[1024]{0:T(1024)S(1)} %copy-done.49, f32[512]{0:T(512)S(1)} %add_rsqrt_fusion, f32[512]{0:T(512)S(1)} %broadcast_multiply_fusion.6), kind=kOutput, calls=%fused_computation.32 | convolution fusion | flops 4301783040 | bytes 14692352 | tf_op jit(solution)/shard_map/dot_general | solution.py:147
  436.6 10.4 %convolution_convert_fusion = bf16[4096,1024]{1,0:T(8,128)(2,1)} fusion(bf16[512,4096]{1,0:T(8,128)(2,1)} %get-tuple-element.65, bf16[1,512,1024]{2,1,0:T(8,128)(2,1)} %param.39), kind=kOutput, calls=%fused_computation.31 | convolution fusion | flops 4299161600 | bytes 13631488 | tf_op jit(solution)/shard_map/dot_general | solution.py:147
  450.2 36.3 %reduce-scatter.13.cloned.1.call-done = bf16[128,1024]{1,0:T(8,128)(2,1)} async-done(((bf16[1024,1024]{1,0:T(8,128)(2,1)}), bf16[128,1024]{1,0:T(8,128)(2,1)}) %reduce-scatter.13.cloned.1.call-update) | async-done | bytes 262160 | tf_op jit(solution)/shard_map/reduce_scatter | solution.py:366
  486.5 36.5 %reduce-scatter.15.cloned.1.call-done = bf16[128,1024]{1,0:T(8,128)(2,1)} async-done(((bf16[1024,1024]{1,0:T(8,128)(2,1)}), bf16[128,1024]{1,0:T(8,128)(2,1)}) %reduce-scatter.15.cloned.1.call-update) | async-done | bytes 262160 | tf_op jit(solution)/shard_map/reduce_scatter | solution.py:366
  523.0 90.4 %reduce-scatter.27.cloned.1.call-done = bf16[128,4096]{1,0:T(8,128)(2,1)} async-done(((bf16[1024,4096]{1,0:T(8,128)(2,1)}), bf16[128,4096]{1,0:T(8,128)(2,1)}) %reduce-scatter.27.cloned.1.call-update) | async-done | bytes 1048592 | tf_op jit(solution)/shard_map/reduce_scatter | solution.py:366
  613.4 90.2 %reduce-scatter.29.cloned.1.call-done = bf16[512,1024]{1,0:T(8,128)(2,1)} async-done(((bf16[4096,1024]{1,0:T(8,128)(2,1)}), bf16[512,1024]{1,0:T(8,128)(2,1)}) %reduce-scatter.29.cloned.1.call-update) | async-done | bytes 1048592 | tf_op jit(solution)/shard_map/reduce_scatter | solution.py:366
  703.7 11.5 %fusion.49 = bf16[1,512,1024]{2,1,0:T(8,128)(2,1)} fusion(f32[512,1024]{1,0:T(8,128)} %copy-done.20, bf16[512,4096]{1,0:T(8,128)(2,1)} %get-tuple-element.65, bf16[4096,1024]{1,0:T(8,128)(2,1)} %param.38), kind=kOutput, calls=%fused_computation.100 | convolution fusion | flops 4296015872 | bytes 15728640 | tf_op jit(solution)/shard_map/dot_general | solution.py:143
  723.4 3.3 fusion.36
  726.8 37.9 %psum.93 = f32[6,1024]{1,0:T(8,128)S(1)} all-reduce(f32[6,1024]{1,0:T(8,128)S(1)} %stack.27), channel_id=1, replica_groups=mesh['seq'=4,'clip'=8] {'clip','seq'}, use_global_device_ids=true, to_apply=%region_26.27 | all-reduce | flops 6144 | bytes 49152 | tf_op jit(solution)/shard_map/psum | solution.py:369
  765.3 4.3 fusion.35
  769.6 40.8 %all-reduce.5.cloned.1.call-done = (bf16[128,1024]{1,0:T(8,128)(2,1)}, bf16[128,1024]{1,0:T(8,128)(2,1)}, bf16[128,1024]{1,0:T(8,128)(2,1)}, bf16[128,1024]{1,0:...) async-done(((bf16[128,1024]{1,0:T(8,128)(2,1)}, ...) | async-done | bytes 4194320 | tf_op jit(solution)/shard_map/psum | solution.py:367
  (220 shorter events, 82.8 us)
Async XLA Ops:
  8.0 126.2 %copy-start = (bf16[1024,1024]{1,0:T(8,128)(2,1)S(1)}, bf16[1024,1024]{1,0:T(8,128)(2,1)}, u32[]{:S(2)}) copy-start(bf16[1024,1024]{1,0:T(8,128)(2,1)} %param.31) | copy-start | bytes 6291460
  8.0 3.3 copy-start.13
  8.0 3.3 copy-start.50
  8.1 3.3 copy-start.57
  9.7 28.7 %copy-start.44 = (f32[512]{0:T(512)}, f32[512]{0:T(512)S(1)}, u32[]{:S(2)}) copy-start(f32[512]{0:T(512)S(1)} %broadcast_multiply_fusion.8) | copy-start | bytes 6148
  11.4 27.0 %copy-start.46 = (f32[512]{0:T(512)}, f32[512]{0:T(512)S(1)}, u32[]{:S(2)}) copy-start(f32[512]{0:T(512)S(1)} %add_rsqrt_fusion.2) | copy-start | bytes 6148
  15.3 18.8 %all-to-all-start.1 = ((bf16[512,4,256]{2,0,1:T(8,128)(2,1)}), bf16[512,4,256]{2,0,1:T(8,128)(2,1)S(1)}, u32[]{:S(2)}, u32[]{:S(2)}) async-start(bf16[512,4,256]{2,0,1:T(8,128)(2,1)} %bitcast.213), calls=%async_computation.1 | async-start | bytes 2097152 | tf_op jit(solution)/shard_map/all_to_all | solution.py:237
  34.1 17.4 %all-to-all-start.2 = ((bf16[512,4,256]{2,0,1:T(8,128)(2,1)}), bf16[512,4,256]{2,0,1:T(8,128)(2,1)}, u32[]{:S(2)}, u32[]{:S(2)}) async-start(bf16[512,4,256]{2,0,1:T(8,128)(2,1)} %bitcast.212), calls=%async_computation.2 | async-start | bytes 2097152 | tf_op jit(solution)/shard_map/all_to_all | solution.py:238
  41.6 14.2 %copy-start.60 = (s32[1,4]{1,0:T(1,128)S(1)}, s32[1,4]{1,0:T(1,128)}, u32[]{:S(2)}) copy-start(s32[1,4]{1,0:T(1,128)} %param.22) | copy-start | bytes 52
  51.5 17.4 %all-to-all-start = ((bf16[512,4,256]{2,0,1:T(8,128)(2,1)}), bf16[512,4,256]{2,0,1:T(8,128)(2,1)}, u32[]{:S(2)}, u32[]{:S(2)}) async-start(bf16[512,4,256]{2,0,1:T(8,128)(2,1)} %bitcast.211), calls=%async_computation | async-start | bytes 2097152 | tf_op jit(solution)/shard_map/all_to_all | solution.py:236
  111.9 17.4 %all-to-all-start.3 = ((bf16[4,512,256]{1,2,0:T(8,128)(2,1)}), bf16[4,512,256]{1,2,0:T(8,128)(2,1)}, u32[]{:S(2)}, u32[]{:S(2)}) async-start(bf16[4,512,256]{1,2,0:T(8,128)(2,1)} %copy.76), calls=%async_computation.3 | async-start | bytes 2097152 | tf_op jit(solution)/shard_map/all_to_all | solution.py:246
  116.2 160.1 %all-reduce.7.cloned.1.call-start = ((), (), s32[]{:S(2)}) async-start(), calls=%async_computation.29 | async-start | bytes 2097152 | tf_op jit(solution)/shard_map/psum | solution.py:320
  146.4 4.6 copy-start.10
  146.4 4.8 copy-start.52
  151.2 40.9 %slice-start = ((s8[8388608]{0:T(1024)(128)(4,1)}), s8[4194304]{0:T(1024)(128)(4,1)S(1)}, s32[]{:S(2)}) async-start(s8[8388608]{0:T(1024)(128)(4,1)} %bitcast.244), calls=%async_computation.30 | async-start | bytes 8388608
  152.5 46.5 %copy-start.20 = (f32[512,1024]{1,0:T(8,128)}, f32[512,1024]{1,0:T(8,128)S(1)}, u32[]{:S(2)}) copy-start(f32[512,1024]{1,0:T(8,128)S(1)} %get-tuple-element.64) | copy-start | bytes 6291460
  153.5 26.9 %copy-start.34 = (bf16[1,512,1024]{2,1,0:T(8,128)(2,1)S(1)}, bf16[1,512,1024]{2,1,0:T(8,128)(2,1)}, u32[]{:S(2)}) copy-start(bf16[1,512,1024]{2,1,0:T(8,128)(2,1)} %param.39) | copy-start | bytes 3145732
  153.5 38.5 %slice-start.1 = ((s8[8388608]{0:T(1024)(128)(4,1)}), s8[4194304]{0:T(1024)(128)(4,1)S(1)}, s32[]{:S(2)}) async-start(s8[8388608]{0:T(1024)(128)(4,1)} %bitcast.244), calls=%async_computation.31 | async-start | bytes 8388608
  205.7 5.3 copy-start.33
  216.6 4.3 copy-start.21
  223.1 224.1 %reduce-scatter.19.cloned.1.call-start = ((), (), s32[]{:S(2)}) async-start(), calls=%async_computation.22 | async-start | bytes 2359296 | tf_op jit(solution)/shard_map/reduce_scatter | solution.py:366
  223.6 4.3 copy-start.11
  230.8 216.4 %reduce-scatter.17.cloned.1.call-start = ((), (), s32[]{:S(2)}) async-start(), calls=%async_computation.21 | async-start | bytes 2359296 | tf_op jit(solution)/shard_map/reduce_scatter | solution.py:366
  230.9 4.1 copy-start.12
  230.9 4.1 copy-start.19
  241.0 206.3 %reduce-scatter.25.cloned.1.call-start = ((), (), s32[]{:S(2)}) async-start(), calls=%async_computation.25 | async-start | bytes 2359296 | tf_op jit(solution)/shard_map/reduce_scatter | solution.py:366
  245.6 201.8 %reduce-scatter.21.cloned.1.call-start = ((), (), s32[]{:S(2)}) async-start(), calls=%async_computation.23 | async-start | bytes 2359296 | tf_op jit(solution)/shard_map/reduce_scatter | solution.py:366
  279.5 167.9 %reduce-scatter.23.cloned.1.call-start = ((), (), s32[]{:S(2)}) async-start(), calls=%async_computation.24 | async-start | bytes 2359296 | tf_op jit(solution)/shard_map/reduce_scatter | solution.py:366
  282.7 167.5 %reduce-scatter.11.cloned.1.call-start = ((), (), s32[]{:S(2)}) async-start(), calls=%async_computation.18 | async-start | bytes 2359296 | tf_op jit(solution)/shard_map/reduce_scatter | solution.py:366
  360.6 19.9 %copy-start.14 = (bf16[1,512,1024]{2,1,0:T(8,128)(2,1)S(1)}, bf16[1,512,1024]{2,1,0:T(8,128)(2,1)}, u32[]{:S(2)}) copy-start(bf16[1,512,1024]{2,1,0:T(8,128)(2,1)} %param.20) | copy-start | bytes 3145732
  360.6 19.9 %copy-start.45 = (f32[512]{0:T(512)S(1)}, f32[512]{0:T(512)}, u32[]{:S(2)}) copy-start(f32[512]{0:T(512)} %copy-done.44) | copy-start | bytes 6148
  360.6 19.9 %copy-start.47 = (f32[512]{0:T(512)S(1)}, f32[512]{0:T(512)}, u32[]{:S(2)}) copy-start(f32[512]{0:T(512)} %copy-done.46) | copy-start | bytes 6148
  360.6 19.9 %copy-start.51 = (f32[1024]{0:T(1024)S(1)}, f32[1024]{0:T(1024)}, u32[]{:S(2)}) copy-start(f32[1024]{0:T(1024)} %param.23) | copy-start | bytes 12292
  360.6 19.9 %copy-start.58 = (f32[1024]{0:T(1024)S(1)}, f32[1024]{0:T(1024)}, u32[]{:S(2)}) copy-start(f32[1024]{0:T(1024)} %param.24) | copy-start | bytes 12292
  383.3 103.1 %reduce-scatter.13.cloned.1.call-start = ((), (), s32[]{:S(2)}) async-start(), calls=%async_computation.19 | async-start | bytes 2359296 | tf_op jit(solution)/shard_map/reduce_scatter | solution.py:366
  385.9 16.2 %copy-start.15 = (bf16[1,512,1024]{2,1,0:T(8,128)(2,1)S(1)}, bf16[1,512,1024]{2,1,0:T(8,128)(2,1)}, u32[]{:S(2)}) copy-start(bf16[1,512,1024]{2,1,0:T(8,128)(2,1)} %param.20) | copy-start | bytes 3145732
  405.0 118.0 %reduce-scatter.15.cloned.1.call-start = ((), (), s32[]{:S(2)}) async-start(), calls=%async_computation.20 | async-start | bytes 2359296 | tf_op jit(solution)/shard_map/reduce_scatter | solution.py:366
  407.5 15.0 %copy-start.16 = (bf16[1,512,1024]{2,1,0:T(8,128)(2,1)S(1)}, bf16[1,512,1024]{2,1,0:T(8,128)(2,1)}, u32[]{:S(2)}) copy-start(bf16[1,512,1024]{2,1,0:T(8,128)(2,1)} %param.20) | copy-start | bytes 3145732
  425.4 188.0 %reduce-scatter.27.cloned.1.call-start = ((), (), s32[]{:S(2)}) async-start(), calls=%async_computation.26 | async-start | bytes 9437184 | tf_op jit(solution)/shard_map/reduce_scatter | solution.py:366
  436.5 267.1 %reduce-scatter.29.cloned.1.call-start = ((), (), s32[]{:S(2)}) async-start(), calls=%async_computation.27 | async-start | bytes 9437184 | tf_op jit(solution)/shard_map/reduce_scatter | solution.py:366
  446.9 363.4 %all-reduce.5.cloned.1.call-start = ((), (), s32[]{:S(2)}) async-start(), calls=%async_computation.28 | async-start | bytes 8388608 | tf_op jit(solution)/shard_map/psum | solution.py:367
  703.6 11.5 %copy-start.22 = (bf16[1024,1024]{1,0:T(8,128)(2,1)S(1)}, bf16[1024,1024]{1,0:T(8,128)(2,1)}, u32[]{:S(2)}) copy-start(bf16[1024,1024]{1,0:T(8,128)(2,1)} %param.32) | copy-start | bytes 6291460
  703.7 11.5 %copy-start.25 = (bf16[256,1024]{0,1:T(8,128)(2,1)S(1)}, bf16[256,1024]{0,1:T(8,128)(2,1)}, u32[]{:S(2)}) copy-start(bf16[256,1024]{0,1:T(8,128)(2,1)} %get-tuple-element.51) | copy-start | bytes 1572868
  813.2 4.1 copy-start.40
  814.8 3.4 copy-start.39
  814.8 4.2 copy-start.38
  815.6 4.2 copy-start.37
  816.5 4.2 copy-start.36
  (32 other events, 48.1 us)
Sparse Core Ops, SparseCore 0:
  223.2 53.0 all-reduce.6
  703.8 106.5 all-reduce.4
Sparse Core Ops, SparseCore 1:
  230.9 35.8 reduce-scatter.18
  269.0 34.2 reduce-scatter.16
  305.4 34.3 reduce-scatter.24
  342.1 34.2 reduce-scatter.20
  378.6 34.3 reduce-scatter.22
  415.9 34.2 reduce-scatter.10
  452.3 34.1 reduce-scatter.12
  488.6 34.3 reduce-scatter.14
  525.1 88.2 reduce-scatter.26
  615.7 87.8 reduce-scatter.28

commit v2 on v1

--- a/solution.py
+++ b/solution.py
@@ -1,3 +1,4 @@
+import functools
 import math
 
 import jax
@@ -89,54 +90,410 @@
       scratch_shapes=[pltpu.VMEM((H,B,T),f32)],
       compiler_params=pltpu.CompilerParams(vmem_limit_bytes=48<<20))(q,k,v,first)
 
-def bwd_kernel(q_ref,k_ref,v_ref,o_ref,g_ref,lse_ref,first_ref,dq_ref,dk_ref,dv_ref,dka,dva):
-    nb=T//B
-    dka[...]=jnp.zeros_like(dka); dva[...]=jnp.zeros_like(dva)
-    def qblock(i,masked):
-        r0=pl.multiple_of(i*B,B)
-        q=q_ref[pl.ds(r0,B),:]; g=g_ref[pl.ds(r0,B),:]
-        go=g.astype(f32)*o_ref[pl.ds(r0,B),:].astype(f32)
-        hm=(lax.broadcasted_iota(jnp.int32,(8,W),1)//HD==lax.broadcasted_iota(jnp.int32,(8,W),0)).astype(f32)
-        delta=lax.dot_general(hm,go,NT,precision=lax.Precision.HIGHEST,preferred_element_type=f32)
-        lse=lse_ref[:,pl.ds(r0,B)]
-        fst=first_ref[:,pl.ds(r0,B)]
-        zero=jnp.zeros_like(q)
-        qm=[jnp.where(lanemask(B,h),q,zero) for h in range(H)]
-        gm=[jnp.where(lanemask(B,h),g,zero) for h in range(H)]
-        kvi=lax.broadcasted_iota(jnp.int32,(B,B),0); qi=lax.broadcasted_iota(jnp.int32,(B,B),1)
-        def tile(j,dq,diag):
-            c0=pl.multiple_of(j*B,B)
-            k=k_ref[pl.ds(c0,B),:]; v=v_ref[pl.ds(c0,B),:]
-            dv=jnp.zeros((B,W),f32); dk=jnp.zeros((B,W),f32)
+def add_blocks(out, ins, rows, cols):
+    step = max(16, min(rows, 65536 // cols))
+
+    def body(i, carry):
+        r = pl.ds(pl.multiple_of(i * step, 16), step)
+        total = ins[0][r, :].astype(f32)
+        for one in ins[1:]:
+            total = total + one[r, :].astype(f32)
+        out[r, :] = total.astype(bf)
+        return carry
+
+    lax.fori_loop(0, rows // step, body, 0)
+
+
+class Job:
+    def __init__(self, order, part, own, bufs, sems, out, env):
+        self.order, self.part, self.own, self.out, self.env = order, part, own, out, env
+        self.r0, self.r1, self.r2 = bufs
+        self.sems = sems
+        self.pairs, self.rb, self.n = self.r0.shape
+        self.q = self.n if order == "own" else self.n // env["seqs"]
+
+    def sem(self, stage, k):
+        return dict(send_sem=self.sems.at[0, stage, k], recv_sem=self.sems.at[1, stage, k])
+
+    def copy(self, stage, k, src, dst, **where):
+        return pltpu.make_async_remote_copy(
+            src_ref=src, dst_ref=dst, device_id=where, device_id_type=pl.DeviceIdType.MESH, **self.sem(stage, k)
+        )
+
+    def cores(self):
+        e = self.env
+        return [
+            self.copy(0, 0, self.part.at[:, 1 - e["c"]], self.r0, clip=2 * e["z"] + 1 - e["c"])
+        ]
+
+    def own_copy(self, p):
+        return pltpu.make_async_copy(
+            self.part.at[p, self.env["c"]], self.own.at[p % 2], self.sems.at[0, 4, p % 2]
+        )
+
+    def columns(self, s):
+        return pl.ds(pl.multiple_of(s * self.q, 128), self.q)
+
+    def seq(self):
+        e, copies = self.env, []
+        for k in range(1, e["seqs"]):
+            to = lax.rem(e["s"] + k, e["seqs"])
+            if self.order == "xy":
+                src, dst = self.r0.at[:, :, self.columns(to)], self.r1.at[k - 1]
+            else:
+                src, dst = self.r1.at[0, :, self.columns(to)], self.r2.at[k - 1]
+            copies.append(self.copy(1, k - 1, src, dst, seq=to))
+        return copies
+
+    def across(self):
+        e, copies = self.env, []
+        for k in range(1, self.pairs):
+            to = lax.rem(e["z"] + k, self.pairs)
+            if self.order == "xy":
+                src, dst = self.r1.at[0, to], self.r2.at[k - 1]
+            elif self.order == "z":
+                src, dst = self.r0.at[to], self.r1.at[k - 1]
+            else:
+                src, dst = self.r0.at[to], self.r2.at[k - 1]
+            copies.append(self.copy(2, k - 1, src, dst, clip=2 * to + e["c"]))
+        return copies
+
+    def gather(self):
+        e, copies = self.env, []
+        for k in range(1, e["seqs"]):
+            to = lax.rem(e["s"] + k, e["seqs"])
+            copies.append(
+                self.copy(3, k - 1, self.r2.at[0], self.out.at[:, self.columns(e["s"])], seq=to)
+            )
+        return copies
+
+    def keep(self):
+        return pltpu.make_async_copy(
+            self.r2.at[0], self.out.at[:, self.columns(self.env["s"])], self.sems.at[1, 4, 0]
+        )
+
+    def sum_cores(self):
+        if self.own is None:
+            for p in range(self.pairs):
+                mine = self.part.at[p, self.env["c"]]
+                add_blocks(self.r0.at[p], [self.r0.at[p], mine], self.rb, self.n)
+            return
+        self.own_copy(0).start()
+        for p in range(self.pairs):
+            if p + 1 < self.pairs:
+                self.own_copy(p + 1).start()
+            self.own_copy(p).wait()
+            add_blocks(self.r0.at[p], [self.r0.at[p], self.own.at[p % 2]], self.rb, self.n)
+
+    def sum_seq(self):
+        e = self.env
+        others = range(e["seqs"] - 1)
+        if self.order == "xy":
+            for p in range(self.pairs):
+                mine = self.r0.at[p, :, self.columns(e["s"])]
+                add_blocks(self.r1.at[0, p], [mine] + [self.r1.at[k, p] for k in others], self.rb, self.q)
+        else:
+            mine = self.r1.at[0, :, self.columns(e["s"])]
+            add_blocks(self.r2.at[0], [mine] + [self.r2.at[k] for k in others], self.rb, self.q)
+
+    def sum_across(self):
+        e = self.env
+        others = range(self.pairs - 1)
+        if self.order == "xy":
+            add_blocks(self.r2.at[0], [self.r1.at[0, e["z"]]] + [self.r2.at[k] for k in others], self.rb, self.q)
+        elif self.order == "z":
+            add_blocks(self.r1.at[0], [self.r0.at[e["z"]]] + [self.r1.at[k] for k in others], self.rb, self.n)
+        else:
+            add_blocks(self.r2.at[0], [self.r0.at[e["z"]]] + [self.r2.at[k] for k in others], self.rb, self.q)
+
+
+def start(copies):
+    for one in copies:
+        one.start()
+
+
+def arrive(copies):
+    for one in copies:
+        one.wait_recv()
+
+
+def finish(copies):
+    for one in copies:
+        one.wait_send()
+
+
+def job_bufs(order, pairs, rb, n, seqs):
+    q = n if order == "own" else n // seqs
+    r0 = pltpu.VMEM((pairs, rb, n), bf)
+    if order == "xy":
+        return [r0, pltpu.VMEM((seqs - 1, pairs, rb, q), bf), pltpu.VMEM((pairs - 1, rb, q), bf)]
+    if order == "z":
+        return [r0, pltpu.VMEM((pairs - 1, rb, n), bf), pltpu.VMEM((seqs - 1, rb, q), bf)]
+    return [r0, pltpu.VMEM((8, 128), bf), pltpu.VMEM((pairs - 1, rb, q), bf)]
+
+LAST = pl.DeviceIdType.MESH
+
+
+def kc_kernel(seqs, pairs, *refs):
+    (q_ref, k_ref, v_ref, o_ref, g_ref, lse_ref, first_ref, n1_hbm, *parts) = refs[:15]
+    dq_f, dk_f, dv_f, *outs = refs[15:28]
+    dq_s, dk_s, dv_s, dka, dva, n1_buf, wacc, own_up, own_down, own_one, wparts, *rest = refs[28:]
+    sems, push_send, push_recv, local_sem = rest[-4:]
+    bufs = rest[:-4]
+    s = lax.axis_index("seq")
+    b = lax.axis_index("clip")
+    c, z = lax.rem(b, 2), lax.div(b, 2)
+    env = dict(seqs=seqs, s=s, c=c, z=z)
+    frames = T // seqs
+
+    barrier = pltpu.get_barrier_semaphore()
+    count = 1
+    pl.semaphore_signal(barrier, inc=1, device_id={"clip": 2 * z + 1 - c}, device_id_type=LAST)
+    for k in range(1, seqs):
+        pl.semaphore_signal(barrier, inc=1, device_id={"seq": lax.rem(s + k, seqs)}, device_id_type=LAST)
+        count += 1
+    for k in range(1, pairs):
+        pl.semaphore_signal(
+            barrier, inc=1, device_id={"clip": 2 * lax.rem(z + k, pairs) + c}, device_id_type=LAST
+        )
+        count += 1
+    pl.semaphore_wait(barrier, count)
+
+    orders = ("xy", "z", "xy", "xy", "xy", "own", "own", "own", "own", "own")
+    owns = (own_up, own_down) + (own_one,) * 3 + (None,) * 5
+    jobs = []
+    for t, order in enumerate(orders):
+        src = parts[t] if t < 7 else wparts.at[t - 7]
+        jobs.append(Job(order, src, owns[t], bufs[3 * t : 3 * t + 3], sems.at[t], outs[t], env))
+    up, down, go, gcq, gco, gxk, gxv, gq, gk, gv = jobs
+    early = [down, up, go, gcq, gco, gxk, gxv]
+    for one in early:
+        start(one.cores())
+    n1_copy = pltpu.make_async_copy(n1_hbm, n1_buf, local_sem.at[0])
+    n1_copy.start()
+
+    dka[...] = jnp.zeros_like(dka)
+    dva[...] = jnp.zeros_like(dva)
+
+    def qblock(i, masked):
+        r0 = pl.multiple_of(i * B, B)
+        q = q_ref[pl.ds(r0, B), :]
+        g = g_ref[pl.ds(r0, B), :]
+        go_ = g.astype(f32) * o_ref[pl.ds(r0, B), :].astype(f32)
+        hm = (
+            lax.broadcasted_iota(jnp.int32, (8, W), 1) // HD == lax.broadcasted_iota(jnp.int32, (8, W), 0)
+        ).astype(f32)
+        delta = lax.dot_general(hm, go_, NT, precision=lax.Precision.HIGHEST, preferred_element_type=f32)
+        lse = lse_ref[:, pl.ds(r0, B)]
+        fst = first_ref[:, pl.ds(r0, B)]
+        zero = jnp.zeros_like(q)
+        qm = [jnp.where(lanemask(B, h), q, zero) for h in range(H)]
+        gm = [jnp.where(lanemask(B, h), g, zero) for h in range(H)]
+        kvi = lax.broadcasted_iota(jnp.int32, (B, B), 0)
+        qi = lax.broadcasted_iota(jnp.int32, (B, B), 1)
+
+        def tile(j, dq, diag):
+            c0 = pl.multiple_of(j * B, B)
+            k = k_ref[pl.ds(c0, B), :]
+            v = v_ref[pl.ds(c0, B), :]
+            dv = jnp.zeros((B, W), f32)
+            dk = jnp.zeros((B, W), f32)
             for h in range(H):
-                st=dg(k,qm[h],NT)
-                p=jnp.exp2(st*C2-lse[h:h+1])
-                if diag: p=jnp.where(kvi<=qi,p,0.0)
-                if masked: p=jnp.where(kvi+c0>=fst,p,0.0)
-                dp=dg(v,gm[h],NT)
-                ds=(p*(dp-delta[h:h+1])).astype(bf)
-                dv=dv+dg(p.astype(bf),gm[h],NN)
-                dk=dk+dg(ds,qm[h],NN)
-                km=jnp.where(lanemask(B,h),k,zero)
-                dq=dq+dg(ds,km,TN)
-            dva[pl.ds(c0,B),:]+=dv
-            dka[pl.ds(c0,B),:]+=dk
+                st = dg(k, qm[h], NT)
+                p = jnp.exp2(st * C2 - lse[h : h + 1])
+                if diag:
+                    p = jnp.where(kvi <= qi, p, 0.0)
+                if masked:
+                    p = jnp.where(kvi + c0 >= fst, p, 0.0)
+                dp = dg(v, gm[h], NT)
+                ds = (p * (dp - delta[h : h + 1])).astype(bf)
+                dv = dv + dg(p.astype(bf), gm[h], NN)
+                dk = dk + dg(ds, qm[h], NN)
+                km = jnp.where(lanemask(B, h), k, zero)
+                dq = dq + dg(ds, km, TN)
+            dva[pl.ds(c0, B), :] += dv
+            dka[pl.ds(c0, B), :] += dk
             return dq
-        dq=jnp.zeros((B,W),f32)
-        dq=lax.fori_loop(0,i,lambda j,c:tile(j,c,False),dq)
-        dq=tile(i,dq,True)
-        dq_ref[pl.ds(r0,B),:]=(dq*0.125).astype(bf)
-    def body(i,c): qblock(i,False); return c
-    lax.fori_loop(0,6,body,0)
-    def body2(i,c): qblock(i,True); return c
-    lax.fori_loop(6,8,body2,0)
-    dk_ref[...]=(dka[...]*0.125).astype(bf); dv_ref[...]=dva[...].astype(bf)
-def bwd(q,k,v,o,g,lse,first):
-    o1=jax.ShapeDtypeStruct((T,W),bf)
-    return pl.pallas_call(bwd_kernel,out_shape=(o1,o1,o1),
-      in_specs=[pl.BlockSpec(memory_space=pltpu.VMEM)]*7,out_specs=(pl.BlockSpec(memory_space=pltpu.VMEM),)*3,
-      scratch_shapes=[pltpu.VMEM((T,W),f32)]*2,
-      compiler_params=pltpu.CompilerParams(vmem_limit_bytes=48<<20))(q,k,v,o,g,lse,first)
+
+        dq = jnp.zeros((B, W), f32)
+        dq = lax.fori_loop(0, i, lambda j, x: tile(j, x, False), dq)
+        dq = tile(i, dq, True)
+        dq_s[pl.ds(r0, B), :] = (dq * 0.125).astype(bf)
+        dk_s[pl.ds(r0, B), :] = (dka[pl.ds(r0, B), :] * 0.125).astype(bf)
+        dv_s[pl.ds(r0, B), :] = dva[pl.ds(r0, B), :].astype(bf)
+
+    lanes = pl.ds(pl.multiple_of(s * W, 128), W)
+
+    def pushes(owner):
+        k = lax.rem(owner - s + seqs, seqs)
+        rows = pl.ds(owner * frames, frames)
+        return [
+            pltpu.make_async_remote_copy(
+                src_ref=src.at[rows, :],
+                dst_ref=dst.at[:, lanes],
+                send_sem=push_send.at[n, owner],
+                recv_sem=push_recv.at[n, k],
+                device_id={"seq": owner},
+                device_id_type=LAST,
+            )
+            for n, (src, dst) in enumerate(((dq_s, dq_f), (dk_s, dk_f), (dv_s, dv_f)))
+        ]
+
+    def keeps(owner):
+        rows = pl.ds(owner * frames, frames)
+        return [
+            pltpu.make_async_copy(src.at[rows, :], dst.at[:, lanes], push_send.at[n, owner])
+            for n, (src, dst) in enumerate(((dq_s, dq_f), (dk_s, dk_f), (dv_s, dv_f)))
+        ]
+
+    per = frames // B
+    for owner in reversed(range(seqs)):
+        def block(n, x, owner=owner):
+            qblock(owner * per + per - 1 - n, (owner + 1) * frames > TAIL)
+            return x
+        lax.fori_loop(0, per, block, 0)
+
+        @pl.when(s != owner)
+        def _():
+            start(pushes(owner))
+
+        @pl.when(s == owner)
+        def _():
+            start(keeps(owner))
+
+        if owner == seqs - 1:
+            arrive(down.cores())
+            down.sum_cores()
+            start(down.across())
+            arrive(up.cores())
+            up.sum_cores()
+            start(up.seq())
+            for one in (go, gcq, gco):
+                arrive(one.cores())
+                one.sum_cores()
+                start(one.seq())
+            for one in (gxk, gxv):
+                arrive(one.cores())
+                one.sum_cores()
+                start(one.across())
+
+    n1_copy.wait()
+    for n, src in enumerate((dq_s, dk_s, dv_s)):
+        def product(r, x, src=src):
+            rows = pl.ds(pl.multiple_of(r * B, B), B)
+            add = dg(n1_buf[rows, :], src[rows, :], TN)
+            wacc[...] = jnp.where(r == 0, add, wacc[...] + add)
+            return x
+        lax.fori_loop(0, T // B, product, 0)
+        rb = gq.rb
+        for p in range(pairs):
+            for cc in range(2):
+                wparts[n, p, cc] = wacc[pl.ds((2 * p + cc) * rb, rb), :].astype(bf)
+        start((gq, gk, gv)[n].cores())
+
+    for one in (gxk, gxv):
+        arrive(one.across())
+        one.sum_across()
+        start(one.gather())
+        one.keep().start()
+    for one in (gq, gk, gv):
+        arrive(one.cores())
+        one.sum_cores()
+        start(one.across())
+    arrive(up.seq())
+    up.sum_seq()
+    start(up.across())
+    for one in (go, gcq, gco):
+        arrive(one.seq())
+        one.sum_seq()
+        start(one.across())
+    arrive(down.across())
+    down.sum_across()
+    start(down.seq())
+    for one in (gq, gk, gv, up, go, gcq, gco):
+        arrive(one.across())
+        one.sum_across()
+        start(one.gather())
+        one.keep().start()
+    arrive(down.seq())
+    down.sum_seq()
+    start(down.gather())
+    down.keep().start()
+
+    for owner in range(seqs):
+        @pl.when(s != owner)
+        def _():
+            finish(pushes(owner))
+
+        @pl.when(s == owner)
+        def _():
+            for one in keeps(owner):
+                one.wait()
+    for k in range(1, seqs):
+        for n, dst in enumerate((dq_f, dk_f, dv_f)):
+            pltpu.make_async_copy(
+                dst.at[:, pl.ds(pl.multiple_of(lax.rem(s - k + seqs, seqs) * W, 128), W)],
+                dst.at[:, pl.ds(pl.multiple_of(lax.rem(s - k + seqs, seqs) * W, 128), W)],
+                push_recv.at[n, k],
+            ).wait()
+    for one in jobs:
+        finish(one.cores())
+        if one.order != "own":
+            finish(one.seq())
+        finish(one.across())
+        finish(one.gather())
+        one.keep().wait()
+        arrive(one.gather())
+
+
+TAIL = 1536
+
+
+def kc(seqs, clips, q, k, v, o, g, lse, first, n1_all, parts):
+    pairs = clips // 2
+    split = []
+    for one in parts:
+        rows, cols = one.shape
+        split.append(one.reshape(pairs, 2, rows // clips, cols))
+    orders = ("xy", "z", "xy", "xy", "xy", "own", "own", "own", "own", "own")
+    shapes = [p.shape for p in split] + [(pairs, 2, D // clips, W)] * 3
+    bufs = []
+    for order, (_, _, rb, n) in zip(orders, shapes):
+        bufs += job_bufs(order, pairs, rb, n, seqs)
+    widths = [n if order != "own" else n * seqs for order, (_, _, _, n) in zip(orders, shapes)]
+    outs = [jax.ShapeDtypeStruct((T // seqs, D), bf)] * 3 + [
+        jax.ShapeDtypeStruct((shape[2], n), bf) for shape, n in zip(shapes, widths)
+    ]
+    hbm = pl.BlockSpec(memory_space=pl.ANY)
+    vmem = pl.BlockSpec(memory_space=pltpu.VMEM)
+    rb = D // clips
+    most = max(seqs, pairs)
+    return pl.pallas_call(
+        functools.partial(kc_kernel, seqs, pairs),
+        out_shape=outs,
+        in_specs=[vmem] * 7 + [hbm] + [hbm] * 5 + [vmem] * 2,
+        out_specs=[hbm] * 13,
+        scratch_shapes=[pltpu.VMEM((T, W), bf)] * 3
+        + [pltpu.VMEM((T, W), f32)] * 2
+        + [
+            pltpu.VMEM((T, D), bf),
+            pltpu.VMEM((D, W), f32),
+            pltpu.VMEM((2,) + shapes[0][2:], bf),
+            pltpu.VMEM((2,) + shapes[1][2:], bf),
+            pltpu.VMEM((2, rb, D), bf),
+            pltpu.VMEM((3, pairs, 2, rb, W), bf),
+        ]
+        + bufs
+        + [
+            pltpu.SemaphoreType.DMA((10, 2, 5, most)),
+            pltpu.SemaphoreType.DMA((3, seqs)),
+            pltpu.SemaphoreType.DMA((3, seqs)),
+            pltpu.SemaphoreType.DMA((1,)),
+        ],
+        compiler_params=pltpu.CompilerParams(
+            collective_id=1, has_side_effects=True, vmem_limit_bytes=60 * 2**20
+        ),
+    )(q, k, v, o, g, lse, first, n1_all, *split)
 
 
 def matmul(left, right):
@@ -229,6 +586,7 @@
     text_rows = text.shape[0]
     normed, unit_one, scale_one = norm_forward(frames, self_gain, self_bias)
     normed_low = normed.astype(jnp.bfloat16)
+    normed_all = lax.all_gather(normed_low, "seq", axis=0, tiled=True)
     query = matmul(normed_low, query_weight).astype(jnp.bfloat16)
     keys = matmul(normed_low, key_weight).astype(jnp.bfloat16)
     values = matmul(normed_low, value_weight).astype(jnp.bfloat16)
@@ -323,14 +681,9 @@
     key_low = key_total.astype(jnp.bfloat16)
     value_low = value_total.astype(jnp.bfloat16)
     text_grad = right_times(key_low, cross_key) + right_times(value_low, cross_value)
-    share = text_rows // count
-    text_share = lax.dynamic_slice_in_dim(text, place * share, share, 0)
-    grad_cross_key = left_times(
-        text_share, lax.dynamic_slice_in_dim(key_low, place * share, share, 0)
-    )
-    grad_cross_value = left_times(
-        text_share, lax.dynamic_slice_in_dim(value_low, place * share, share, 0)
-    )
+    share = D // count
+    grad_cross_key = left_times(text, lax.dynamic_slice_in_dim(key_low, place * share, share, 1))
+    grad_cross_value = left_times(text, lax.dynamic_slice_in_dim(value_low, place * share, share, 1))
     grad_cross_query = left_times(normed_two_low, grad_query_cross)
     grad_normed_two = right_times(grad_query_cross, cross_query)
     back_two, grad_cross_gain, grad_cross_bias = norm_backward(
@@ -342,17 +695,31 @@
     grad_attended = right_times(grad_self_low, output_weight).astype(jnp.bfloat16)
     grad_heads = lax.all_to_all(grad_attended, "seq", split_axis=1, concat_axis=0, tiled=True)
 
-    grad_query_heads, grad_key_heads, grad_value_heads = bwd(
-        query_heads, key_heads, value_heads, attended, grad_heads, log_totals, first_all[None]
-    )
-    grad_query, grad_key, grad_value = (
-        lax.all_to_all(grad_query_heads, "seq", split_axis=0, concat_axis=1, tiled=True),
-        lax.all_to_all(grad_key_heads, "seq", split_axis=0, concat_axis=1, tiled=True),
-        lax.all_to_all(grad_value_heads, "seq", split_axis=0, concat_axis=1, tiled=True),
-    )
-    grad_query_w = left_times(normed_low, grad_query)
-    grad_key_w = left_times(normed_low, grad_key)
-    grad_value_w = left_times(normed_low, grad_value)
+    grad_query, grad_key, grad_value, *mats = kc(
+        count,
+        lax.axis_size("clip"),
+        query_heads,
+        key_heads,
+        value_heads,
+        attended,
+        grad_heads,
+        log_totals,
+        first_all[None],
+        normed_all,
+        [
+            one.astype(bf)
+            for one in (
+                grad_up,
+                grad_down,
+                grad_output_w,
+                grad_cross_query,
+                grad_cross_out,
+                grad_cross_key,
+                grad_cross_value,
+            )
+        ],
+    )
+    w_up, w_down, w_o, w_cq, w_co, w_xk, w_xv, w_q, w_k, w_v = [one.astype(f32) for one in mats]
     grad_normed = (
         right_times(grad_query, query_weight)
         + right_times(grad_key, key_weight)
@@ -362,30 +729,26 @@
         grad_normed, unit_one, scale_one, self_gain
     )
     frames_grad = grad_self + back_one
-    def reduce_matrix(part):
-        part = lax.psum_scatter(part.astype(bf), "clip", scatter_dimension=0, tiled=True)
-        return lax.psum(part, "seq").astype(f32)
-
     vectors = lax.psum(jnp.stack([grad_self_gain, grad_self_bias, grad_cross_gain, grad_cross_bias, grad_feed_gain, grad_feed_bias]), ("clip", "seq"))
     width_out = vectors.shape[1] // lax.axis_size("clip")
     vectors = lax.dynamic_slice_in_dim(vectors, lax.axis_index("clip") * width_out, width_out, 1)
     summed = (
         vectors[0],
         vectors[1],
-        reduce_matrix(grad_query_w),
-        reduce_matrix(grad_key_w),
-        reduce_matrix(grad_value_w),
-        reduce_matrix(grad_output_w),
+        w_q,
+        w_k,
+        w_v,
+        w_o,
         vectors[2],
         vectors[3],
-        reduce_matrix(grad_cross_query),
-        reduce_matrix(grad_cross_key),
-        reduce_matrix(grad_cross_value),
-        reduce_matrix(grad_cross_out),
+        w_cq,
+        w_xk,
+        w_xv,
+        w_co,
         vectors[4],
         vectors[5],
-        reduce_matrix(grad_up),
-        reduce_matrix(grad_down),
+        w_up,
+        w_down,
     )
     return (
         output.astype(jnp.bfloat16)[None],

time: 837 us -> 628 us (0.75)
  waiting for transfers between devices: 360 us -> 87.9 us
  Pallas kernels: 92.1 us -> 248 us
  blocking collectives: 101 us -> 46.5 us
  matrix products: 174 us -> 151 us
  local copies, waits for them, and re-layouts: 40.1 us -> 28.5 us
    reduce_scatter x10 -> x0, waiting for transfers between devices: 256 us -> none  [reduce_matrix(): lax.psum_scatter(part.astype(bf), 'clip', scatter_dimension=0, tiled=True)]
    pallas_call x1, Pallas kernels: 53.5 us -> 210 us  [kc(): pl.pallas_call(functools.partial(kc_kernel, seqs, pairs), out_shape=outs,...]
    all_to_all x4 -> x0, blocking collectives: 63.4 us -> none  [the longest x1 17.7 us: shards(): lax.all_to_all(grad_attended, 'seq', split_axis=1, concat_axis=0, tiled=T...]
    all_gather x0 -> x1, waiting for transfers between devices: none -> 41.3 us  [shards(): normed_all = lax.all_gather(normed_low, 'seq', axis=0, tiled=True)]
    psum x1 -> x0, waiting for transfers between devices: 40.8 us -> none  [reduce_matrix(): return lax.psum(part, 'seq').astype(f32)]
    psum x1, waiting for transfers between devices: 30.7 us -> 12.3 us  [shards(): lax.psum(key_part.astype(jnp.bfloat16), 'seq').astype(jnp.float32)]
    dot_general x10 -> x7, matrix products: 47.4 us -> 31 us  [left_times(): lax.dot_general(left, right, (((0,), (0,)), ((), ())), preferred_element_...]
    unnamed x128 -> x140, local copies, waits for them, and re-layouts: 19 us -> 8.98 us
  transfers between devices with their start and end apart: 16 -> 7, of which waited for: 11 -> 6; matrix products, arithmetic and copies ran while one was open for 13% -> 12% of each run, Pallas kernels for 6% -> 0%
where the time goes in v2:
time: 628 us; the launch traced here: 620 us
  Pallas kernels  248 us (39%)
  matrix products  151 us (24%)
  waiting for transfers between devices  87.9 us (14%)
  blocking collectives  46.5 us (7%)
  local copies, waits for them, and re-layouts  28.5 us (5%)
  other arithmetic  21.9 us (3%)
  starting transfers between devices  21.9 us (3%)
  between operations  15 us (2%)
    pallas_call x1, Pallas kernels, kc(): pl.pallas_call(functools.partial(kc_kernel, seqs, pairs), out_shape=outs,...  210 us
    dot_general x10, matrix products, matmul(): return jnp.dot(left, right, preferred_element_type=jnp.float32)  54.8 us
    psum x1, blocking collectives, shards(): lax.psum(jnp.stack([grad_self_gain, grad_self_bias, grad_cross_gain, grad...  46.5 us
    all_gather x1, waiting for transfers between devices, shards(): normed_all = lax.all_gather(normed_low, 'seq', axis=0, tiled=True)  41.3 us
    pallas_call x1, Pallas kernels, fwd(): pl.pallas_call(fwd_kernel, out_shape=(jax.ShapeDtypeStruct((T, W), bf), j...  38.1 us
    dot_general x10, matrix products, right_times(): lax.dot_general(left, right, (((1,), (1,)), ((), ())), preferred_element_...  37 us
    dot_general x7, matrix products, left_times(): lax.dot_general(left, right, (((0,), (0,)), ((), ())), preferred_element_...  31 us
  transfers between devices with their start and end apart: 7, of which 6 were waited for; matrix products, arithmetic and copies ran while one was open for 12% of the time, Pallas kernels for 0%

profile of v2, /device:TPU:0, one launch (start us, length us, event | category | flops | bytes accessed | tf_op | source)
XLA Modules:
  0.0 620.3 jit_solution(15751153711685781150)
XLA Ops:
  11.6 3.2 convolution_convert_fusion.10
  15.8 5.2 all-to-all-start
  21.0 3.2 convolution_convert_fusion.9
  25.2 9.4 %all-to-all-done = bf16[512,4,256]{2,0,1:T(8,128)(2,1)S(1)} async-done(((bf16[512,4,256]{2,0,1:T(8,128)(2,1)}), bf16[512,4,256]{2,0,1:T(8,128)(2,1)S(1)}, u32[]{:S(2)}, u32[]{:S(2)}) %all-to-all-start) | async-done | bytes 1048608 | tf_op jit(solution)/shard_map/all_to_all | solution.py:594
  34.6 4.2 all-to-all-start.1
  38.9 3.2 convolution_convert_fusion.8
  43.1 8.9 %all-to-all-done.1 = bf16[512,4,256]{2,0,1:T(8,128)(2,1)} async-done(((bf16[512,4,256]{2,0,1:T(8,128)(2,1)}), bf16[512,4,256]{2,0,1:T(8,128)(2,1)}, u32[]{:S(2)}, u32[]{:S(2)}) %all-to-all-start.1) | async-done | bytes 1048608 | tf_op jit(solution)/shard_map/all_to_all | solution.py:595
  52.0 4.3 all-to-all-start.2
  58.0 11.4 %all-to-all-done.2 = bf16[512,4,256]{2,0,1:T(8,128)(2,1)} async-done(((bf16[512,4,256]{2,0,1:T(8,128)(2,1)}), bf16[512,4,256]{2,0,1:T(8,128)(2,1)}, u32[]{:S(2)}, u32[]{:S(2)}) %all-to-all-start.2) | async-done | bytes 1048608 | tf_op jit(solution)/shard_map/all_to_all | solution.py:596
  70.7 38.1 %shard_map.339 = (bf16[2048,256]{1,0:T(8,128)(2,1)S(1)}, f32[8,2048]{1,0:T(8,128)S(1)}) custom-call(bf16[2048,256]{1,0:T(8,128)(2,1)S(1)} %bitcast.193, bf16[2048,256]{1,0:T(8,128)(2,1)} %bitcast.4.k_ref.refs_1_, bf16[2048,256]{1,0:T(8,128)(2,1)} %bitcast.6.v_ref.refs_2_, s32[2048,1]{1,0:T(8,128)S(1)} %copy-done.3), custom_call_target="tpu_custom_call" | custom-call | tf_op jit(solution)/shard_map/pallas_call | solution.py:88
  110.4 2.3 copy.77
  112.7 4.2 all-to-all-start.3
  117.2 2.3 convolution_convert_fusion.13
  120.6 3.3 convolution_convert_fusion.14
  126.1 4.0 all-to-all-done.3
  130.1 3.3 fusion.73
  134.7 2.3 convolution_convert_fusion.7
  138.5 7.4 %fusion.74 = (f32[16,512]{1,0:T(8,128)S(1)}, f32[16,512,256]{1,2,0:T(8,128)}) fusion(pred[512,256]{0,1:T(8,128)(4,1)S(1)} %broadcast_compare_fusion, bf16[512,16,64]{0,2,1:T(8,128)(2,1)S(1)} %bitcast.205, bf16[256,16,64]{0,2,1:T(8,128)(2,1)} %bitcast.212), kind=kOutput, calls=%fused_computation.157 | convolution fusion | flops 276824320 | bytes 10125312 | tf_op jit(solution)/shard_map/sub | solution.py:541
  145.9 4.5 fusion.42
  153.0 27.1 %fusion.3 = (bf16[512,4096]{1,0:T(8,128)(2,1)}, f32[512,4096]{1,0:T(8,128)}) fusion(bf16[1024,4096]{1,0:T(8,128)(2,1)} %param.37, f32[512,1024]{1,0:T(8,128)S(1)} %get-tuple-element.74, f32[1024]{0:T(1024)S(1)} %copy-done.59, f32[1024]{0:T(1024)S(1)} %copy-done.52, f32[512]{0:T(512)S(1)} %add_rsqrt_fusion, f32[512]{0:T(512)S(1)} %broadcast_multiply_fusion.6), kind=kOutput, calls=%fused_computation.5 | convolution fusion | flops 4433903616 | bytes 23080960 | tf_op jit(solution)/shard_map/dot_general | solution.py:500
  180.2 12.0 %fusion.9 = bf16[512,4096]{1,0:T(8,128)(2,1)} fusion(f32[512,4096]{1,0:T(8,128)} %get-tuple-element.76, bf16[4096,1024]{1,0:T(8,128)(2,1)} %param.38, bf16[1,512,1024]{2,1,0:T(8,128)(2,1)S(1)} %copy-done.29), kind=kOutput, calls=%fused_computation.11 | convolution fusion | flops 4315938816 | bytes 22020096 | tf_op jit(solution)/shard_map/dot_general | solution.py:510
  192.1 7.0 %multiply_reduce_fusion.1 = (f32[1024]{0:T(1024)S(1)}, f32[512]{0:T(512)S(1)}, f32[512]{0:T(512)S(1)}, f32[1024]{0:T(1024)S(1)}, f32[512,1024]{1,0:T(8,128)S(1)}) fusion(f32[512,1024]{1,0:T(8,128)S(1)} %get-tuple-element.74, f32[512]{0:T(512)S(1)} %add_rsqrt_fusion, f32[512]{0:T(512)S(1)} %broadcast_multiply_fusion.6, f32[1024]{0:T(1024)S(1)} %copy-done.52, ...), kind=kOutput, calls=%fused_computation.57 | convolution fusion | flops 4299682816 | bytes 16797696 | tf_op jit(solution)/shard_map/dot_general | solution.py:510
  201.3 2.3 convolution_convert_fusion.6
  203.6 2.3 copy.82
  205.8 6.0 fusion.47
  211.9 4.5 multiply_reduce_fusion
  216.5 2.5 multiply_convert_fusion
  219.0 2.2 fusion.50
  222.3 3.2 multiply_convert_fusion.1
  231.7 3.5 all-to-all-start.4
  235.3 4.7 convolution_convert_fusion.4
  240.0 2.6 convolution_convert_fusion.2
  242.6 2.9 convolution_convert_fusion.3
  245.4 9.5 %convolution_convert_fusion.1 = bf16[1024,4096]{1,0:T(8,128)(2,1)} fusion(bf16[512,4096]{1,0:T(8,128)(2,1)} %fusion.9, f32[512,1024]{1,0:T(8,128)S(1)} %copy-done.19, f32[1024]{0:T(1024)S(1)} %copy-done.59, f32[1024]{0:T(1024)S(1)} %copy-done.52, f32[512]{0:T(512)S(1)} %add_rsqrt_fusion, f32[512]{0:T(512)S(1)} %broadcast_multiply_fusion.6), kind=kOutput, calls=%fused_computation.32 | convolution fusion | flops 4301783040 | bytes 14692352 | tf_op jit(solution)/shard_map/dot_general | solution.py:504
  254.9 7.0 %convolution_convert_fusion = bf16[4096,1024]{1,0:T(8,128)(2,1)} fusion(bf16[512,4096]{1,0:T(8,128)(2,1)S(1)} %copy-done.63, bf16[1,512,1024]{2,1,0:T(8,128)(2,1)S(1)} %copy-done.30), kind=kOutput, calls=%fused_computation.31 | convolution fusion | flops 4299161600 | bytes 13631488 | tf_op jit(solution)/shard_map/dot_general | solution.py:504
  261.9 5.5 fusion.45
  267.4 12.3 %all-reduce.3.cloned.1.call-done = (bf16[256,1024]{0,1:T(8,128)(2,1)}, bf16[256,1024]{0,1:T(8,128)(2,1)}) async-done(((bf16[256,1024]{0,1:T(8,128)(2,1)}, bf16[256,1024]{0,1:T(8,128)(2,1)}), (bf16[256,1024]{0,1:T(8,128)(2,1)}, bf16[256,1024]{0,1:T(8,128)(2,1)})) %all-reduce.3.cloned.1.call-update) | async-done | bytes 1048592 | tf_op jit(solution)/shard_map/psum | solution.py:678
  279.7 2.2 fusion.52
  281.9 2.0 copy.88
  284.0 2.2 fusion.51
  286.2 2.0 copy.86
  288.2 3.0 fusion.78
  293.0 41.3 %all-gather.2.cloned.1.call-done.refs_7_ = bf16[2048,1024]{1,0:T(8,128)(2,1)} async-done(((bf16[512,1024]{1,0:T(8,128)(2,1)}), bf16[2048,1024]{1,0:T(8,128)(2,1)}) %all-gather.2.cloned.1.call-update) | async-done | bytes 4194320 | tf_op jit(solution)/shard_map/all_gather | solution.py:589
  334.3 209.8 %shard_map.340 = (bf16[512,1024]{1,0:T(8,128)(2,1)}, bf16[512,1024]{1,0:T(8,128)(2,1)}, bf16[512,1024]{1,0:T(8,128)(2,1)}, bf16[128,4096]{1,0:T(8,128)(2,1)}, bf...) custom-call(bf16[2048,256]{1,0:T(8,128)(2,1)} %bitcast.194, ...), custom_call_target="tpu_custom_call" | custom-call | tf_op jit(solution)/shard_map/pallas_call | solution.py:471
  544.2 3.3 fusion.76
  549.8 3.2 fusion.36
  553.0 46.5 %psum.23 = f32[6,1024]{1,0:T(8,128)S(1)} all-reduce(f32[6,1024]{1,0:T(8,128)S(1)} %stack.27), channel_id=1, replica_groups=mesh['seq'=4,'clip'=8] {'clip','seq'}, use_global_device_ids=true, to_apply=%region_26.27 | all-reduce | flops 6144 | bytes 49152 | tf_op jit(solution)/shard_map/psum | solution.py:732
  600.1 2.8 convert_element_type.216
  (199 shorter events, 45.0 us)
Async XLA Ops:
  7.2 127.5 %copy-start = (bf16[1024,1024]{1,0:T(8,128)(2,1)S(1)}, bf16[1024,1024]{1,0:T(8,128)(2,1)}, u32[]{:S(2)}) copy-start(bf16[1024,1024]{1,0:T(8,128)(2,1)} %param.31) | copy-start | bytes 6291460
  7.2 3.9 copy-start.6
  7.2 3.9 copy-start.48
  7.2 3.9 copy-start.50
  11.5 3.2 copy-start.21
  15.8 18.8 %all-to-all-start = ((bf16[512,4,256]{2,0,1:T(8,128)(2,1)}), bf16[512,4,256]{2,0,1:T(8,128)(2,1)S(1)}, u32[]{:S(2)}, u32[]{:S(2)}) async-start(bf16[512,4,256]{2,0,1:T(8,128)(2,1)} %bitcast.204), calls=%async_computation | async-start | bytes 2097152 | tf_op jit(solution)/shard_map/all_to_all | solution.py:594
  34.6 34.8 %copy-start.1 = (bf16[512,4,256]{2,0,1:T(8,128)(2,1)}, bf16[512,4,256]{2,0,1:T(8,128)(2,1)S(1)}, u32[]{:S(2)}) copy-start(bf16[512,4,256]{2,0,1:T(8,128)(2,1)S(1)} %all-to-all-done) | copy-start | bytes 3145732
  34.6 17.4 %all-to-all-start.1 = ((bf16[512,4,256]{2,0,1:T(8,128)(2,1)}), bf16[512,4,256]{2,0,1:T(8,128)(2,1)}, u32[]{:S(2)}, u32[]{:S(2)}) async-start(bf16[512,4,256]{2,0,1:T(8,128)(2,1)} %bitcast.203), calls=%async_computation.1 | async-start | bytes 2097152 | tf_op jit(solution)/shard_map/all_to_all | solution.py:595
  42.1 14.3 %copy-start.60 = (s32[1,4]{1,0:T(1,128)S(1)}, s32[1,4]{1,0:T(1,128)}, u32[]{:S(2)}) copy-start(s32[1,4]{1,0:T(1,128)} %param.22) | copy-start | bytes 52
  52.0 17.4 %all-to-all-start.2 = ((bf16[512,4,256]{2,0,1:T(8,128)(2,1)}), bf16[512,4,256]{2,0,1:T(8,128)(2,1)}, u32[]{:S(2)}, u32[]{:S(2)}) async-start(bf16[512,4,256]{2,0,1:T(8,128)(2,1)} %bitcast.202), calls=%async_computation.2 | async-start | bytes 2097152 | tf_op jit(solution)/shard_map/all_to_all | solution.py:596
  56.6 52.1 %copy-start.43 = (s32[2048]{0:T(1024)}, s32[2048]{0:T(1024)S(1)}, u32[]{:S(2)}) copy-start(s32[2048]{0:T(1024)S(1)} %select_reduce_fusion) | copy-start | bytes 24580
  110.4 6.8 %copy-start.24 = (bf16[1,256,1024]{2,1,0:T(8,128)(2,1)S(1)}, bf16[1,256,1024]{2,1,0:T(8,128)(2,1)}, u32[]{:S(2)}) copy-start(bf16[1,256,1024]{2,1,0:T(8,128)(2,1)} %param.21) | copy-start | bytes 1572868
  112.7 17.4 %all-to-all-start.3 = ((bf16[4,512,256]{1,2,0:T(8,128)(2,1)}), bf16[4,512,256]{1,2,0:T(8,128)(2,1)}, u32[]{:S(2)}, u32[]{:S(2)}) async-start(bf16[4,512,256]{1,2,0:T(8,128)(2,1)} %copy.77), calls=%async_computation.3 | async-start | bytes 2097152 | tf_op jit(solution)/shard_map/all_to_all | solution.py:604
  117.0 162.7 %all-reduce.3.cloned.1.call-start = ((), (), s32[]{:S(2)}) async-start(), calls=%async_computation.6 | async-start | bytes 2097152 | tf_op jit(solution)/shard_map/psum | solution.py:678
  120.6 9.5 %copy-start.7 = (bf16[1,512,1024]{2,1,0:T(8,128)(2,1)S(1)}, bf16[1,512,1024]{2,1,0:T(8,128)(2,1)}, u32[]{:S(2)}) copy-start(bf16[1,512,1024]{2,1,0:T(8,128)(2,1)} %param.20) | copy-start | bytes 3145732
  145.9 4.6 copy-start.10
  145.9 4.8 copy-start.53
  150.7 41.4 %slice-start.2 = ((s8[8388608]{0:T(1024)(128)(4,1)}), s8[4194304]{0:T(1024)(128)(4,1)S(1)}, s32[]{:S(2)}) async-start(s8[8388608]{0:T(1024)(128)(4,1)} %bitcast.234), calls=%async_computation.9 | async-start | bytes 8388608
  152.1 47.1 %copy-start.18 = (f32[512,1024]{1,0:T(8,128)}, f32[512,1024]{1,0:T(8,128)S(1)}, u32[]{:S(2)}) copy-start(f32[512,1024]{1,0:T(8,128)S(1)} %get-tuple-element.74) | copy-start | bytes 6291460
  153.0 27.1 %copy-start.29 = (bf16[1,512,1024]{2,1,0:T(8,128)(2,1)S(1)}, bf16[1,512,1024]{2,1,0:T(8,128)(2,1)}, u32[]{:S(2)}) copy-start(bf16[1,512,1024]{2,1,0:T(8,128)(2,1)} %param.39) | copy-start | bytes 3145732
  153.0 39.1 %slice-start.3 = ((s8[8388608]{0:T(1024)(128)(4,1)}), s8[4194304]{0:T(1024)(128)(4,1)S(1)}, s32[]{:S(2)}) async-start(s8[8388608]{0:T(1024)(128)(4,1)} %bitcast.234), calls=%async_computation.10 | async-start | bytes 8388608
  205.8 6.0 copy-start.28
  205.8 6.1 copy-start.34
  205.8 10.6 %slice-start = ((s8[8388608]{0:T(1024)(128)(4,1)}), s8[4194304]{0:T(1024)(128)(4,1)S(1)}, s32[]{:S(2)}) async-start(s8[8388608]{0:T(1024)(128)(4,1)} %bitcast.198), calls=%async_computation.7 | async-start | bytes 8388608
  211.9 4.6 slice-start.1
  221.3 113.0 %all-gather.2.cloned.1.call-start = ((), (), s32[]{:S(2)}) async-start(), calls=%async_computation.5 | async-start | bytes 5242880 | tf_op jit(solution)/shard_map/all_gather | solution.py:589
  222.3 3.2 copy-start.11
  231.7 61.2 %all-to-all-start.4 = ((bf16[512,4,256]{2,0,1:T(8,128)(2,1)}), bf16[512,4,256]{2,0,1:T(8,128)(2,1)S(1)}, u32[]{:S(2)}, u32[]{:S(2)}) async-start(bf16[512,4,256]{2,0,1:T(8,128)(2,1)} %bitcast.201), calls=%async_computation.4 | async-start | bytes 2097152 | tf_op jit(solution)/shard_map/all_to_all | solution.py:696
  235.3 4.7 copy-start.17
  235.3 4.7 copy-start.62
  242.6 19.3 %slice-start.4 = ((s8[8388608]{0:T(1024)(128)(4,1)}), s8[4194304]{0:T(1024)(128)(4,1)S(1)}, s32[]{:S(2)}) async-start(s8[8388608]{0:T(1024)(128)(4,1)} %bitcast.236), calls=%async_computation.11 | async-start | bytes 8388608
  245.4 9.5 %copy-start.30 = (bf16[1,512,1024]{2,1,0:T(8,128)(2,1)S(1)}, bf16[1,512,1024]{2,1,0:T(8,128)(2,1)}, u32[]{:S(2)}) copy-start(bf16[1,512,1024]{2,1,0:T(8,128)(2,1)} %param.39) | copy-start | bytes 3145732
  245.4 9.5 %copy-start.63 = (bf16[512,4096]{1,0:T(8,128)(2,1)S(1)}, bf16[512,4096]{1,0:T(8,128)(2,1)}, u32[]{:S(2)}) copy-start(bf16[512,4096]{1,0:T(8,128)(2,1)} %get-tuple-element.75) | copy-start | bytes 12582916
  245.4 16.5 %slice-start.5 = ((s8[8388608]{0:T(1024)(128)(4,1)}), s8[4194304]{0:T(1024)(128)(4,1)S(1)}, s32[]{:S(2)}) async-start(s8[8388608]{0:T(1024)(128)(4,1)} %bitcast.236), calls=%async_computation.12 | async-start | bytes 8388608
  288.2 3.0 copy-start.23
  288.2 3.0 copy-start.33
  292.9 41.3 %copy-start.20 = (bf16[512,4,256]{2,0,1:T(8,128)(2,1)}, bf16[512,4,256]{2,0,1:T(8,128)(2,1)S(1)}, u32[]{:S(2)}) copy-start(bf16[512,4,256]{2,0,1:T(8,128)(2,1)S(1)} %all-to-all-done.4) | copy-start | bytes 3145732
  544.1 3.4 copy-start.54
  544.1 3.4 copy-start.57
  599.5 3.3 copy-start.27
  602.9 3.3 copy-start.40
  602.9 4.1 copy-start.39
  604.4 3.4 copy-start.38
  604.4 4.2 copy-start.37
  605.3 4.2 copy-start.36
  606.1 4.2 copy-start.35
  606.1 5.1 copy-start.25
  607.0 4.2 copy-start.14
  (29 other events, 45.8 us)
Sparse Core Ops, SparseCore 0:
  221.4 58.2 all-reduce.2
  281.6 52.6 all-gather.1

commit v3 on v2

v3 whole, which is shorter than its diff:
```python
import functools
import math

import jax
import jax.numpy as jnp
from jax import lax
from jax.experimental import pallas as pl
from jax.experimental.pallas import tpu as pltpu
from jax.sharding import PartitionSpec as P

D = 1024
HEADS = 16
HD = 64
TEXT = 64
CLIPS = 4


EPS = 1e-05
NEG = -1e30
SQRT_HALF = 0.7071067811865476
INV_ROOT_TWO_PI = 0.3989422804014327

bf = jnp.bfloat16
f32 = jnp.float32
T, W, H, B = 2048, 256, 4, 256
LOG2E = math.log2(math.e)
C2 = LOG2E / 8.0
NT = (((1,), (1,)), ((), ()))
NN = (((1,), (0,)), ((), ()))
TN = (((0,), (0,)), ((), ()))


def dg(a, b, d):
    return lax.dot_general(a, b, d, preferred_element_type=f32)


def lanemask(rows,h):
    l=lax.broadcasted_iota(jnp.int32,(rows,W),1)
    return (l//HD)==h
def fwd_kernel(q_ref,k_ref,v_ref,first_ref,o_ref,lse_ref,s_ref):
    nb=T//B
    def qblock(i,masked):
        r0=pl.multiple_of(i*B,B)
        q=q_ref[pl.ds(r0,B),:]
        row=lax.broadcasted_iota(jnp.int32,(B,B),0); col=lax.broadcasted_iota(jnp.int32,(B,B),1)
        qm=[jnp.where(lanemask(B,h),q,jnp.zeros_like(q)) for h in range(H)]
        fst=first_ref[pl.ds(r0,B),:]
        def scores(j,carry,diag):
            c0=pl.multiple_of(j*B,B)
            k=k_ref[pl.ds(c0,B),:]
            out=[]
            for h in range(H):
                s=dg(qm[h],k,NT)
                if diag: s=jnp.where(col<=row,s,NEG)
                if masked: s=jnp.where(col+c0>=fst,s,NEG)
                s_ref[h,:,pl.ds(c0,B)]=s
                m=jnp.maximum(s[:,:128],s[:,128:])
                out.append(jnp.maximum(carry[h],m))
            return tuple(out)
        m=tuple(jnp.full((B,128),NEG,f32) for _ in range(H))
        m=lax.fori_loop(0,i,lambda j,c:scores(j,c,False),m)
        m=scores(i,m,True)
        m=[jnp.max(x,axis=1,keepdims=True) for x in m]
        def mix(j,carry):
            acc,ls=carry
            c0=pl.multiple_of(j*B,B)
            v=v_ref[pl.ds(c0,B),:]
            acc=list(acc); ls=list(ls)
            for h in range(H):
                p=jnp.exp2((s_ref[h,:,pl.ds(c0,B)]-m[h])*C2)
                ls[h]=ls[h]+p[:,:128]+p[:,128:]
                acc[h]=acc[h]+dg(p.astype(bf),v,NN)
            return tuple(acc),tuple(ls)
        acc,ls=lax.fori_loop(0,i+1,mix,(tuple(jnp.zeros((B,W),f32) for _ in range(H)),tuple(jnp.zeros((B,128),f32) for _ in range(H))))
        o=jnp.zeros((B,W),f32)
        lane=lax.broadcasted_iota(jnp.int32,(B,128),1)
        lse=jnp.zeros((B,128),f32)
        for h in range(H):
            l=jnp.sum(ls[h],axis=1,keepdims=True)
            o=jnp.where(lanemask(B,h),acc[h]/l,o)
            lse=jnp.where(lane==h,m[h]*C2+jnp.log2(l),lse)
        o_ref[pl.ds(r0,B),:]=o.astype(bf)
        lse_ref[:,pl.ds(r0,B)]=lse.T[:8]
    def body(i,c): qblock(i,False); return c
    lax.fori_loop(0,6,body,0)
    def body2(i,c): qblock(i,True); return c
    lax.fori_loop(6,8,body2,0)
def fwd(q,k,v,first):
    return pl.pallas_call(fwd_kernel,out_shape=(jax.ShapeDtypeStruct((T,W),bf),jax.ShapeDtypeStruct((8,T),f32)),
      in_specs=[pl.BlockSpec(memory_space=pltpu.VMEM)]*4,out_specs=(pl.BlockSpec(memory_space=pltpu.VMEM),)*2,
      scratch_shapes=[pltpu.VMEM((H,B,T),f32)],
      compiler_params=pltpu.CompilerParams(vmem_limit_bytes=48<<20))(q,k,v,first)

def add_blocks(out, ins, rows, cols):
    step = max(16, min(rows, 65536 // cols))

    def body(i, carry):
        r = pl.ds(pl.multiple_of(i * step, 16), step)
        total = ins[0][r, :].astype(f32)
        for one in ins[1:]:
            total = total + one[r, :].astype(f32)
        out[r, :] = total.astype(bf)
        return carry

    lax.fori_loop(0, rows // step, body, 0)


def each(count, fn):
    def body(i, x):
        fn(i)
        return x

    lax.fori_loop(0, count, body, 0)


def tile_of(i, size=256):
    return pl.ds(pl.multiple_of(i * size, size), size)


def unit_rows(v):
    center = v - jnp.mean(v, axis=-1, keepdims=True)
    scaled = lax.rsqrt(jnp.mean(center * center, axis=-1, keepdims=True) + EPS)
    return center * scaled, scaled


def norm_rows(src, gain, bias, dst, rows):
    def chunk(i):
        r = tile_of(i, 64)
        unit, _ = unit_rows(src[r, :])
        dst[r, :] = (unit * gain[...] + bias[...]).astype(bf)

    each(rows // 64, chunk)


def norm_back_rows(up, src, gain, add, dst, dst_low, rows):
    def chunk(i, sums):
        r = tile_of(i, 64)
        unit, scaled = unit_rows(src[r, :])
        u = up[r, :]
        along = u * gain[...]
        inner = (
            along
            - jnp.mean(along, axis=-1, keepdims=True)
            - unit * jnp.mean(along * unit, axis=-1, keepdims=True)
        )
        total = add[r, :].astype(f32) + inner * scaled
        dst[r, :] = total
        dst_low[r, :] = total.astype(bf)
        fold = lambda v: jnp.sum(v.reshape(8, 8, v.shape[1]), axis=0)
        return sums[0] + fold(u * unit), sums[1] + fold(u)

    zero = jnp.zeros((8, src.shape[1]), f32)
    a, b = lax.fori_loop(0, rows // 64, chunk, (zero, zero))
    return jnp.sum(a, axis=0, keepdims=True), jnp.sum(b, axis=0, keepdims=True)


def remote(src, dst, send, recv, **where):
    return pltpu.make_async_remote_copy(
        src_ref=src, dst_ref=dst, send_sem=send, recv_sem=recv, device_id=where,
        device_id_type=pl.DeviceIdType.MESH,
    )


def greet(env, pairs):
    s, c, z, seqs = env["s"], env["c"], env["z"], env["seqs"]
    barrier = pltpu.get_barrier_semaphore()
    count = 1
    pl.semaphore_signal(
        barrier, inc=1, device_id={"clip": 2 * z + 1 - c}, device_id_type=pl.DeviceIdType.MESH
    )
    for k in range(1, seqs):
        pl.semaphore_signal(
            barrier, inc=1, device_id={"seq": lax.rem(s + k, seqs)}, device_id_type=pl.DeviceIdType.MESH
        )
        count += 1
    for k in range(1, pairs):
        pl.semaphore_signal(
            barrier, inc=1, device_id={"clip": 2 * lax.rem(z + k, pairs) + c},
            device_id_type=pl.DeviceIdType.MESH,
        )
        count += 1
    pl.semaphore_wait(barrier, count)


def place(seqs):
    b = lax.axis_index("clip")
    return dict(seqs=seqs, s=lax.axis_index("seq"), c=lax.rem(b, 2), z=lax.div(b, 2))


def kb_kernel(seqs, *refs):
    (
        att, x_ref, gb, ck, cv, owner, g2, b2, g3, b3,
        w_o, w_cq, w_co, w_up, w_dn, n1_hbm,
    ) = refs[:16]
    (x1, fo, vec, c_up, c_dn, c_o, c_cq, c_co, heads, n1_all, kq, vq) = refs[16:28]
    (
        ring, up_st, dn_st, up_rv, dn_rv, sq_rv, x2, n2, n3, n3t, cq, co, probs, u, ut, dh,
        acc, dn3, dck, dcv, kv_low, kv_rv, ring_sem, st_send, st_recv, out_sem, n1_sem, head_sem, kv_sem,
        own_sem,
    ) = refs[28:]
    env = place(seqs)
    s, c, z = env["s"], env["c"], env["z"]
    rows, d = x_ref.shape
    pairs, rb = up_rv.shape[0], up_rv.shape[1]
    ppc, rbd = dn_st.shape[0], dn_st.shape[2]
    steps = w_up.shape[1] // d
    width = d // seqs
    texts = ck.shape[0]
    depth = ring.shape[0]

    items = [w_o, w_cq, w_co]
    for t in range(steps):
        items += [w_up.at[:, pl.ds(t * d, d)], w_dn.at[pl.ds(t * d, d), :]]
    items += [w_co, w_cq, w_o]

    def load(i):
        return pltpu.make_async_copy(items[i], ring.at[i % depth], ring_sem.at[i % depth])

    def take(i):
        load(i).wait()
        return ring.at[i % depth]

    def drop(i):
        if i + depth < len(items):
            load(i + depth).start()

    for i in range(depth):
        load(i).start()
    greet(env, 1)

    peers = [(k, lax.rem(s + k, seqs)) for k in range(1, seqs)]
    spots = pl.ds(pl.multiple_of(s * rows, rows), rows)
    n1_out = [
        remote(n1_hbm, n1_all.at[spots, :], n1_sem.at[0, k], n1_sem.at[1, k], seq=to) for k, to in peers
    ]
    n1_own = pltpu.make_async_copy(n1_hbm, n1_all.at[spots, :], n1_sem.at[0, 0])
    start(n1_out)
    n1_own.start()

    w = take(0)

    def f(t):
        x1[:, tile_of(t)] = x_ref[:, tile_of(t)].astype(f32) + dg(att[...], w[:, tile_of(t)], NN)

    each(d // 256, f)
    drop(0)
    norm_rows(x1, g2, b2, n2, rows)
    w = take(1)

    def f(t):
        cq[:, tile_of(t)] = dg(n2[...], w[:, tile_of(t)], NN).astype(bf)

    each(d // 256, f)
    drop(1)
    half = 256
    key_clip = lax.broadcasted_iota(jnp.int32, (half, texts), 1) // TEXT

    def masked(v, h):
        lane = lax.broadcasted_iota(jnp.int32, v.shape, 1)
        return jnp.where(lane // HD == h, v, jnp.zeros_like(v))

    def f(n):
        t, r = lax.div(n, rows // half), tile_of(lax.rem(n, rows // half), half)
        allowed = owner[r, :] == key_clip
        q, k, v = cq[r, tile_of(t)], ck[:, tile_of(t)], cv[:, tile_of(t)]
        total = jnp.zeros((half, 256), f32)
        for h in range(256 // HD):
            sc = jnp.where(allowed, dg(masked(q, h), k, NT), NEG)
            p = jnp.exp2((sc - jnp.max(sc, axis=-1, keepdims=True)) * C2)
            p = (p / jnp.sum(p, axis=-1, keepdims=True)).astype(bf)
            probs[t * (256 // HD) + h, r, :] = p
            total = total + dg(p, masked(v, h), NN)
        co[r, tile_of(t)] = total.astype(bf)

    each(d // 256 * (rows // half), f)
    w = take(2)

    def f(t):
        x2[:, tile_of(t)] = x1[:, tile_of(t)] + dg(co[...], w[:, tile_of(t)], NN)

    each(d // 256, f)
    drop(2)
    norm_rows(x2, g3, b3, n3, rows)

    def turn(src, dst):
        def f(t):
            dst[tile_of(t), :] = src[:, tile_of(t)].T

        each(d // 256, f)

    turn(n3, n3t)

    def swap(n, src, dst):
        return remote(src, dst, st_send.at[n], st_recv.at[n], clip=2 * z + 1 - c)

    def up_swap(t):
        return swap(2 * t, up_st.at[0, :, 1 - c], up_rv.at[:, :, pl.ds(t * d, d)])

    def dn_swap(t):
        return swap(2 * t + 1, dn_st.at[:, 1 - c], dn_rv.at[pl.ds(t * ppc, ppc)])

    def up_out(t):
        cols = pl.ds(t * d, d)
        return pltpu.make_async_copy(up_rv.at[:, :, cols], c_up.at[:, :, cols], out_sem.at[2 * t])

    def dn_out(t):
        blocks = pl.ds(t * ppc, ppc)
        return pltpu.make_async_copy(dn_rv.at[blocks], c_dn.at[blocks], out_sem.at[2 * t + 1])

    def settle(t):
        one = up_swap(t)
        one.wait_recv()
        for p in range(pairs):
            dst = up_rv.at[p, :, pl.ds(t * d, d)]
            add_blocks(dst, [dst, up_st.at[0, p, c]], rb, d)
        one.wait_send()
        up_out(t).start()
        one = dn_swap(t)
        one.wait_recv()
        for p in range(ppc):
            dst = dn_rv.at[t * ppc + p]
            add_blocks(dst, [dst, dn_st.at[p, c]], rbd, d)
        one.wait_send()
        dn_out(t).start()

    for t in range(steps):
        wu, wd = take(3 + 2 * t), take(4 + 2 * t)

        def f(i):
            h = dg(n3[...], wu[:, tile_of(i)], NN)
            du = dg(gb[...], wd[tile_of(i), :], NT)
            part = 0.5 * (1.0 + lax.erf(h * SQRT_HALF))
            slope = part + h * jnp.exp2(h * h * (-0.5 * LOG2E)) * INV_ROOT_TWO_PI
            dh[:, tile_of(i)] = (du * slope).astype(bf)
            act = (h * part).astype(bf)
            u[:, tile_of(i)] = act
            ut[tile_of(i), :] = act.T

        each(d // 256, f)
        if t > 0:
            settle(t - 1)

        def f(i, t=t):
            a = dg(u[...], wd[:, tile_of(i)], NN)
            b = dg(dh[...], wu[tile_of(i), :], NT)
            if t == 0:
                acc[:, tile_of(i)] = a
                dn3[:, tile_of(i)] = b
            else:
                acc[:, tile_of(i)] += a
                dn3[:, tile_of(i)] += b
            g = dg(n3t[...], dh[:, tile_of(i)], NN).astype(bf)
            up_st[0, :, :, :, tile_of(i)] = g.reshape(pairs, 2, rb, 256)
            g = dg(ut[...], gb[:, tile_of(i)], NN).astype(bf)
            dn_st[:, :, :, tile_of(i)] = g.reshape(ppc, 2, rbd, 256)

        each(d // 256, f)
        drop(3 + 2 * t)
        drop(4 + 2 * t)
        up_swap(t).start()
        dn_swap(t).start()

    def f(i):
        r = tile_of(i, 64)
        fo[r, :] = (x2[r, :] + acc[r, :]).astype(bf)

    each(rows // 64, f)
    base = 3 + 2 * steps
    low = u
    sums = norm_back_rows(dn3, x2, g3, gb, acc, low, rows)
    vec[2:3, :], vec[3:4, :] = sums
    w = take(base)
    dco = dh

    def f(t):
        dco[:, tile_of(t)] = dg(low[...], w[tile_of(t), :], NT).astype(bf)

    each(d // 256, f)
    drop(base)
    settle(steps - 1)

    def grad(n, slot, a, low):
        turn(a, n3t)

        def f(t):
            g = dg(n3t[...], low[:, tile_of(t)], NN).astype(bf)
            up_st[slot, :, :, :, tile_of(t)] = g.reshape(pairs, 2, rb, 256)

        each(d // 256, f)
        grad_swap(n, slot).start()

    def grad_swap(n, slot):
        return swap(2 * steps + n, up_st.at[slot, :, 1 - c], sq_rv.at[n])

    def grad_out(n):
        return pltpu.make_async_copy(sq_rv.at[n], (c_co, c_cq, c_o)[n], out_sem.at[2 * steps + n])

    def grad_settle(n, slot):
        one = grad_swap(n, slot)
        one.wait_recv()
        for p in range(pairs):
            add_blocks(sq_rv.at[n, p], [sq_rv.at[n, p], up_st.at[slot, p, c]], rb, d)
        one.wait_send()
        grad_out(n).start()

    grad(0, 0, co, low)
    dcq = n3

    def f(t):
        k, v = ck[:, tile_of(t)], cv[:, tile_of(t)]
        sum_k = jnp.zeros((texts, 256), f32)
        sum_v = jnp.zeros((texts, 256), f32)
        for n in range(rows // half):
            r = pl.ds(n * half, half)
            q, g = cq[r, tile_of(t)], dco[r, tile_of(t)]
            out = jnp.zeros((half, 256), f32)
            for h in range(256 // HD):
                p_low = probs[t * (256 // HD) + h, r, :]
                p = p_low.astype(f32)
                dp = dg(masked(g, h), v, NT)
                inner = jnp.sum(p * dp, axis=-1, keepdims=True)
                ds = (p * (dp - inner)).astype(bf)
                out = out + dg(ds, masked(k, h), NN)
                sum_k = sum_k + dg(ds, masked(q, h), TN)
                sum_v = sum_v + dg(p_low, masked(g, h), TN)
            dcq[r, tile_of(t)] = (out * 0.125).astype(bf)
        kv_low[0, :, tile_of(t)] = (sum_k * 0.125).astype(bf)
        kv_low[1, :, tile_of(t)] = sum_v.astype(bf)

    each(d // 256, f)
    mine = pl.ds(pl.multiple_of(s * width, 128), width)
    kv_out = [
        remote(
            kv_low.at[:, :, pl.ds(pl.multiple_of(to * width, 128), width)], kv_rv.at[k - 1],
            kv_sem.at[0, k], kv_sem.at[1, k], seq=to,
        )
        for k, to in peers
    ]
    start(kv_out)
    w = take(base + 1)
    dn2 = dn3

    def f(t):
        dn2[:, tile_of(t)] = dg(dcq[...], w[tile_of(t), :], NT)

    each(d // 256, f)
    drop(base + 1)
    sums = norm_back_rows(dn2, x1, g2, acc, x1, low, rows)
    vec[0:1, :], vec[1:2, :] = sums
    vec[4:8, :] = jnp.zeros((4, d), f32)
    w = take(base + 2)
    do = dh

    def f(t):
        do[:, tile_of(t)] = dg(low[...], w[tile_of(t), :], NT).astype(bf)

    each(d // 256, f)
    head_out = [
        remote(
            do.at[:, pl.ds(pl.multiple_of(to * width, 128), width)], heads.at[spots, :],
            head_sem.at[0, k], head_sem.at[1, k], seq=to,
        )
        for k, to in peers
    ]
    head_own = pltpu.make_async_copy(do.at[:, mine], heads.at[spots, :], head_sem.at[0, 0])
    start(head_out)
    head_own.start()
    grad(1, 1, n2, dcq)
    grad_settle(0, 0)
    grad(2, 0, att, low)
    grad_settle(1, 1)
    arrive(kv_out)
    for n, dst in enumerate((kq, vq)):
        total = kv_low[n, :, mine].astype(f32)
        for k in range(1, seqs):
            total = total + kv_rv[k - 1, n].astype(f32)
        dst[...] = total.astype(bf)
    grad_settle(2, 0)
    finish(kv_out)
    head_own.wait()
    n1_own.wait()
    for one in head_out + n1_out:
        one.wait()
    for t in range(steps):
        up_out(t).wait()
        dn_out(t).wait()
    for n in range(3):
        grad_out(n).wait()


def kb(seqs, clips, att, x, gb, ck, cv, owner, g2, b2, g3, b3, w_o, w_cq, w_co, w_up, w_dn, n1):
    rows, d = x.shape
    pairs = clips // 2
    rb, rbd = d // clips, w_dn.shape[0] // clips
    steps = w_up.shape[1] // d
    ppc = pairs // steps
    texts = ck.shape[0]
    width = d // seqs
    hbm = pl.BlockSpec(memory_space=pl.ANY)
    vmem = pl.BlockSpec(memory_space=pltpu.VMEM)
    low = lambda *shape: pltpu.VMEM(shape, bf)
    full = lambda *shape: pltpu.VMEM(shape, f32)
    s_low = lambda *shape: jax.ShapeDtypeStruct(shape, bf)
    dma = pltpu.SemaphoreType.DMA
    return pl.pallas_call(
        functools.partial(kb_kernel, seqs),
        out_shape=[
            jax.ShapeDtypeStruct((rows, d), f32),
            s_low(rows, d),
            jax.ShapeDtypeStruct((8, d), f32),
            s_low(pairs, rb, steps * d),
            s_low(pairs, rbd, d),
            s_low(pairs, rb, d),
            s_low(pairs, rb, d),
            s_low(pairs, rb, d),
            s_low(rows * seqs, width),
            s_low(rows * seqs, d),
            s_low(texts, width),
            s_low(texts, width),
        ],
        in_specs=[vmem] * 10 + [hbm] * 6,
        out_specs=[vmem] * 3 + [hbm] * 7 + [vmem] * 2,
        scratch_shapes=[
            low(4, d, d),
            low(2, pairs, 2, rb, d),
            low(ppc, 2, rbd, d),
            low(pairs, rb, steps * d),
            low(pairs, rbd, d),
            low(3, pairs, rb, d),
            full(rows, d),
            low(rows, d),
            low(rows, d),
            low(d, rows),
            low(rows, d),
            low(rows, d),
            low(d // HD, rows, texts),
            low(rows, d),
            low(d, rows),
            low(rows, d),
            full(rows, d),
            full(rows, d),
            full(8, 128),
            full(8, 128),
            low(2, texts, d),
            low(seqs - 1, 2, texts, width),
            dma((4,)),
            dma((2 * steps + 3,)),
            dma((2 * steps + 3,)),
            dma((2 * steps + 3,)),
            dma((2, seqs)),
            dma((2, seqs)),
            dma((2, seqs)),
            dma((1,)),
        ],
        compiler_params=pltpu.CompilerParams(
            collective_id=2, has_side_effects=True, vmem_limit_bytes=60 * 2**20
        ),
    )(
        att, x, gb, ck, cv, owner[:, None],
        *[v[None] for v in (g2, b2, g3, b3)],
        w_o, w_cq, w_co, w_up, w_dn, n1,
    )


class Job:
    def __init__(self, order, part, bufs, sems, out, env, pairs):
        self.order, self.part, self.out, self.env, self.pairs = order, part, out, env, pairs
        self.r0, self.r1, self.r2 = bufs
        self.sems = sems
        self.rb, self.n = part.shape[-2:]
        self.q = self.n if order == "own" else self.n // env["seqs"]

    def copy(self, stage, k, src, dst, **where):
        return remote(src, dst, self.sems.at[0, stage, k], self.sems.at[1, stage, k], **where)

    def cores(self):
        e = self.env
        return [
            self.copy(0, 0, self.part.at[:, 1 - e["c"]], self.r0, clip=2 * e["z"] + 1 - e["c"])
        ]

    def mine(self):
        src = self.part.at[:, :, self.columns(self.env["s"])] if self.order == "xy" else self.part.at[self.env["z"]]
        return pltpu.make_async_copy(src, self.r0, self.sems.at[0, 4, 0])

    def columns(self, s):
        return pl.ds(pl.multiple_of(s * self.q, 128), self.q)

    def seq(self):
        e, copies = self.env, []
        for k in range(1, e["seqs"]):
            to = lax.rem(e["s"] + k, e["seqs"])
            if self.order == "xy":
                src, dst = self.part.at[:, :, self.columns(to)], self.r1.at[k - 1]
            else:
                src, dst = self.r1.at[0, :, self.columns(to)], self.r2.at[k - 1]
            copies.append(self.copy(1, k - 1, src, dst, seq=to))
        return copies

    def across(self):
        e, copies = self.env, []
        for k in range(1, self.pairs):
            to = lax.rem(e["z"] + k, self.pairs)
            if self.order == "xy":
                src, dst = self.r1.at[0, to], self.r2.at[k - 1]
            elif self.order == "z":
                src, dst = self.part.at[to], self.r1.at[k - 1]
            else:
                src, dst = self.r0.at[to], self.r2.at[k - 1]
            copies.append(self.copy(2, k - 1, src, dst, clip=2 * to + e["c"]))
        return copies

    def gather(self):
        e, copies = self.env, []
        for k in range(1, e["seqs"]):
            to = lax.rem(e["s"] + k, e["seqs"])
            copies.append(
                self.copy(3, k - 1, self.r2.at[0], self.out.at[:, self.columns(e["s"])], seq=to)
            )
        return copies

    def keep(self):
        return pltpu.make_async_copy(
            self.r2.at[0], self.out.at[:, self.columns(self.env["s"])], self.sems.at[1, 4, 0]
        )

    def sum_cores(self):
        for p in range(self.pairs):
            add_blocks(self.r0.at[p], [self.r0.at[p], self.part.at[p, self.env["c"]]], self.rb, self.n)

    def sum_seq(self):
        others = range(self.env["seqs"] - 1)
        if self.order == "xy":
            self.mine().wait()
            for p in range(self.pairs):
                add_blocks(self.r1.at[0, p], [self.r0.at[p]] + [self.r1.at[k, p] for k in others], self.rb, self.q)
        else:
            mine = self.r1.at[0, :, self.columns(self.env["s"])]
            add_blocks(self.r2.at[0], [mine] + [self.r2.at[k] for k in others], self.rb, self.q)

    def sum_across(self):
        e = self.env
        others = range(self.pairs - 1)
        if self.order == "xy":
            add_blocks(self.r2.at[0], [self.r1.at[0, e["z"]]] + [self.r2.at[k] for k in others], self.rb, self.q)
        elif self.order == "z":
            self.mine().wait()
            add_blocks(self.r1.at[0], [self.r0] + [self.r1.at[k] for k in others], self.rb, self.n)
        else:
            add_blocks(self.r2.at[0], [self.r0.at[e["z"]]] + [self.r2.at[k] for k in others], self.rb, self.q)


def start(copies):
    for one in copies:
        one.start()


def arrive(copies):
    for one in copies:
        one.wait_recv()


def finish(copies):
    for one in copies:
        one.wait_send()


def job_bufs(order, pairs, rb, n, seqs):
    q = n if order == "own" else n // seqs
    low = lambda *shape: pltpu.VMEM(shape, bf)
    if order == "xy":
        return [low(pairs, rb, q), low(seqs - 1, pairs, rb, q), low(pairs - 1, rb, q)]
    if order == "z":
        return [low(rb, n), low(pairs - 1, rb, n), low(seqs - 1, rb, q)]
    return [low(pairs, rb, q), low(16, 128), low(pairs - 1, rb, q)]


LAST = pl.DeviceIdType.MESH


def kc_kernel(seqs, pairs, *refs):
    (q_ref, k_ref, v_ref, o_ref, g_ref, lse_ref, first_ref) = refs[:7]
    (kq, vq, text, x_ref, dx1, g1, vec_in, n1_hbm, w_q, w_k, w_v, *parts) = refs[7:23]
    (frames_grad, vec, k_all, v_all, *outs) = refs[23:37]
    dq_s, dk_s, dv_s, dka, dva, n1_buf, wacc, wparts, dqkv, w_buf, dn1, vec_rv, low_buf, *rest = refs[37:]
    sems, push_send, push_recv, local_sem, kv_sem, vec_sem = rest[-6:]
    bufs = rest[:-6]
    env = place(seqs)
    s, c, z = env["s"], env["c"], env["z"]
    frames = T // seqs
    d = n1_hbm.shape[1]
    greet(env, pairs)

    orders = ORDERS
    jobs = []
    for t, order in enumerate(orders):
        src = parts[t] if t < 5 else wparts.at[t - 5]
        jobs.append(Job(order, src, bufs[3 * t : 3 * t + 3], sems.at[t], outs[t], env, pairs))
    up, down, go, gcq, gco, gxk, gxv, gq, gk, gv = jobs
    start(down.across())
    start(up.seq())
    for one in (go, gcq, gco):
        start(one.seq())
    for one in (up, down, go, gcq, gco):
        one.mine().start()
    width = kq.shape[1]
    spot = pl.ds(pl.multiple_of(s * width, 128), width)
    kv_out, kv_own = [], []
    for n, (src, dst) in enumerate(((kq, k_all), (vq, v_all))):
        for k in range(1, seqs):
            kv_out.append(
                remote(src, dst.at[:, spot], kv_sem.at[0, n, k], kv_sem.at[1, n, k], seq=lax.rem(s + k, seqs))
            )
        kv_own.append(pltpu.make_async_copy(src, dst.at[:, spot], kv_sem.at[0, n, 0]))
    start(kv_out)
    start(kv_own)
    loads = [pltpu.make_async_copy(n1_hbm, n1_buf, local_sem.at[0])]
    for n, one in enumerate((w_q, w_k, w_v)):
        loads.append(pltpu.make_async_copy(one, w_buf.at[n], local_sem.at[1 + n]))
    start(loads)

    def place_product(n, rb):
        for p in range(pairs):
            for cc in range(2):
                wparts[n, p, cc] = wacc[pl.ds((2 * p + cc) * rb, rb), :].astype(bf)

    for n, src in enumerate((kq, vq)):
        wacc[...] = dg(text[...], src[...], TN)
        place_product(n, gxk.rb)
        start((gxk, gxv)[n].cores())

    dka[...] = jnp.zeros_like(dka)
    dva[...] = jnp.zeros_like(dva)

    def qblock(i, masked):
        r0 = pl.multiple_of(i * B, B)
        q = q_ref[pl.ds(r0, B), :]
        g = g_ref[pl.ds(r0, B), :]
        go_ = g.astype(f32) * o_ref[pl.ds(r0, B), :].astype(f32)
        hm = (
            lax.broadcasted_iota(jnp.int32, (8, W), 1) // HD == lax.broadcasted_iota(jnp.int32, (8, W), 0)
        ).astype(f32)
        delta = lax.dot_general(hm, go_, NT, precision=lax.Precision.HIGHEST, preferred_element_type=f32)
        lse = lse_ref[:, pl.ds(r0, B)]
        fst = first_ref[:, pl.ds(r0, B)]
        zero = jnp.zeros_like(q)
        qm = [jnp.where(lanemask(B, h), q, zero) for h in range(H)]
        gm = [jnp.where(lanemask(B, h), g, zero) for h in range(H)]
        kvi = lax.broadcasted_iota(jnp.int32, (B, B), 0)
        qi = lax.broadcasted_iota(jnp.int32, (B, B), 1)

        def tile(j, dq, diag):
            c0 = pl.multiple_of(j * B, B)
            k = k_ref[pl.ds(c0, B), :]
            v = v_ref[pl.ds(c0, B), :]
            dv = jnp.zeros((B, W), f32)
            dk = jnp.zeros((B, W), f32)
            for h in range(H):
                st = dg(k, qm[h], NT)
                p = jnp.exp2(st * C2 - lse[h : h + 1])
                if diag:
                    p = jnp.where(kvi <= qi, p, 0.0)
                if masked:
                    p = jnp.where(kvi + c0 >= fst, p, 0.0)
                dp = dg(v, gm[h], NT)
                ds = (p * (dp - delta[h : h + 1])).astype(bf)
                dv = dv + dg(p.astype(bf), gm[h], NN)
                dk = dk + dg(ds, qm[h], NN)
                km = jnp.where(lanemask(B, h), k, zero)
                dq = dq + dg(ds, km, TN)
            dva[pl.ds(c0, B), :] += dv
            dka[pl.ds(c0, B), :] += dk
            return dq

        dq = jnp.zeros((B, W), f32)
        dq = lax.fori_loop(0, i, lambda j, x: tile(j, x, False), dq)
        dq = tile(i, dq, True)
        dq_s[pl.ds(r0, B), :] = (dq * 0.125).astype(bf)
        dk_s[pl.ds(r0, B), :] = (dka[pl.ds(r0, B), :] * 0.125).astype(bf)
        dv_s[pl.ds(r0, B), :] = dva[pl.ds(r0, B), :].astype(bf)

    lanes = pl.ds(pl.multiple_of(s * W, 128), W)
    moved = [(src, dqkv.at[n]) for n, src in enumerate((dq_s, dk_s, dv_s))]

    def pushes(owner):
        k = lax.rem(owner - s + seqs, seqs)
        rows = pl.ds(owner * frames, frames)
        return [
            pltpu.make_async_remote_copy(
                src_ref=src.at[rows, :],
                dst_ref=dst.at[:, lanes],
                send_sem=push_send.at[n, owner],
                recv_sem=push_recv.at[n, k],
                device_id={"seq": owner},
                device_id_type=LAST,
            )
            for n, (src, dst) in enumerate(moved)
        ]

    def keeps(owner):
        rows = pl.ds(owner * frames, frames)
        return [
            pltpu.make_async_copy(src.at[rows, :], dst.at[:, lanes], push_send.at[n, owner])
            for n, (src, dst) in enumerate(moved)
        ]

    per = frames // B
    for owner in reversed(range(seqs)):
        def block(n, x, owner=owner):
            qblock(owner * per + per - 1 - n, (owner + 1) * frames > TAIL)
            return x
        lax.fori_loop(0, per, block, 0)

        @pl.when(s != owner)
        def _():
            start(pushes(owner))

        @pl.when(s == owner)
        def _():
            start(keeps(owner))

        if owner == seqs - 1:
            for one in (gxk, gxv):
                arrive(one.cores())
                one.sum_cores()
                start(one.across())

    loads[0].wait()
    for n, src in enumerate((dq_s, dk_s, dv_s)):
        def product(r, x, src=src):
            rows = pl.ds(pl.multiple_of(r * B, B), B)
            add = dg(n1_buf[rows, :], src[rows, :], TN)
            wacc[...] = jnp.where(r == 0, add, wacc[...] + add)
            return x
        lax.fori_loop(0, T // B, product, 0)
        place_product(2 + n, gq.rb)
        start((gq, gk, gv)[n].cores())

    for one in (gxk, gxv):
        arrive(one.across())
        one.sum_across()
        start(one.gather())
        one.keep().start()
    for one in (gq, gk, gv):
        arrive(one.cores())
        one.sum_cores()
        start(one.across())
    arrive(up.seq())
    up.sum_seq()
    start(up.across())
    for one in (go, gcq, gco):
        arrive(one.seq())
        one.sum_seq()
        start(one.across())

    for k in range(1, seqs):
        for n in range(3):
            dst = dqkv.at[n, :, pl.ds(pl.multiple_of(lax.rem(s - k + seqs, seqs) * W, 128), W)]
            pltpu.make_async_copy(dst, dst, push_recv.at[n, k]).wait()
    for owner in range(seqs):
        @pl.when(s != owner)
        def _():
            finish(pushes(owner))

        @pl.when(s == owner)
        def _():
            for one in keeps(owner):
                one.wait()
    for n in range(3):
        loads[1 + n].wait()

        def f(t, n=n):
            add = dg(dqkv[n], w_buf[n, tile_of(t), :], NT)
            if n == 0:
                dn1[:, tile_of(t)] = add
            else:
                dn1[:, tile_of(t)] += add

        each(d // 256, f)

    def f(i):
        r = tile_of(i, 64)
        wide_x[r, :] = x_ref[r, :].astype(f32)

    wide_x = frames_grad
    each(frames // 64, f)
    vec[...] = vec_in[...]
    sums = norm_back_rows(dn1, wide_x, g1, dx1, frames_grad, low_buf, frames)
    vec[4:5, :], vec[5:6, :] = sums
    swap = [remote(vec, vec_rv.at[0], vec_sem.at[0, 0, 0], vec_sem.at[1, 0, 0], clip=2 * z + 1 - c)]
    start(swap)

    arrive(down.across())
    down.sum_across()
    start(down.seq())
    arrive(swap)
    finish(swap)
    vec[...] = vec[...] + vec_rv[0]
    base = 1
    vec_rv[base + s] = vec[...]
    round_seq = [
        remote(vec, vec_rv.at[base + s], vec_sem.at[0, 1, k], vec_sem.at[1, 1, k], seq=lax.rem(s + k, seqs))
        for k in range(1, seqs)
    ]
    start(round_seq)
    for one in (gq, gk, gv, up, go, gcq, gco):
        arrive(one.across())
        one.sum_across()
        start(one.gather())
        one.keep().start()
    arrive(round_seq)
    finish(round_seq)
    total = vec_rv[base]
    for k in range(1, seqs):
        total = total + vec_rv[base + k]
    vec[...] = total
    base = 1 + seqs
    round_z = [
        remote(
            vec, vec_rv.at[base + k - 1], vec_sem.at[0, 2, k], vec_sem.at[1, 2, k],
            clip=2 * lax.rem(z + k, pairs) + c,
        )
        for k in range(1, pairs)
    ]
    start(round_z)
    arrive(down.seq())
    down.sum_seq()
    start(down.gather())
    down.keep().start()
    arrive(round_z)
    finish(round_z)
    total = vec[...]
    for k in range(1, pairs):
        total = total + vec_rv[base + k - 1]
    vec[...] = total

    for one in kv_out + kv_own:
        one.wait()
    for one in jobs:
        if one.order == "own":
            finish(one.cores())
        else:
            finish(one.seq())
        finish(one.across())
        finish(one.gather())
        one.keep().wait()
        arrive(one.gather())


ORDERS = ("xy", "z", "xy", "xy", "xy", "own", "own", "own", "own", "own")
TAIL = 1536


def kc(seqs, clips, heads, lse, first, kq, vq, text, x, dx1, g1, vec, n1_all, weights, parts):
    pairs = clips // 2
    rows, d = x.shape
    rb = d // clips
    shapes = [p.shape for p in parts] + [(pairs, 2, rb, W)] * 5
    bufs = []
    for order, shape in zip(ORDERS, shapes):
        bufs += job_bufs(order, pairs, shape[-2], shape[-1], seqs)
    outs = [
        jax.ShapeDtypeStruct((rows, d), f32),
        jax.ShapeDtypeStruct((8, d), f32),
        jax.ShapeDtypeStruct((text.shape[0], d), bf),
        jax.ShapeDtypeStruct((text.shape[0], d), bf),
    ]
    for order, shape in zip(ORDERS, shapes):
        outs.append(jax.ShapeDtypeStruct((shape[-2], shape[-1] * (seqs if order == "own" else 1)), bf))
    hbm = pl.BlockSpec(memory_space=pl.ANY)
    vmem = pl.BlockSpec(memory_space=pltpu.VMEM)
    most = max(seqs, pairs)
    dma = pltpu.SemaphoreType.DMA
    return pl.pallas_call(
        functools.partial(kc_kernel, seqs, pairs),
        out_shape=outs,
        in_specs=[vmem] * 14 + [hbm] * 9,
        out_specs=[vmem] * 2 + [hbm] * 12,
        scratch_shapes=[pltpu.VMEM((T, W), bf)] * 3
        + [pltpu.VMEM((T, W), f32)] * 2
        + [
            pltpu.VMEM((T, d), bf),
            pltpu.VMEM((d, W), f32),
            pltpu.VMEM((5, pairs, 2, rb, W), bf),
            pltpu.VMEM((3, rows, d), bf),
            pltpu.VMEM((3, d, d), bf),
            pltpu.VMEM((rows, d), f32),
            pltpu.VMEM((1 + seqs + pairs - 1, 8, d), f32),
            pltpu.VMEM((rows, d), bf),
        ]
        + bufs
        + [
            dma((10, 2, 5, most)),
            dma((3, seqs)),
            dma((3, seqs)),
            dma((4,)),
            dma((2, 2, seqs)),
            dma((2, 3, most)),
        ],
        compiler_params=pltpu.CompilerParams(
            collective_id=1, has_side_effects=True, vmem_limit_bytes=60 * 2**20
        ),
    )(*heads, lse, first, kq, vq, text, x, dx1, g1[None], vec, n1_all, *weights, *parts)


def matmul(left, right):
    return jnp.dot(left, right, preferred_element_type=jnp.float32)


def left_times(left, right):
    return lax.dot_general(
        left, right, (((0,), (0,)), ((), ())), preferred_element_type=jnp.float32
    )


def right_times(left, right):
    return lax.dot_general(
        left, right, (((1,), (1,)), ((), ())), preferred_element_type=jnp.float32
    )


def norm_forward(values, gain, bias):
    center = values - jnp.mean(values, axis=-1, keepdims=True)
    scaled = lax.rsqrt(jnp.mean(center * center, axis=-1, keepdims=True) + EPS)
    unit = center * scaled
    return (unit * gain + bias, unit, scaled)


def norm_backward(upstream, unit, scaled, gain):
    along = upstream * gain
    inner = (
        along
        - jnp.mean(along, axis=-1, keepdims=True)
        - unit * jnp.mean(along * unit, axis=-1, keepdims=True)
    )
    return (inner * scaled, jnp.sum(upstream * unit, axis=0), jnp.sum(upstream, axis=0))


def gelu_slope(values):
    return (
        0.5 * (1.0 + lax.erf(values * SQRT_HALF))
        + values * jnp.exp(-0.5 * values * values) * INV_ROOT_TWO_PI
    )


def softmax_rows(scores):
    top = jnp.max(scores, axis=-1, keepdims=True)
    expo = jnp.exp(scores - top)
    total = jnp.sum(expo, axis=-1, keepdims=True)
    return (expo / total, top[..., 0] + jnp.log(total[..., 0]))


def shards(
    frames_in,
    text_states,
    clip_lengths,
    self_gain,
    self_bias,
    query_weight,
    key_weight,
    value_weight,
    output_weight,
    cross_gain,
    cross_bias,
    cross_query,
    cross_key,
    cross_value,
    cross_output,
    feed_gain,
    feed_bias,
    feed_upward,
    feed_downward,
    grad_out,
):
    count = lax.axis_size("seq")
    place = lax.axis_index("seq")
    local = frames_in.shape[1]
    total_frames = local * count
    block = min(512, total_frames)
    blocks = total_frames // block
    scale = HD ** (-0.5)
    lengths = clip_lengths[0]
    slot = jnp.arange(CLIPS, dtype=jnp.int32)
    ends = jnp.sum(jnp.where(slot[None, :] <= slot[:, None], lengths[None, :], 0), axis=1)
    begins = ends - lengths
    slots = jnp.arange(CLIPS, dtype=jnp.int32)
    positions = jnp.arange(total_frames, dtype=jnp.int32)
    owner_all = jnp.sum((ends[None, :] <= positions[:, None]).astype(jnp.int32), axis=1)
    first_all = jnp.sum(jnp.where(owner_all[:, None] == slots[None, :], begins[None, :], 0), axis=1)
    owner_mine = lax.dynamic_slice_in_dim(owner_all, place * local, local, 0)
    frames = frames_in[0].astype(jnp.float32)
    text = text_states[0]
    text_rows = text.shape[0]
    normed, _, _ = norm_forward(frames, self_gain, self_bias)
    normed_low = normed.astype(bf)
    query = matmul(normed_low, query_weight).astype(bf)
    keys = matmul(normed_low, key_weight).astype(bf)
    values = matmul(normed_low, value_weight).astype(bf)
    query_heads, key_heads, value_heads = (
        lax.all_to_all(query, "seq", split_axis=1, concat_axis=0, tiled=True),
        lax.all_to_all(keys, "seq", split_axis=1, concat_axis=0, tiled=True),
        lax.all_to_all(values, "seq", split_axis=1, concat_axis=0, tiled=True),
    )
    attended, log_totals = fwd(query_heads, key_heads, value_heads, first_all[:, None])
    attended_frames = lax.all_to_all(attended, "seq", split_axis=0, concat_axis=1, tiled=True)
    cross_k = matmul(text, cross_key).astype(bf)
    cross_v = matmul(text, cross_value).astype(bf)
    clips = lax.axis_size("clip")
    dx1, output, vec, c_up, c_dn, c_o, c_cq, c_co, grad_heads, normed_all, key_own, value_own = kb(
        count,
        clips,
        attended_frames,
        frames_in[0],
        grad_out[0],
        cross_k,
        cross_v,
        owner_mine,
        cross_gain,
        cross_bias,
        feed_gain,
        feed_bias,
        output_weight,
        cross_query,
        cross_output,
        feed_upward,
        feed_downward,
        normed_low,
    )
    frames_grad, vec, key_low, value_low, *mats = kc(
        count,
        clips,
        (query_heads, key_heads, value_heads, attended, grad_heads),
        log_totals,
        first_all[None],
        key_own,
        value_own,
        text,
        frames_in[0],
        dx1,
        self_gain,
        vec,
        normed_all,
        (query_weight, key_weight, value_weight),
        (c_up, c_dn, c_o, c_cq, c_co),
    )
    text_grad = right_times(key_low, cross_key) + right_times(value_low, cross_value)
    w_up, w_dn, w_o, w_cq, w_co, w_xk, w_xv, w_q, w_k, w_v = [one.astype(f32) for one in mats]
    width_out = D // clips
    vec = lax.dynamic_slice_in_dim(vec, lax.axis_index("clip") * width_out, width_out, 1)
    return (
        output[None],
        frames_grad[None],
        text_grad[None],
        vec[4],
        vec[5],
        w_q,
        w_k,
        w_v,
        w_o,
        vec[0],
        vec[1],
        w_cq,
        w_xk,
        w_xv,
        w_co,
        vec[2],
        vec[3],
        w_up,
        w_dn,
    )


def solution(mesh):
    return jax.shard_map(
        shards,
        mesh=mesh,
        in_specs=(
            P("clip", "seq", None),
            P("clip", None, None),
            P("clip", None),
            P(),
            P(),
            P(),
            P(),
            P(),
            P(),
            P(),
            P(),
            P(),
            P(),
            P(),
            P(),
            P(),
            P(),
            P(),
            P(),
            P("clip", "seq", None),
        ),
        out_specs=(
            P("clip", "seq", None),
            P("clip", "seq", None),
            P("clip", None, None),
            P("clip"),
            P("clip"),
            P("clip", None),
            P("clip", None),
            P("clip", None),
            P("clip", None),
            P("clip"),
            P("clip"),
            P("clip", None),
            P("clip", None),
            P("clip", None),
            P("clip", None),
            P("clip"),
            P("clip"),
            P("clip", None),
            P("clip", None),
        ),
        check_vma=False,
    )
```

time: 628 us -> 453 us (0.72)
  matrix products: 151 us -> 14.3 us
  Pallas kernels: 248 us -> 344 us
  waiting for transfers between devices: 87.9 us -> 37.7 us
  blocking collectives: 46.5 us -> 0 us
  between operations: 15 us -> 1.38 us
  local copies, waits for them, and re-layouts: 28.5 us -> 14.9 us
    pallas_call x0 -> x1, Pallas kernels: none -> 105 us  [kb(): pl.pallas_call(functools.partial(kb_kernel, seqs), out_shape=[jax.ShapeDt...]
    dot_general x12 -> x0, matrix products: 51.5 us -> none  [the longest x7 31 us: left_times(): lax.dot_general(left, right, (((0,), (0,)), ((), ())), preferred_element_...]
    psum x1 -> x0, blocking collectives: 46.5 us -> none  [shards(): lax.psum(jnp.stack([grad_self_gain, grad_self_bias, grad_cross_gain, grad...]
    dot_general x10 -> x5, matrix products: 54.8 us -> 11.8 us  [matmul(): return jnp.dot(left, right, preferred_element_type=jnp.float32)]
    all_gather x1 -> x0, waiting for transfers between devices: 41.3 us -> none  [shards(): normed_all = lax.all_gather(normed_low, 'seq', axis=0, tiled=True)]
    dot_general x10 -> x2, matrix products: 37 us -> 2.46 us  [right_times(): lax.dot_general(left, right, (((1,), (1,)), ((), ())), preferred_element_...]
    psum x1 -> x0, waiting for transfers between devices: 12.3 us -> none  [shards(): lax.psum(key_part.astype(jnp.bfloat16), 'seq').astype(jnp.float32)]
    convert_element_type x6 -> x0, local copies, waits for them, and re-layouts: 10.9 us -> none  [the longest x2 4.08 us: shards(): one.astype(bf)]
  transfers between devices with their start and end apart: 7 -> 4, of which waited for: 6 -> 4; matrix products, arithmetic and copies ran while one was open for 12% -> 3% of each run, Pallas kernels for 0% -> 0%
where the time goes in v3:
time: 453 us; the launch traced here: 447 us
  Pallas kernels  344 us (76%)
  waiting for transfers between devices  37.7 us (8%)
  starting transfers between devices  17.3 us (4%)
  other arithmetic  16.8 us (4%)
  local copies, waits for them, and re-layouts  14.9 us (3%)
  matrix products  14.3 us (3%)
    pallas_call x1, Pallas kernels, kc(): pl.pallas_call(functools.partial(kc_kernel, seqs, pairs), out_shape=outs,...  201 us
    pallas_call x1, Pallas kernels, kb(): pl.pallas_call(functools.partial(kb_kernel, seqs), out_shape=[jax.ShapeDt...  105 us
    pallas_call x1, Pallas kernels, fwd(): pl.pallas_call(fwd_kernel, out_shape=(jax.ShapeDtypeStruct((T, W), bf), j...  38.1 us
    convert_element_type x10, other arithmetic, shards(): one.astype(f32)  12.8 us
    dot_general x5, matrix products, matmul(): return jnp.dot(left, right, preferred_element_type=jnp.float32)  11.8 us
    all_to_all x1, waiting for transfers between devices, shards(): lax.all_to_all(query, 'seq', split_axis=1, concat_axis=0, tiled=True)  11.4 us
    all_to_all x1, waiting for transfers between devices, shards(): lax.all_to_all(values, 'seq', split_axis=1, concat_axis=0, tiled=True)  9.42 us
  transfers between devices with their start and end apart: 4, of which 4 were waited for; matrix products, arithmetic and copies ran while one was open for 3% of the time, Pallas kernels for 0%

profile of v3, /device:TPU:0, one launch (start us, length us, event | category | flops | bytes accessed | tf_op | source)
XLA Modules:
  0.0 446.6 jit_solution(8318612829519062823)
XLA Ops:
  0.7 1.6 convert_reduce_fusion
  2.3 1.7 fusion.2
  4.1 0.4 fusion.5.refs_15_
  4.5 1.3 convolution_convert_fusion
  5.8 1.0 copy.68
  6.9 5.2 %all-to-all-start.2 = ((bf16[512,4,256]{2,0,1:T(8,128)(2,1)}), bf16[512,4,256]{2,0,1:T(8,128)(2,1)S(1)}, u32[]{:S(2)}, u32[]{:S(2)}) async-start(bf16[512,4,256]{2,0,1:T(8,128)(2,1)} %bitcast.87), calls=%async_computation.2 | async-start | bytes 2097152 | tf_op jit(solution)/shard_map/all_to_all | solution.py:1102
  12.0 3.2 convolution_convert_fusion.1
  15.2 1.0 copy.69
  16.2 9.4 %all-to-all-done.2 = bf16[512,4,256]{2,0,1:T(8,128)(2,1)S(1)} async-done(((bf16[512,4,256]{2,0,1:T(8,128)(2,1)}), bf16[512,4,256]{2,0,1:T(8,128)(2,1)S(1)}, u32[]{:S(2)}, u32[]{:S(2)}) %all-to-all-start.2) | async-done | bytes 1048608 | tf_op jit(solution)/shard_map/all_to_all | solution.py:1102
  25.7 4.3 all-to-all-start.1
  29.9 3.2 convolution_convert_fusion.2
  33.1 1.0 copy.70
  34.2 8.9 %all-to-all-done.1 = bf16[512,4,256]{2,0,1:T(8,128)(2,1)} async-done(((bf16[512,4,256]{2,0,1:T(8,128)(2,1)}), bf16[512,4,256]{2,0,1:T(8,128)(2,1)}, u32[]{:S(2)}, u32[]{:S(2)}) %all-to-all-start.1) | async-done | bytes 1048608 | tf_op jit(solution)/shard_map/all_to_all | solution.py:1101
  43.1 4.2 all-to-all-start
  47.3 0.1 select_reduce_fusion.1
  47.5 0.1 convert_reduce_fusion.1
  47.7 1.3 copy.58.first_ref
  49.0 11.4 %all-to-all-done = bf16[512,4,256]{2,0,1:T(8,128)(2,1)} async-done(((bf16[512,4,256]{2,0,1:T(8,128)(2,1)}), bf16[512,4,256]{2,0,1:T(8,128)(2,1)}, u32[]{:S(2)}, u32[]{:S(2)}) %all-to-all-start) | async-done | bytes 1048608 | tf_op jit(solution)/shard_map/all_to_all | solution.py:1100
  60.5 1.2 copy-done.3
  61.7 38.1 %shard_map.339 = (bf16[2048,256]{1,0:T(8,128)(2,1)S(1)}, f32[8,2048]{1,0:T(8,128)S(1)}) custom-call(bf16[2048,256]{1,0:T(8,128)(2,1)} %bitcast.2.q_ref.refs_0_, bf16[2048,256]{1,0:T(8,128)(2,1)} %bitcast.4.k_ref.refs_1_, bf16[2048,256]{1,0:T(8,128)(2,1)S(1)} %bitcast.78, s32[2048,1]{1,0:T(8,128)S(1)} %copy-done.3), custom_call_target="tpu_custom_call" | custom-call | tf_op jit(solution)/shard_map/pallas_call | solution.py:89
  99.8 1.0 copy-done.2
  100.8 0.6 copy-done.4
  101.4 3.7 all-to-all-start.3
  105.2 0.9 copy.60.refs_5_
  106.0 2.7 convolution_convert_fusion.4.refs_3_
  108.7 1.5 convolution_convert_fusion.3.refs_4_
  110.3 7.9 %all-to-all-done.3 = bf16[4,512,256]{2,1,0:T(8,128)(2,1)S(1)} async-done(((bf16[4,512,256]{2,1,0:T(8,128)(2,1)}), bf16[4,512,256]{2,1,0:T(8,128)(2,1)S(1)}, u32[]{:S(2)}, u32[]{:S(2)}) %all-to-all-start.3) | async-done | bytes 1048608 | tf_op jit(solution)/shard_map/all_to_all | solution.py:1105
  118.1 1.1 copy.64
  119.2 105.1 %shard_map.340 = (f32[512,1024]{1,0:T(8,128)}, bf16[512,1024]{1,0:T(8,128)(2,1)}, f32[8,1024]{1,0:T(8,128)}, bf16[4,128,4096]{2,1,0:T(8,128)(2,1)}, bf16[4,512,1...) custom-call(bf16[512,1024]{1,0:T(8,128)(2,1)} %bitcast.83, ...), custom_call_target="tpu_custom_call" | custom-call | tf_op jit(solution)/shard_map/pallas_call | solution.py:505
  224.3 201.0 %shard_map.341 = (f32[512,1024]{1,0:T(8,128)}, f32[8,1024]{1,0:T(8,128)}, bf16[256,1024]{1,0:T(8,128)(2,1)}, bf16[256,1024]{1,0:T(8,128)(2,1)}, bf16[128,4096]{1...) custom-call(bf16[2048,256]{1,0:T(8,128)(2,1)} %bitcast.2.q_ref.refs_, ...), custom_call_target="tpu_custom_call" | custom-call | tf_op jit(solution)/shard_map/pallas_call | solution.py:974
  425.4 0.7 constant_dynamic-slice_fusion
  426.2 0.5 slice_bitcast_fusion
  426.7 1.8 convert_element_type.62
  428.5 1.8 convert_element_type.63
  430.3 1.8 convert_element_type.64
  432.2 0.8 convert_element_type.65
  433.0 0.8 convert_element_type.66
  433.9 0.8 convert_element_type.67
  434.7 0.8 convert_element_type.68
  435.6 0.8 convert_element_type.69
  436.4 0.7 fusion.10
  437.2 1.5 convert_element_type.70
  438.7 1.6 convert_element_type.71
  440.3 0.8 copy-done.8
  441.1 1.7 fusion.6
  442.8 1.0 copy.73
  443.8 1.0 copy-done.9
  444.8 1.3 copy.74
  (52 shorter events, 0.4 us)
Async XLA Ops:
  0.7 105.4 %copy-start = (bf16[1024,1024]{1,0:T(8,128)(2,1)S(1)}, bf16[1024,1024]{1,0:T(8,128)(2,1)}, u32[]{:S(2)}) copy-start(bf16[1024,1024]{1,0:T(8,128)(2,1)} %param.32) | copy-start | bytes 6291460
  0.7 3.4 copy-start.5
  0.7 3.4 copy-start.23
  0.7 3.4 copy-start.24
  0.7 3.8 copy-start.10
  4.5 1.3 copy-start.6
  6.9 18.8 %all-to-all-start.2 = ((bf16[512,4,256]{2,0,1:T(8,128)(2,1)}), bf16[512,4,256]{2,0,1:T(8,128)(2,1)S(1)}, u32[]{:S(2)}, u32[]{:S(2)}) async-start(bf16[512,4,256]{2,0,1:T(8,128)(2,1)} %bitcast.87), calls=%async_computation.2 | async-start | bytes 2097152 | tf_op jit(solution)/shard_map/all_to_all | solution.py:1102
  25.7 34.8 %copy-start.1 = (bf16[512,4,256]{2,0,1:T(8,128)(2,1)}, bf16[512,4,256]{2,0,1:T(8,128)(2,1)S(1)}, u32[]{:S(2)}) copy-start(bf16[512,4,256]{2,0,1:T(8,128)(2,1)S(1)} %all-to-all-done.2) | copy-start | bytes 3145732
  25.7 17.4 %all-to-all-start.1 = ((bf16[512,4,256]{2,0,1:T(8,128)(2,1)}), bf16[512,4,256]{2,0,1:T(8,128)(2,1)}, u32[]{:S(2)}, u32[]{:S(2)}) async-start(bf16[512,4,256]{2,0,1:T(8,128)(2,1)} %bitcast.86), calls=%async_computation.1 | async-start | bytes 2097152 | tf_op jit(solution)/shard_map/all_to_all | solution.py:1101
  33.1 14.2 %copy-start.25 = (s32[1,4]{1,0:T(1,128)S(1)}, s32[1,4]{1,0:T(1,128)}, u32[]{:S(2)}) copy-start(s32[1,4]{1,0:T(1,128)} %param.22) | copy-start | bytes 52
  43.1 17.4 %all-to-all-start = ((bf16[512,4,256]{2,0,1:T(8,128)(2,1)}), bf16[512,4,256]{2,0,1:T(8,128)(2,1)}, u32[]{:S(2)}, u32[]{:S(2)}) async-start(bf16[512,4,256]{2,0,1:T(8,128)(2,1)} %bitcast.85), calls=%async_computation | async-start | bytes 2097152 | tf_op jit(solution)/shard_map/all_to_all | solution.py:1100
  47.7 52.1 %copy-start.22 = (s32[2048]{0:T(1024)}, s32[2048]{0:T(1024)S(1)}, u32[]{:S(2)}) copy-start(s32[2048]{0:T(1024)S(1)} %select_reduce_fusion) | copy-start | bytes 24580
  60.5 1.2 copy-start.3
  99.8 1.0 copy-start.2
  100.8 0.6 copy-start.4
  101.4 16.7 %all-to-all-start.3 = ((bf16[4,512,256]{2,1,0:T(8,128)(2,1)}), bf16[4,512,256]{2,1,0:T(8,128)(2,1)S(1)}, u32[]{:S(2)}, u32[]{:S(2)}) async-start(bf16[4,512,256]{2,1,0:T(8,128)(2,1)} %bitcast.80), calls=%async_computation.3 | async-start | bytes 2097152 | tf_op jit(solution)/shard_map/all_to_all | solution.py:1105
  106.0 2.7 copy-start.7
  106.0 2.7 copy-start.14
  425.4 6.8 %copy-start.21 = (bf16[128,1024]{1,0:T(8,128)(2,1)S(1)}, bf16[128,1024]{1,0:T(8,128)(2,1)}, u32[]{:S(2)}) copy-start(bf16[128,1024]{1,0:T(8,128)(2,1)} %get-tuple-element.68) | copy-start | bytes 786436
  425.4 7.6 %copy-start.20 = (bf16[128,1024]{1,0:T(8,128)(2,1)S(1)}, bf16[128,1024]{1,0:T(8,128)(2,1)}, u32[]{:S(2)}) copy-start(bf16[128,1024]{1,0:T(8,128)(2,1)} %get-tuple-element.69) | copy-start | bytes 786436
  425.4 8.5 %copy-start.19 = (bf16[128,1024]{1,0:T(8,128)(2,1)S(1)}, bf16[128,1024]{1,0:T(8,128)(2,1)}, u32[]{:S(2)}) copy-start(bf16[128,1024]{1,0:T(8,128)(2,1)} %get-tuple-element.70) | copy-start | bytes 786436
  428.5 6.2 %copy-start.18 = (bf16[128,1024]{1,0:T(8,128)(2,1)S(1)}, bf16[128,1024]{1,0:T(8,128)(2,1)}, u32[]{:S(2)}) copy-start(bf16[128,1024]{1,0:T(8,128)(2,1)} %get-tuple-element.71) | copy-start | bytes 786436
  430.3 5.2 %copy-start.17 = (bf16[128,1024]{1,0:T(8,128)(2,1)S(1)}, bf16[128,1024]{1,0:T(8,128)(2,1)}, u32[]{:S(2)}) copy-start(bf16[128,1024]{1,0:T(8,128)(2,1)} %get-tuple-element.72) | copy-start | bytes 786436
  432.2 4.2 copy-start.16
  435.5 1.6 copy-start.12
  437.1 1.6 copy-start.11
  438.7 2.3 copy-start.8
  438.7 2.4 copy-start.15
  441.1 1.7 copy-start.13
  442.8 2.0 copy-start.9
